TPU v7x, 32 devices: a whole 2x2x4 slice. The times are simulated.
32 devices in a mesh: row: 4 (over x, core), col: 8 (over z, y).
Axes of the slice: x: 2, y: 2, z: 4, core: 2. Of those that a mesh axis runs over, the one named last changes fastest.
Arguments:
- features: bfloat16 [8192, 256], P(('row', 'col')), may hold values from -6 to 6
- node_order: int32 [8192], P(('row', 'col')), may hold values from 0 to 8191, as said below
- tile_vals: bfloat16 [4, 8, 192, 128, 128], P('row', 'col'), may hold values from -0.109375 to 0.109375
- tile_coord: int32 [4, 8, 192], P('row', 'col'), may hold values from 0 to 127
- tile_count: int32 [4, 8], P('row', 'col'), may hold values from 12 to 192, as said below
- weight: bfloat16 [256, 256], replicated, may hold values from -0.375 to 0.375
- cotangent: bfloat16 [8192, 256], P(('row', 'col')), may hold values from -6 to 6
Outputs:
- activations: bfloat16 [8192, 256], P(('row', 'col'))
- weight_grad: float32 [256, 256], replicated
- feature_grad: bfloat16 [8192, 256], P(('row', 'col'))
Inputs may be any that keep to these rules, and one draw needn't show every extreme that they name: `node_order`: each aligned block of 256 entries is a permutation of that block's own indices. `tile_count`: some device holds exactly 192 used slots.
All inputs are finite; a program needn't handle non-finite values.
Results may differ from a plain program's by a relative error of at most 0.015.
Values may be sent and summed in bfloat16 or wider, within the bound.
No kernel may reach another device: no remote copies, remote signals or barrier semaphores. Data moves between devices by JAX's collectives and lax.ppermute only.
A program may use at most 128 MiB of HBM per device.

v0:
```python
import functools

import jax
import jax.numpy as jnp
from jax import lax
from jax.experimental import pallas as pl
from jax.experimental.pallas import tpu as pltpu
from jax.sharding import PartitionSpec as P

CORES = 2
GROUP = 4
UNROLL = 2
LOADS = 4
PACK_BITS = 8
PACK = 1 << PACK_BITS
VMEM_BYTES = 40 * 1024 * 1024
F32 = jnp.float32
BF16 = jnp.bfloat16


def elu_value(pre_act):
    return jnp.where(pre_act > 0, pre_act, jnp.expm1(jnp.minimum(pre_act, 0.0)))


def elu_slope(pre_act):
    return jnp.where(pre_act > 0, 1.0, jnp.exp(jnp.minimum(pre_act, 0.0)))


def permuter(node_order, nodes_here):
    local_pos = node_order % nodes_here
    return (local_pos[:, None] == jnp.arange(nodes_here, dtype=jnp.int32)[None, :]).astype(BF16)


def reorder(onehot, values):
    return jnp.dot(onehot, values, preferred_element_type=F32).astype(BF16)


def restore(onehot, values):
    moved = lax.dot_general(onehot, values, (((0,), (0,)), ((), ())), preferred_element_type=F32)
    return moved.astype(BF16)


def tile_table(bins, bin_total, sources, tile_total):
    slot_total = bins.shape[0]
    group_total = slot_total // GROUP + bin_total + 1
    slots = jnp.arange(slot_total, dtype=jnp.int32)
    marks = jnp.arange(bin_total, dtype=jnp.int32)
    live = slots < tile_total
    held = jnp.where(live, bins, bin_total)
    same = held[:, None] == held[None, :]
    before = jnp.sum((same & (slots[None, :] < slots[:, None])).astype(jnp.int32), axis=1)
    counts = jnp.sum((held[None, :] == marks[:, None]).astype(jnp.int32), axis=1)
    groups = (counts + GROUP - 1) // GROUP
    edges = jnp.arange(bin_total + 1, dtype=jnp.int32)
    firsts = jnp.sum(jnp.where(marks[None, :] < edges[:, None], groups[None, :], 0), axis=1)
    mine = jnp.sum(jnp.where(marks[None, :] < held[:, None], groups[None, :], 0), axis=1)
    place = jnp.where(live, mine * GROUP + before, -1)
    places = jnp.arange(group_total * GROUP, dtype=jnp.int32)
    empty = slot_total * PACK
    member = (slots * PACK + sources - empty)[None, :]
    members = empty + jnp.sum(jnp.where(place[None, :] == places[:, None], member, 0), axis=1)
    numbers = jnp.arange(group_total, dtype=jnp.int32)
    group_bin = jnp.sum((firsts[None, 1:] <= numbers[:, None]).astype(jnp.int32), axis=1)
    return jnp.concatenate([members, group_bin, firsts])


def load_kernel(tiles_ref, out_ref, sems):
    slot_total = tiles_ref.shape[0]
    share = slot_total // LOADS
    copies = [
        pltpu.make_async_copy(
            tiles_ref.at[pl.ds(k * share, share)], out_ref.at[pl.ds(k * share, share)], sems.at[k]
        )
        for k in range(LOADS)
    ]
    for copy in copies:
        copy.start()
    out_ref[slot_total] = jnp.zeros(out_ref.shape[1:], out_ref.dtype)
    for copy in copies:
        copy.wait()


def load_tiles(tiles):
    slot_total, tile_size, _ = tiles.shape
    nbytes = 2 * slot_total * tile_size * tile_size
    return pl.pallas_call(
        load_kernel,
        out_shape=jax.ShapeDtypeStruct((slot_total + 1, tile_size, tile_size), BF16),
        in_specs=[pl.BlockSpec(memory_space=pl.ANY)],
        out_specs=pl.BlockSpec(memory_space=pltpu.VMEM),
        scratch_shapes=[pltpu.SemaphoreType.DMA((LOADS,))],
        compiler_params=pltpu.CompilerParams(vmem_limit_bytes=VMEM_BYTES),
        cost_estimate=pl.CostEstimate(flops=0, bytes_accessed=nbytes, transcendentals=0),
    )(tiles)


def part_kernel(spec, table_ref, tiles_ref, *refs):
    transposed, first_bin, bin_count, bin_total, source_count, carried, finish = spec
    source_refs = refs[:source_count]
    acc_ref = refs[source_count] if carried is not None else None
    out_refs = refs[source_count + (carried is not None) : -2]
    source, total = refs[-2:]
    slot_total = tiles_ref.shape[0] - 1
    tile_size = tiles_ref.shape[1]
    group_total = slot_total // GROUP + bin_total + 1
    at = 0
    for ref in source_refs:
        source[at : at + ref.shape[0], :] = ref[...]
        at += ref.shape[0]
    if carried is None:
        total[...] = jnp.zeros_like(total)
    else:
        total[...] = acc_ref[carried * tile_size : carried * tile_size + total.shape[0], :]
    bins_at = group_total * GROUP
    firsts_at = bins_at + group_total
    begin = table_ref[firsts_at + first_bin]
    end = table_ref[firsts_at + first_bin + bin_count]
    contract = 0 if transposed else 1

    def step(number, carry):
        products = []
        for member in range(UNROLL):
            group = begin + number * UNROLL + member
            group = jnp.where(group < end, group, group_total - 1)
            left, right = [], []
            for k in range(GROUP):
                packed = table_ref[group * GROUP + k]
                left.append(tiles_ref[packed >> PACK_BITS])
                row = pl.multiple_of((packed & (PACK - 1)) * tile_size, tile_size)
                right.append(source[pl.ds(row, tile_size), :])
            product = lax.dot_general(
                jnp.concatenate(left, axis=contract),
                jnp.concatenate(right, axis=0),
                (((contract,), (0,)), ((), ())),
                preferred_element_type=F32,
            )
            products.append((jnp.minimum(table_ref[bins_at + group] - first_bin, bin_count - 1), product))
        for place, product in products:
            rows = pl.ds(pl.multiple_of(place * tile_size, tile_size), tile_size)
            total[rows, :] += product
        return carry

    lax.fori_loop(0, (end - begin + UNROLL - 1) // UNROLL, step, 0)
    if finish:
        at = 0
        for ref in out_refs:
            ref[...] = total[at : at + ref.shape[0], :].astype(ref.dtype)
            at += ref.shape[0]
    else:
        out_refs[0][...] = total[...]


def tile_part(transposed, table, bins, bin_total, tiles, sources, acc=None, acc_at=0, pieces=None):
    first_bin, bin_count = bins
    slot_total, tile_size = tiles.shape[0] - 1, tiles.shape[1]
    width = sources[0].shape[1]
    rows = bin_count * tile_size
    vmem = pl.BlockSpec(memory_space=pltpu.VMEM)
    if pieces is None:
        out_shape = [jax.ShapeDtypeStruct((rows, width), F32)]
    else:
        out_shape = [jax.ShapeDtypeStruct((pieces, width), BF16)] * (rows // pieces)
    carried = None if acc is None else acc_at
    share = slot_total * bin_count // bin_total
    given = [table, tiles, *sources] + ([] if acc is None else [acc])
    spec = (transposed, first_bin, bin_count, bin_total, len(sources), carried, pieces is not None)
    return pl.pallas_call(
        functools.partial(part_kernel, spec),
        out_shape=out_shape,
        in_specs=[pl.BlockSpec(memory_space=pltpu.SMEM)] + [vmem] * (len(given) - 1),
        out_specs=[vmem] * len(out_shape),
        scratch_shapes=[
            pltpu.VMEM((sum(source.shape[0] for source in sources), width), BF16),
            pltpu.VMEM((rows, width), F32),
        ],
        compiler_params=pltpu.CompilerParams(vmem_limit_bytes=VMEM_BYTES),
        cost_estimate=pl.CostEstimate(
            flops=2 * share * tile_size * tile_size * width,
            bytes_accessed=2 * share * tile_size * tile_size,
            transcendentals=0,
        ),
    )(*given)


def grid_cycle(size):
    ny = 1
    while (2 * ny) ** 2 <= size:
        ny *= 2
    nz = size // ny
    walk = [0]
    for z in range(nz):
        ys = range(1, ny) if z % 2 == 0 else range(ny - 1, 0, -1)
        walk += [z * ny + y for y in ys]
    walk += [z * ny for z in range(nz - 1, 0, -1)]
    return walk


class Grid:
    def __init__(self, rows, cols):
        self.rows, self.cols, self.chips = rows, cols, rows // CORES
        self.walk = grid_cycle(cols)
        self.place_of = [self.walk.index(c) for c in range(cols)]
        self.row, self.col = lax.axis_index("row"), lax.axis_index("col")
        self.x, self.core = self.row // CORES, self.row % CORES
        place = sum(jnp.where(self.col == c, self.place_of[c], 0) for c in range(cols))
        self.ahead_of = [
            jnp.where(self.core == 0, self.place_of[c] - place, place - self.place_of[c]) % cols
            for c in range(cols)
        ]

    def along_walk(self, step):
        pairs = []
        for r in range(self.rows):
            walk = self.walk if r % CORES == 0 else self.walk[::-1]
            for k in range(self.cols):
                pairs.append((r * self.cols + walk[k], r * self.cols + walk[(k + step) % self.cols]))
        return pairs

    def along_x(self, step):
        return [
            (r * self.cols + c, ((r + step * CORES) % self.rows) * self.cols + c)
            for r in range(self.rows)
            for c in range(self.cols)
        ]

    def across(self, row_bit, col_bit):
        return [
            (r * self.cols + c, (r ^ row_bit) * self.cols + (c ^ col_bit))
            for r in range(self.rows)
            for c in range(self.cols)
        ]


def move(value, pairs):
    return lax.ppermute(value, ("row", "col"), pairs)


def ring_gather(own, size, pairs_of):
    found = {0: own}
    ahead = behind = own
    for step in range(1, size // 2 + 1):
        behind = move(behind, pairs_of(1))
        found[size - step] = behind
        if step <= (size - 1) // 2:
            ahead = move(ahead, pairs_of(-1))
            found[step] = ahead
    return [found[k] for k in range(size)]


def ring_scatter(chunks, size, pairs_of):
    def travel(hops, sign):
        running = None
        for hop in range(hops, 0, -1):
            term = chunks[(sign * hop) % size]
            if running is not None:
                term = (running.astype(F32) + term.astype(F32)).astype(BF16)
            running = move(term, pairs_of(sign))
        return running

    total = chunks[0].astype(F32)
    for hops, sign in ((size // 2, 1), ((size - 1) // 2, -1)):
        if hops:
            total = total + travel(hops, sign).astype(F32)
    return total


def summed_everywhere(part, grid):
    row_bits = [1 << k for k in range(grid.rows.bit_length() - 1)]
    col_bits = [1 << k for k in range(grid.cols.bit_length() - 1)]
    held = part.astype(BF16)
    for bit in row_bits:
        half = held.shape[0] // 2
        mine = (grid.row // bit) % 2
        keep = lax.dynamic_slice_in_dim(held, mine * half, half, 0)
        give = lax.dynamic_slice_in_dim(held, (1 - mine) * half, half, 0)
        got = move(give, grid.across(bit, 0))
        held = (keep.astype(F32) + got.astype(F32)).astype(BF16)
    for bit in col_bits:
        got = move(held, grid.across(0, bit))
        held = (held.astype(F32) + got.astype(F32)).astype(BF16)
    for bit in reversed(row_bits):
        got = move(held, grid.across(bit, 0))
        mine = (grid.row // bit) % 2
        held = jnp.where(mine == 0, jnp.concatenate([held, got]), jnp.concatenate([got, held]))
    return held.astype(F32)


def scatter_order(size):
    groups = []
    for step in range(size // 2):
        group = [size // 2 - step]
        back = (size - 1) // 2 - step
        if back > 0:
            group.append(size - back)
        groups.append(group)
    groups[-1].append(0)
    return groups


def ahead_bins(ahead, size):
    order = [k for group in scatter_order(size) for k in group]
    return sum(jnp.where(ahead == k, place, 0) for place, k in enumerate(order))


def arrival_order(size):
    groups = []
    for step in range(1, size // 2 + 1):
        groups.append([size - step] + ([step] if step <= (size - 1) // 2 else []))
    groups[0].append(0)
    return groups


def per_device(features, node_order, tile_vals, tile_coord, tile_count, weight, cotangent):
    nodes_here, feat_width = features.shape
    tile_size = tile_vals.shape[3]
    row_devices = lax.axis_size("row")
    col_devices = lax.axis_size("col")
    piece = nodes_here // tile_size
    block_cols = row_devices * piece
    block_rows = col_devices * piece
    grad_scale = float(nodes_here * row_devices * col_devices) ** (-0.5)
    grid = Grid(row_devices, col_devices)
    chips = grid.chips

    onehot = permuter(node_order, nodes_here)
    placed = reorder(onehot, features)
    tiles = load_tiles(tile_vals[0, 0])
    coord_here = tile_coord[0, 0]
    tile_total = tile_count[0, 0]
    row_of = coord_here // block_cols
    col_of = coord_here % block_cols

    row_dev = col_of // piece
    far = (row_dev // CORES - grid.x) % chips
    swap = (row_dev % CORES - grid.core) % CORES
    col_dev = row_of // piece
    ahead = sum(jnp.where(col_dev == c, grid.ahead_of[c], 0) for c in range(col_devices))
    source_out = (swap * chips + far) * piece + col_of % piece
    table_out = tile_table(ahead_bins(ahead, col_devices) * piece + row_of % piece, block_rows, source_out, tile_total)

    along_x = ring_gather(placed, chips, grid.along_x)
    other_core = [move(block, grid.across(1, 0)) for block in along_x]
    grads_in = reorder(onehot, cotangent)
    chunks = {}
    at = 0
    for group in scatter_order(col_devices):
        made = tile_part(
            False, table_out, (at, len(group) * piece), block_rows, tiles, along_x + other_core, pieces=nodes_here
        )
        chunks.update(zip(group, made))
        at += len(group) * piece
    own_rows = ring_scatter(chunks, col_devices, grid.along_walk).astype(BF16)

    pre_act = jnp.dot(own_rows, weight, preferred_element_type=F32)
    own_act = elu_value(pre_act).astype(BF16)
    own_grad = (grads_in.astype(F32) * elu_slope(pre_act)).astype(BF16)
    own_agg_grad = lax.dot_general(
        own_grad, weight, (((1,), (1,)), ((), ())), preferred_element_type=F32
    ).astype(BF16)
    grad_blocks = ring_gather(own_agg_grad, col_devices, grid.along_walk)
    weight_part = (
        lax.dot_general(own_rows, own_grad, (((0,), (0,)), ((), ())), preferred_element_type=F32)
        * grad_scale
    )
    weight_grad = summed_everywhere(weight_part, grid)

    arrivals = arrival_order(col_devices)
    part_of = sum(jnp.where(ahead == k, p, 0) for p, group in enumerate(arrivals) for k in group)
    block_at = sum(jnp.where(ahead == k, i, 0) for group in arrivals for i, k in enumerate(group))
    place_back = ((far - 1) % chips * CORES + swap) * piece + col_of % piece
    bins_back = len(arrivals) * block_cols
    table_back = tile_table(
        part_of * block_cols + place_back, bins_back, block_at * piece + row_of % piece, tile_total
    )
    acc = None
    for number, group in enumerate(arrivals[:-1]):
        (acc,) = tile_part(
            True,
            table_back,
            (number * block_cols, block_cols),
            bins_back,
            tiles,
            [grad_blocks[k] for k in group],
            acc=acc,
        )
    last = [grad_blocks[k] for k in arrivals[-1]]
    last_bin = (len(arrivals) - 1) * block_cols
    near_bins = CORES * piece
    far_bins = block_cols - near_bins
    far_chunks = tile_part(
        True, table_back, (last_bin, far_bins), bins_back, tiles, last, acc=acc, pieces=nodes_here
    )
    near_chunks = tile_part(
        True,
        table_back,
        (last_bin + far_bins, near_bins),
        bins_back,
        tiles,
        last,
        acc=acc,
        acc_at=far_bins,
        pieces=nodes_here,
    )
    sums = {}
    for distance in range(1, chips):
        mine, theirs = far_chunks[CORES * (distance - 1) : CORES * distance]
        got = move(theirs, grid.across(1, 0))
        sums[distance] = (mine.astype(F32) + got.astype(F32)).astype(BF16)
    got = move(near_chunks[1], grid.across(1, 0))
    sums[0] = near_chunks[0].astype(F32) + got.astype(F32)
    placed_grad = ring_scatter(sums, chips, grid.along_x).astype(BF16)
    activations = restore(onehot, own_act)
    feature_grad = restore(onehot, placed_grad)
    return (activations, weight_grad, feature_grad)


def solution(mesh):
    in_specs = (
        P(("row", "col"), None),
        P(("row", "col")),
        P("row", "col", None, None, None),
        P("row", "col", None),
        P("row", "col"),
        P(),
        P(("row", "col"), None),
    )
    out_specs = (P(("row", "col"), None), P(), P(("row", "col"), None))
    return jax.shard_map(
        per_device, mesh=mesh, in_specs=in_specs, out_specs=out_specs, check_vma=False
    )
```

profile of v0, /device:TPU:0, one launch (start us, length us, event | category | flops | bytes accessed | tf_op | source)
XLA Modules:
  0.0 85.8 jit_solution(3881298439575353617)
XLA Ops:
  0.6 0.7 and_select_fusion.13
  1.4 1.1 %convolution_convert_fusion.4.refs_0_ = bf16[256,256]{1,0:T(8,128)(2,1)S(1)} fusion(bf16[256,256]{1,0:T(8,128)(2,1)} %param.7, s32[256]{0:T(256)S(1)} %and_select_fusion.13), kind=kOutput, calls=%fused_computation.9 | convolution fusion | flops 33685504 | bytes 263168 | tf_op jit(solution)/shard_map/dot_general | solution.py:35
  2.5 0.5 collective-permute-start.1
  3.0 2.6 %collective-permute-start = (bf16[256,256]{1,0:T(8,128)(2,1)S(1)}, bf16[256,256]{1,0:T(8,128)(2,1)S(1)}, u32[]{:S(2)}, u32[]{:S(2)}) collective-permute-start(bf16[256,256]{1,0:T(8,128)(2,1)S(1)} %convolution_convert_fusion.4.refs_0_), channel_id=1, source_target_pairs={{0,16},{1,17},{2,18},{3,19},{4,20},{5,21},{6,22},{7,23},{8,24},{9,... | collective-permute-start | bytes 393224 | tf_op jit(solution)/shard_map/ppermute | solution.py:235
  6.3 0.7 fusion.42
  7.0 0.7 fusion.22
  8.7 0.7 add_add_fusion
  9.9 2.8 %copy-done.4 = bf16[1,1,192,128,128]{4,3,2,1,0:T(8,128)(2,1)S(1)} copy-done((bf16[1,1,192,128,128]{4,3,2,1,0:T(8,128)(2,1)S(1)}, bf16[1,1,192,128,128]{4,3,2,1,0:T(8,128)(2,1)}, u32[]{:S(2)}) %copy-start.4) | copy-done | bytes 6291480
  12.7 0.5 shard_map.94.tiles_ref
  13.2 1.4 %shard_map.96 = (bf16[256,256]{1,0:T(8,128)(2,1)S(1)}, bf16[256,256]{1,0:T(8,128)(2,1)S(1)}) custom-call(s32[342]{0:T(512)S(1)} %pad_add_fusion.table_ref, bf16[193,128,128]{2,1,0:T(8,128)(2,1)S(1)} %shard_map.94.tiles_ref, bf16[256,256]{1,0:T(8,128)(2,1)S(1)} %convolution_convert_fusion.4.refs_0_, bf16[256,256]{1,0:T(8,128)(2,1)S(1)} %collective-permute-done.refs_1_, ...), custom_call_target="tpu_custom_call" | custom-call | flops 402653184 | bytes 1572864 | tf_op jit(solution)/shard_map/pallas_call | solution.py:167
  14.7 2.7 %copy-done.1 = bf16[193,128,128]{2,1,0:T(8,128)(2,1)} copy-done((bf16[193,128,128]{2,1,0:T(8,128)(2,1)}, bf16[193,128,128]{2,1,0:T(8,128)(2,1)S(1)}, u32[]{:S(2)}) %copy-start.1) | copy-done | bytes 6324248
  17.4 1.7 %collective-permute-start.3 = (bf16[256,256]{1,0:T(8,128)(2,1)S(1)}, bf16[256,256]{1,0:T(8,128)(2,1)S(1)}, u32[]{:S(2)}, u32[]{:S(2)}) collective-permute-start(bf16[256,256]{1,0:T(8,128)(2,1)S(1)} %get-tuple-element.16), channel_id=1, source_target_pairs={{0,1},{1,3},{3,5},{5,7},{7,6},{6,4},{4,2},{2,0},{10,12},{12,14},{1... | collective-permute-start | bytes 393224 | tf_op jit(solution)/shard_map/ppermute | solution.py:235
  19.2 1.4 %collective-permute-start.7 = (bf16[256,256]{1,0:T(8,128)(2,1)S(1)}, bf16[256,256]{1,0:T(8,128)(2,1)S(1)}, u32[]{:S(2)}, u32[]{:S(2)}) collective-permute-start(bf16[256,256]{1,0:T(8,128)(2,1)S(1)} %get-tuple-element.20), channel_id=1, source_target_pairs={{0,2},{1,0},{3,1},{5,3},{7,5},{6,7},{4,6},{2,4},{10,8},{12,10},{14... | collective-permute-start | bytes 393224 | tf_op jit(solution)/shard_map/ppermute | solution.py:235
  20.6 2.8 %copy-done.2 = bf16[193,128,128]{2,1,0:T(8,128)(2,1)S(1)} copy-done((bf16[193,128,128]{2,1,0:T(8,128)(2,1)S(1)}, bf16[193,128,128]{2,1,0:T(8,128)(2,1)}, u32[]{:S(2)}) %copy-start.2) | copy-done | bytes 6324248
  23.4 1.2 %shard_map.98 = (bf16[256,256]{1,0:T(8,128)(2,1)S(1)}, bf16[256,256]{1,0:T(8,128)(2,1)S(1)}) custom-call(s32[342]{0:T(512)S(1)} %pad_add_fusion.table_ref, bf16[193,128,128]{2,1,0:T(8,128)(2,1)S(1)} %copy-done.2, bf16[256,256]{1,0:T(8,128)(2,1)S(1)} %convolution_convert_fusion.4.refs_0_, bf16[256,256]{1,0:T(8,128)(2,1)S(1)} %collective-permute-done.refs_1_, ...), custom_call_target="tpu_custom_call" | custom-call | flops 402653184 | bytes 1572864 | tf_op jit(solution)/shard_map/pallas_call | solution.py:167
  24.5 1.4 %shard_map.97 = (bf16[256,256]{1,0:T(8,128)(2,1)S(1)}, bf16[256,256]{1,0:T(8,128)(2,1)S(1)}) custom-call(s32[342]{0:T(512)S(1)} %pad_add_fusion.table_ref, bf16[193,128,128]{2,1,0:T(8,128)(2,1)S(1)} %copy-done.2, bf16[256,256]{1,0:T(8,128)(2,1)S(1)} %convolution_convert_fusion.4.refs_0_, bf16[256,256]{1,0:T(8,128)(2,1)S(1)} %collective-permute-done.refs_1_, ...), custom_call_target="tpu_custom_call" | custom-call | flops 402653184 | bytes 1572864 | tf_op jit(solution)/shard_map/pallas_call | solution.py:167
  26.0 1.2 %shard_map.95 = (bf16[256,256]{1,0:T(8,128)(2,1)S(1)}, bf16[256,256]{1,0:T(8,128)(2,1)S(1)}) custom-call(s32[342]{0:T(512)S(1)} %pad_add_fusion.table_ref, bf16[193,128,128]{2,1,0:T(8,128)(2,1)S(1)} %copy-done.2, bf16[256,256]{1,0:T(8,128)(2,1)S(1)} %convolution_convert_fusion.4.refs_0_, bf16[256,256]{1,0:T(8,128)(2,1)S(1)} %collective-permute-done.refs_1_, ...), custom_call_target="tpu_custom_call" | custom-call | flops 402653184 | bytes 1572864 | tf_op jit(solution)/shard_map/pallas_call | solution.py:167
  27.2 1.0 %collective-permute-start.4 = (bf16[256,256]{1,0:T(8,128)(2,1)S(1)}, bf16[256,256]{1,0:T(8,128)(2,1)S(1)}, u32[]{:S(2)}, u32[]{:S(2)}) collective-permute-start(bf16[256,256]{1,0:T(8,128)(2,1)S(1)} %add_convert_fusion.7), channel_id=1, source_target_pairs={{0,1},{1,3},{3,5},{5,7},{7,6},{6,4},{4,2},{2,0},{10,12},{12,14},{1... | collective-permute-start | bytes 393224 | tf_op jit(solution)/shard_map/ppermute | solution.py:235
  28.2 4.7 %collective-permute-start.8 = (bf16[256,256]{1,0:T(8,128)(2,1)S(1)}, bf16[256,256]{1,0:T(8,128)(2,1)S(1)}, u32[]{:S(2)}, u32[]{:S(2)}) collective-permute-start(bf16[256,256]{1,0:T(8,128)(2,1)S(1)} %add_convert_fusion.4), channel_id=1, source_target_pairs={{0,2},{1,0},{3,1},{5,3},{7,5},{6,7},{4,6},{2,4},{10,8},{12,10},{14... | collective-permute-start | bytes 393224 | tf_op jit(solution)/shard_map/ppermute | solution.py:235
  32.9 2.8 %collective-permute-done.4 = bf16[256,256]{1,0:T(8,128)(2,1)S(1)} collective-permute-done((bf16[256,256]{1,0:T(8,128)(2,1)S(1)}, bf16[256,256]{1,0:T(8,128)(2,1)S(1)}, u32[]{:S(2)}, u32[]{:S(2)}) %collective-permute-start.4) | collective-permute-done | bytes 131104 | tf_op jit(solution)/shard_map/ppermute | solution.py:235
  35.8 0.5 collective-permute-done.8
  36.3 2.5 %collective-permute-start.9 = (bf16[256,256]{1,0:T(8,128)(2,1)S(1)}, bf16[256,256]{1,0:T(8,128)(2,1)S(1)}, u32[]{:S(2)}, u32[]{:S(2)}) collective-permute-start(bf16[256,256]{1,0:T(8,128)(2,1)S(1)} %add_convert_fusion.3), channel_id=1, source_target_pairs={{0,2},{1,0},{3,1},{5,3},{7,5},{6,7},{4,6},{2,4},{10,8},{12,10},{14... | collective-permute-start | bytes 393224 | tf_op jit(solution)/shard_map/ppermute | solution.py:235
  38.8 2.1 %collective-permute-done.5 = bf16[256,256]{1,0:T(8,128)(2,1)S(1)} collective-permute-done((bf16[256,256]{1,0:T(8,128)(2,1)S(1)}, bf16[256,256]{1,0:T(8,128)(2,1)S(1)}, u32[]{:S(2)}, u32[]{:S(2)}) %collective-permute-start.5) | collective-permute-done | bytes 131104 | tf_op jit(solution)/shard_map/ppermute | solution.py:235
  41.1 0.3 collective-permute-done.9
  41.4 4.6 %collective-permute-done.6 = bf16[256,256]{1,0:T(8,128)(2,1)S(1)} collective-permute-done((bf16[256,256]{1,0:T(8,128)(2,1)S(1)}, bf16[256,256]{1,0:T(8,128)(2,1)S(1)}, u32[]{:S(2)}, u32[]{:S(2)}) %collective-permute-start.6) | collective-permute-done | bytes 131104 | tf_op jit(solution)/shard_map/ppermute | solution.py:235
  47.0 1.1 %collective-permute-done.10 = bf16[128,256]{1,0:T(8,128)(2,1)S(1)} collective-permute-done((bf16[128,256]{1,0:T(8,128)(2,1)S(1)}, bf16[128,256]{1,0:T(8,128)(2,1)S(1)}, u32[]{:S(2)}, u32[]{:S(2)}) %collective-permute-start.10) | collective-permute-done | bytes 65568 | tf_op jit(solution)/shard_map/ppermute | solution.py:235
  48.6 3.5 %collective-permute-done.11 = bf16[64,256]{1,0:T(8,128)(2,1)S(1)} collective-permute-done((bf16[64,256]{1,0:T(8,128)(2,1)S(1)}, bf16[64,256]{1,0:T(8,128)(2,1)S(1)}, u32[]{:S(2)}, u32[]{:S(2)}) %collective-permute-start.11) | collective-permute-done | bytes 32800 | tf_op jit(solution)/shard_map/ppermute | solution.py:235
  52.3 2.1 %collective-permute-start.21 = (bf16[256,256]{1,0:T(8,128)(2,1)S(1)}, bf16[256,256]{1,0:T(8,128)(2,1)S(1)}, u32[]{:S(2)}, u32[]{:S(2)}) collective-permute-start(bf16[256,256]{1,0:T(8,128)(2,1)S(1)} %convolution_convert_fusion.1.refs_2_), channel_id=1, source_target_pairs={{0,2},{1,0},{3,1},{5,3},{7,5},{6,7},{4,6},{2,4},{10,8},{12,10},{14... | collective-permute-start | bytes 393224 | tf_op jit(solution)/shard_map/ppermute | solution.py:235
  54.4 2.0 %collective-permute-done.12 = bf16[64,256]{1,0:T(8,128)(2,1)S(1)} collective-permute-done((bf16[64,256]{1,0:T(8,128)(2,1)S(1)}, bf16[64,256]{1,0:T(8,128)(2,1)S(1)}, u32[]{:S(2)}, u32[]{:S(2)}) %collective-permute-start.12) | collective-permute-done | bytes 32800 | tf_op jit(solution)/shard_map/ppermute | solution.py:235
  56.5 1.7 %collective-permute-start.13 = (bf16[64,256]{1,0:T(8,128)(2,1)S(1)}, bf16[64,256]{1,0:T(8,128)(2,1)S(1)}, u32[]{:S(2)}, u32[]{:S(2)}) collective-permute-start(bf16[64,256]{1,0:T(8,128)(2,1)S(1)} %add_convert_fusion.12), channel_id=1, source_target_pairs={{0,2},{1,3},{2,0},{3,1},{4,6},{5,7},{6,4},{7,5},{8,10},{9,11},{10,... | collective-permute-start | bytes 98312 | tf_op jit(solution)/shard_map/ppermute | solution.py:235
  58.3 0.6 collective-permute-done.21.refs_1_
  58.8 1.7 %collective-permute-start.22 = (bf16[256,256]{1,0:T(8,128)(2,1)S(1)}, bf16[256,256]{1,0:T(8,128)(2,1)S(1)}, u32[]{:S(2)}, u32[]{:S(2)}) collective-permute-start(bf16[256,256]{1,0:T(8,128)(2,1)S(1)} %collective-permute-done.21.refs_1_), channel_id=1, source_target_pairs={{0,2},{1,0},{3,1},{5,3},{7,5},{6,7},{4,6},{2,4},{10,8},{12,10},{14... | collective-permute-start | bytes 393224 | tf_op jit(solution)/shard_map/ppermute | solution.py:235
  61.0 2.4 %collective-permute-start.14 = (bf16[64,256]{1,0:T(8,128)(2,1)S(1)}, bf16[64,256]{1,0:T(8,128)(2,1)S(1)}, u32[]{:S(2)}, u32[]{:S(2)}) collective-permute-start(bf16[64,256]{1,0:T(8,128)(2,1)S(1)} %add_convert_fusion.11), channel_id=1, source_target_pairs={{0,4},{1,5},{2,6},{3,7},{4,0},{5,1},{6,2},{7,3},{8,12},{9,13},{10,... | collective-permute-start | bytes 98312 | tf_op jit(solution)/shard_map/ppermute | solution.py:235
  63.4 2.8 %copy-done.3 = bf16[193,128,128]{2,1,0:T(8,128)(2,1)S(1)} copy-done((bf16[193,128,128]{2,1,0:T(8,128)(2,1)S(1)}, bf16[193,128,128]{2,1,0:T(8,128)(2,1)}, u32[]{:S(2)}) %copy-start.3) | copy-done | bytes 6324248
  66.2 1.5 %shard_map.99.refs_2_ = f32[1024,256]{1,0:T(8,128)S(1)} custom-call(s32[438]{0:T(512)S(1)} %pad_add_fusion.1.table_ref, bf16[193,128,128]{2,1,0:T(8,128)(2,1)S(1)} %copy-done.3, bf16[256,256]{1,0:T(8,128)(2,1)S(1)} %collective-permute-done.17.refs_0_, bf16[256,256]{1,0:T(8,128)(2,1)S(1)} %collective-permute-done.21.refs_1_, ...), custom_call_target="tpu_custom_call" | custom-call | flops 402653184 | bytes 1572864 | tf_op jit(solution)/shard_map/pallas_call | solution.py:167
  67.8 3.5 %collective-permute-start.23 = (bf16[256,256]{1,0:T(8,128)(2,1)S(1)}, bf16[256,256]{1,0:T(8,128)(2,1)S(1)}, u32[]{:S(2)}, u32[]{:S(2)}) collective-permute-start(bf16[256,256]{1,0:T(8,128)(2,1)S(1)} %collective-permute-done.22.refs_1_), channel_id=1, source_target_pairs={{0,2},{1,0},{3,1},{5,3},{7,5},{6,7},{4,6},{2,4},{10,8},{12,10},{14... | collective-permute-start | bytes 393224 | tf_op jit(solution)/shard_map/ppermute | solution.py:235
  71.3 1.4 %collective-permute-start.15 = (bf16[64,256]{1,0:T(8,128)(2,1)S(1)}, bf16[64,256]{1,0:T(8,128)(2,1)S(1)}, u32[]{:S(2)}, u32[]{:S(2)}) collective-permute-start(bf16[64,256]{1,0:T(8,128)(2,1)S(1)} %add_convert_fusion.10), channel_id=1, source_target_pairs={{0,16},{1,17},{2,18},{3,19},{4,20},{5,21},{6,22},{7,23},{8,24},{9,... | collective-permute-start | bytes 98312 | tf_op jit(solution)/shard_map/ppermute | solution.py:235
  72.7 1.5 %shard_map.100.refs_2_ = f32[1024,256]{1,0:T(8,128)S(1)} custom-call(s32[438]{0:T(512)S(1)} %pad_add_fusion.1.table_ref, bf16[193,128,128]{2,1,0:T(8,128)(2,1)S(1)} %copy-done.3, bf16[256,256]{1,0:T(8,128)(2,1)S(1)} %collective-permute-done.18.refs_0_, bf16[256,256]{1,0:T(8,128)(2,1)S(1)} %collective-permute-done.22.refs_1_, f32[1024,256]{1,0:T(8,128)S(1)} %shard_map.99.refs_2_), custom_call_target="tpu_custom_call" | custom-call | flops 402653184 | bytes 1572864 | tf_op jit(solution)/shard_map/pallas_call | solution.py:167
  74.3 1.8 %shard_map.101.refs_1_ = f32[1024,256]{1,0:T(8,128)S(1)} custom-call(s32[438]{0:T(512)S(1)} %pad_add_fusion.1.table_ref, bf16[193,128,128]{2,1,0:T(8,128)(2,1)S(1)} %copy-done.3, bf16[256,256]{1,0:T(8,128)(2,1)S(1)} %collective-permute-done.19.refs_0_, bf16[256,256]{1,0:T(8,128)(2,1)S(1)} %collective-permute-done.23.refs_1_, f32[1024,256]{1,0:T(8,128)S(1)} %shard_map.100.refs_2_), custom_call_target="tpu_custom_call" | custom-call | flops 402653184 | bytes 1572864 | tf_op jit(solution)/shard_map/pallas_call | solution.py:167
  76.2 0.9 %shard_map.103 = (bf16[256,256]{1,0:T(8,128)(2,1)S(1)}, bf16[256,256]{1,0:T(8,128)(2,1)S(1)}) custom-call(s32[438]{0:T(512)S(1)} %pad_add_fusion.1.table_ref, bf16[193,128,128]{2,1,0:T(8,128)(2,1)S(1)} %copy-done.3, bf16[256,256]{1,0:T(8,128)(2,1)S(1)} %collective-permute-done.20.refs_0_, f32[1024,256]{1,0:T(8,128)S(1)} %shard_map.101.refs_1_), custom_call_target="tpu_custom_call" | custom-call | flops 201326592 | bytes 786432 | tf_op jit(solution)/shard_map/pallas_call | solution.py:167
  77.3 0.5 collective-permute-start.16
  77.8 0.9 %shard_map.102 = (bf16[256,256]{1,0:T(8,128)(2,1)S(1)}, bf16[256,256]{1,0:T(8,128)(2,1)S(1)}) custom-call(s32[438]{0:T(512)S(1)} %pad_add_fusion.1.table_ref, bf16[193,128,128]{2,1,0:T(8,128)(2,1)S(1)} %copy-done.3, bf16[256,256]{1,0:T(8,128)(2,1)S(1)} %collective-permute-done.20.refs_0_, f32[1024,256]{1,0:T(8,128)S(1)} %shard_map.101.refs_1_), custom_call_target="tpu_custom_call" | custom-call | flops 201326592 | bytes 786432 | tf_op jit(solution)/shard_map/pallas_call | solution.py:167
  78.7 0.4 collective-permute-start.24
  79.1 1.5 %collective-permute-start.26 = (bf16[256,256]{1,0:T(8,128)(2,1)S(1)}, bf16[256,256]{1,0:T(8,128)(2,1)S(1)}, u32[]{:S(2)}, u32[]{:S(2)}) collective-permute-start(bf16[256,256]{1,0:T(8,128)(2,1)S(1)} %add_convert_fusion.1), channel_id=1, source_target_pairs={{0,16},{1,17},{2,18},{3,19},{4,20},{5,21},{6,22},{7,23},{8,24},{9,... | collective-permute-start | bytes 393224 | tf_op jit(solution)/shard_map/ppermute | solution.py:235
  80.6 1.0 %convolution_convert_fusion.3 = bf16[256,256]{1,0:T(8,128)(2,1)} fusion(f32[256,256]{1,0:T(8,128)S(1)} %fusion.44, s32[256]{0:T(256)S(1)} %and_select_fusion.13), kind=kOutput, calls=%fused_computation.8 | convolution fusion | flops 33947648 | bytes 394240 | tf_op jit(solution)/shard_map/dot_general | solution.py:39
  81.6 0.7 fusion.8
  82.4 2.4 %collective-permute-done.26 = bf16[256,256]{1,0:T(8,128)(2,1)S(1)} collective-permute-done((bf16[256,256]{1,0:T(8,128)(2,1)S(1)}, bf16[256,256]{1,0:T(8,128)(2,1)S(1)}, u32[]{:S(2)}, u32[]{:S(2)}) %collective-permute-start.26) | collective-permute-done | bytes 131104 | tf_op jit(solution)/shard_map/ppermute | solution.py:235
  84.8 1.0 %convolution_convert_fusion = bf16[256,256]{1,0:T(8,128)(2,1)} fusion(bf16[256,256]{1,0:T(8,128)(2,1)S(1)} %collective-permute-done.26, bf16[256,256]{1,0:T(8,128)(2,1)S(1)} %collective-permute-done.24, bf16[256,256]{1,0:T(8,128)(2,1)S(1)} %get-tuple-element.23, s32[256]{0:T(256)S(1)} %and_select_fusion.13), kind=kOutput, calls=%fused_computation.2 | convolution fusion | flops 34078720 | bytes 525312 | tf_op jit(solution)/shard_map/dot_general | solution.py:39
  (75 shorter events, 4.4 us)
Async XLA Ops:
  0.6 45.4 %copy-start = (bf16[256,256]{1,0:T(8,128)(2,1)S(1)}, bf16[256,256]{1,0:T(8,128)(2,1)}, u32[]{:S(2)}) copy-start(bf16[256,256]{1,0:T(8,128)(2,1)} %param.12) | copy-start | bytes 393220
  2.5 10.7 %collective-permute-start.1 = (bf16[256,256]{1,0:T(8,128)(2,1)S(1)}, bf16[256,256]{1,0:T(8,128)(2,1)S(1)}, u32[]{:S(2)}, u32[]{:S(2)}) collective-permute-start(bf16[256,256]{1,0:T(8,128)(2,1)S(1)} %convolution_convert_fusion.4.refs_0_), channel_id=1, source_target_pairs={{0,8},{1,9},{2,10},{3,11},{4,12},{5,13},{6,14},{7,15},{8,0},{9,1},... | collective-permute-start | bytes 393224 | tf_op jit(solution)/shard_map/ppermute | solution.py:235
  3.0 6.7 %collective-permute-start = (bf16[256,256]{1,0:T(8,128)(2,1)S(1)}, bf16[256,256]{1,0:T(8,128)(2,1)S(1)}, u32[]{:S(2)}, u32[]{:S(2)}) collective-permute-start(bf16[256,256]{1,0:T(8,128)(2,1)S(1)} %convolution_convert_fusion.4.refs_0_), channel_id=1, source_target_pairs={{0,16},{1,17},{2,18},{3,19},{4,20},{5,21},{6,22},{7,23},{8,24},{9,... | collective-permute-start | bytes 393224 | tf_op jit(solution)/shard_map/ppermute | solution.py:235
  9.7 3.6 %collective-permute-start.2 = (bf16[256,256]{1,0:T(8,128)(2,1)S(1)}, bf16[256,256]{1,0:T(8,128)(2,1)S(1)}, u32[]{:S(2)}, u32[]{:S(2)}) collective-permute-start(bf16[256,256]{1,0:T(8,128)(2,1)S(1)} %collective-permute-done.refs_1_), channel_id=1, source_target_pairs={{0,8},{1,9},{2,10},{3,11},{4,12},{5,13},{6,14},{7,15},{8,0},{9,1},... | collective-permute-start | bytes 393224 | tf_op jit(solution)/shard_map/ppermute | solution.py:235
  9.9 2.8 %copy-start.4 = (bf16[1,1,192,128,128]{4,3,2,1,0:T(8,128)(2,1)S(1)}, bf16[1,1,192,128,128]{4,3,2,1,0:T(8,128)(2,1)}, u32[]{:S(2)}) copy-start(bf16[1,1,192,128,128]{4,3,2,1,0:T(8,128)(2,1)} %param.9) | copy-start | bytes 18874372
  14.7 2.7 %copy-start.1 = (bf16[193,128,128]{2,1,0:T(8,128)(2,1)}, bf16[193,128,128]{2,1,0:T(8,128)(2,1)S(1)}, u32[]{:S(2)}) copy-start(bf16[193,128,128]{2,1,0:T(8,128)(2,1)S(1)} %shard_map.94.tiles_ref) | copy-start | bytes 18972676
  17.4 9.8 %collective-permute-start.3 = (bf16[256,256]{1,0:T(8,128)(2,1)S(1)}, bf16[256,256]{1,0:T(8,128)(2,1)S(1)}, u32[]{:S(2)}, u32[]{:S(2)}) collective-permute-start(bf16[256,256]{1,0:T(8,128)(2,1)S(1)} %get-tuple-element.16), channel_id=1, source_target_pairs={{0,1},{1,3},{3,5},{5,7},{7,6},{6,4},{4,2},{2,0},{10,12},{12,14},{1... | collective-permute-start | bytes 393224 | tf_op jit(solution)/shard_map/ppermute | solution.py:235
  19.2 9.0 %collective-permute-start.7 = (bf16[256,256]{1,0:T(8,128)(2,1)S(1)}, bf16[256,256]{1,0:T(8,128)(2,1)S(1)}, u32[]{:S(2)}, u32[]{:S(2)}) collective-permute-start(bf16[256,256]{1,0:T(8,128)(2,1)S(1)} %get-tuple-element.20), channel_id=1, source_target_pairs={{0,2},{1,0},{3,1},{5,3},{7,5},{6,7},{4,6},{2,4},{10,8},{12,10},{14... | collective-permute-start | bytes 393224 | tf_op jit(solution)/shard_map/ppermute | solution.py:235
  20.6 2.8 %copy-start.2 = (bf16[193,128,128]{2,1,0:T(8,128)(2,1)S(1)}, bf16[193,128,128]{2,1,0:T(8,128)(2,1)}, u32[]{:S(2)}) copy-start(bf16[193,128,128]{2,1,0:T(8,128)(2,1)} %copy-done.1) | copy-start | bytes 18972676
  26.0 20.3 %copy-start.5 = (bf16[256,256]{1,0:T(8,128)(2,1)S(1)}, bf16[256,256]{1,0:T(8,128)(2,1)}, u32[]{:S(2)}) copy-start(bf16[256,256]{1,0:T(8,128)(2,1)} %param.13) | copy-start | bytes 393220
  27.2 8.5 %collective-permute-start.4 = (bf16[256,256]{1,0:T(8,128)(2,1)S(1)}, bf16[256,256]{1,0:T(8,128)(2,1)S(1)}, u32[]{:S(2)}, u32[]{:S(2)}) collective-permute-start(bf16[256,256]{1,0:T(8,128)(2,1)S(1)} %add_convert_fusion.7), channel_id=1, source_target_pairs={{0,1},{1,3},{3,5},{5,7},{7,6},{6,4},{4,2},{2,0},{10,12},{12,14},{1... | collective-permute-start | bytes 393224 | tf_op jit(solution)/shard_map/ppermute | solution.py:235
  28.2 8.1 %collective-permute-start.8 = (bf16[256,256]{1,0:T(8,128)(2,1)S(1)}, bf16[256,256]{1,0:T(8,128)(2,1)S(1)}, u32[]{:S(2)}, u32[]{:S(2)}) collective-permute-start(bf16[256,256]{1,0:T(8,128)(2,1)S(1)} %add_convert_fusion.4), channel_id=1, source_target_pairs={{0,2},{1,0},{3,1},{5,3},{7,5},{6,7},{4,6},{2,4},{10,8},{12,10},{14... | collective-permute-start | bytes 393224 | tf_op jit(solution)/shard_map/ppermute | solution.py:235
  35.7 5.2 %collective-permute-start.5 = (bf16[256,256]{1,0:T(8,128)(2,1)S(1)}, bf16[256,256]{1,0:T(8,128)(2,1)S(1)}, u32[]{:S(2)}, u32[]{:S(2)}) collective-permute-start(bf16[256,256]{1,0:T(8,128)(2,1)S(1)} %add_convert_fusion.6), channel_id=1, source_target_pairs={{0,1},{1,3},{3,5},{5,7},{7,6},{6,4},{4,2},{2,0},{10,12},{12,14},{1... | collective-permute-start | bytes 393224 | tf_op jit(solution)/shard_map/ppermute | solution.py:235
  36.3 5.1 %collective-permute-start.9 = (bf16[256,256]{1,0:T(8,128)(2,1)S(1)}, bf16[256,256]{1,0:T(8,128)(2,1)S(1)}, u32[]{:S(2)}, u32[]{:S(2)}) collective-permute-start(bf16[256,256]{1,0:T(8,128)(2,1)S(1)} %add_convert_fusion.3), channel_id=1, source_target_pairs={{0,2},{1,0},{3,1},{5,3},{7,5},{6,7},{4,6},{2,4},{10,8},{12,10},{14... | collective-permute-start | bytes 393224 | tf_op jit(solution)/shard_map/ppermute | solution.py:235
  41.0 5.0 %collective-permute-start.6 = (bf16[256,256]{1,0:T(8,128)(2,1)S(1)}, bf16[256,256]{1,0:T(8,128)(2,1)S(1)}, u32[]{:S(2)}, u32[]{:S(2)}) collective-permute-start(bf16[256,256]{1,0:T(8,128)(2,1)S(1)} %add_convert_fusion.5), channel_id=1, source_target_pairs={{0,1},{1,3},{3,5},{5,7},{7,6},{6,4},{4,2},{2,0},{10,12},{12,14},{1... | collective-permute-start | bytes 393224 | tf_op jit(solution)/shard_map/ppermute | solution.py:235
  46.8 1.3 %collective-permute-start.10 = (bf16[128,256]{1,0:T(8,128)(2,1)S(1)}, bf16[128,256]{1,0:T(8,128)(2,1)S(1)}, u32[]{:S(2)}, u32[]{:S(2)}) collective-permute-start(bf16[128,256]{1,0:T(8,128)(2,1)S(1)} %constant_dynamic-slice_fusion.1), channel_id=1, source_target_pairs={{0,8},{1,9},{2,10},{3,11},{4,12},{5,13},{6,14},{7,15},{8,0},{9,1},... | collective-permute-start | bytes 196616 | tf_op jit(solution)/shard_map/ppermute | solution.py:235
  48.1 4.0 %collective-permute-start.11 = (bf16[64,256]{1,0:T(8,128)(2,1)S(1)}, bf16[64,256]{1,0:T(8,128)(2,1)S(1)}, u32[]{:S(2)}, u32[]{:S(2)}) collective-permute-start(bf16[64,256]{1,0:T(8,128)(2,1)S(1)} %constant_dynamic-slice_fusion), channel_id=1, source_target_pairs={{0,16},{1,17},{2,18},{3,19},{4,20},{5,21},{6,22},{7,23},{8,24},{9,... | collective-permute-start | bytes 98312 | tf_op jit(solution)/shard_map/ppermute | solution.py:235
  48.4 5.9 %collective-permute-start.17 = (bf16[256,256]{1,0:T(8,128)(2,1)S(1)}, bf16[256,256]{1,0:T(8,128)(2,1)S(1)}, u32[]{:S(2)}, u32[]{:S(2)}) collective-permute-start(bf16[256,256]{1,0:T(8,128)(2,1)S(1)} %convolution_convert_fusion.1.refs_2_), channel_id=1, source_target_pairs={{0,1},{1,3},{3,5},{5,7},{7,6},{6,4},{4,2},{2,0},{10,12},{12,14},{1... | collective-permute-start | bytes 393224 | tf_op jit(solution)/shard_map/ppermute | solution.py:235
  52.1 4.3 %collective-permute-start.12 = (bf16[64,256]{1,0:T(8,128)(2,1)S(1)}, bf16[64,256]{1,0:T(8,128)(2,1)S(1)}, u32[]{:S(2)}, u32[]{:S(2)}) collective-permute-start(bf16[64,256]{1,0:T(8,128)(2,1)S(1)} %add_convert_fusion.13), channel_id=1, source_target_pairs={{0,1},{1,0},{2,3},{3,2},{4,5},{5,4},{6,7},{7,6},{8,9},{9,8},{10,11... | collective-permute-start | bytes 98312 | tf_op jit(solution)/shard_map/ppermute | solution.py:235
  52.3 6.5 %collective-permute-start.21 = (bf16[256,256]{1,0:T(8,128)(2,1)S(1)}, bf16[256,256]{1,0:T(8,128)(2,1)S(1)}, u32[]{:S(2)}, u32[]{:S(2)}) collective-permute-start(bf16[256,256]{1,0:T(8,128)(2,1)S(1)} %convolution_convert_fusion.1.refs_2_), channel_id=1, source_target_pairs={{0,2},{1,0},{3,1},{5,3},{7,5},{6,7},{4,6},{2,4},{10,8},{12,10},{14... | collective-permute-start | bytes 393224 | tf_op jit(solution)/shard_map/ppermute | solution.py:235
  54.4 6.2 %collective-permute-start.18 = (bf16[256,256]{1,0:T(8,128)(2,1)S(1)}, bf16[256,256]{1,0:T(8,128)(2,1)S(1)}, u32[]{:S(2)}, u32[]{:S(2)}) collective-permute-start(bf16[256,256]{1,0:T(8,128)(2,1)S(1)} %collective-permute-done.17.refs_0_), channel_id=1, source_target_pairs={{0,1},{1,3},{3,5},{5,7},{7,6},{6,4},{4,2},{2,0},{10,12},{12,14},{1... | collective-permute-start | bytes 393224 | tf_op jit(solution)/shard_map/ppermute | solution.py:235
  56.5 4.5 %collective-permute-start.13 = (bf16[64,256]{1,0:T(8,128)(2,1)S(1)}, bf16[64,256]{1,0:T(8,128)(2,1)S(1)}, u32[]{:S(2)}, u32[]{:S(2)}) collective-permute-start(bf16[64,256]{1,0:T(8,128)(2,1)S(1)} %add_convert_fusion.12), channel_id=1, source_target_pairs={{0,2},{1,3},{2,0},{3,1},{4,6},{5,7},{6,4},{7,5},{8,10},{9,11},{10,... | collective-permute-start | bytes 98312 | tf_op jit(solution)/shard_map/ppermute | solution.py:235
  58.8 8.9 %collective-permute-start.22 = (bf16[256,256]{1,0:T(8,128)(2,1)S(1)}, bf16[256,256]{1,0:T(8,128)(2,1)S(1)}, u32[]{:S(2)}, u32[]{:S(2)}) collective-permute-start(bf16[256,256]{1,0:T(8,128)(2,1)S(1)} %collective-permute-done.21.refs_1_), channel_id=1, source_target_pairs={{0,2},{1,0},{3,1},{5,3},{7,5},{6,7},{4,6},{2,4},{10,8},{12,10},{14... | collective-permute-start | bytes 393224 | tf_op jit(solution)/shard_map/ppermute | solution.py:235
  60.5 10.7 %collective-permute-start.19 = (bf16[256,256]{1,0:T(8,128)(2,1)S(1)}, bf16[256,256]{1,0:T(8,128)(2,1)S(1)}, u32[]{:S(2)}, u32[]{:S(2)}) collective-permute-start(bf16[256,256]{1,0:T(8,128)(2,1)S(1)} %collective-permute-done.18.refs_0_), channel_id=1, source_target_pairs={{0,1},{1,3},{3,5},{5,7},{7,6},{6,4},{4,2},{2,0},{10,12},{12,14},{1... | collective-permute-start | bytes 393224 | tf_op jit(solution)/shard_map/ppermute | solution.py:235
  61.0 10.3 %collective-permute-start.14 = (bf16[64,256]{1,0:T(8,128)(2,1)S(1)}, bf16[64,256]{1,0:T(8,128)(2,1)S(1)}, u32[]{:S(2)}, u32[]{:S(2)}) collective-permute-start(bf16[64,256]{1,0:T(8,128)(2,1)S(1)} %add_convert_fusion.11), channel_id=1, source_target_pairs={{0,4},{1,5},{2,6},{3,7},{4,0},{5,1},{6,2},{7,3},{8,12},{9,13},{10,... | collective-permute-start | bytes 98312 | tf_op jit(solution)/shard_map/ppermute | solution.py:235
  63.4 2.8 %copy-start.3 = (bf16[193,128,128]{2,1,0:T(8,128)(2,1)S(1)}, bf16[193,128,128]{2,1,0:T(8,128)(2,1)}, u32[]{:S(2)}) copy-start(bf16[193,128,128]{2,1,0:T(8,128)(2,1)} %copy-done.1) | copy-start | bytes 18972676
  67.8 6.5 %collective-permute-start.23 = (bf16[256,256]{1,0:T(8,128)(2,1)S(1)}, bf16[256,256]{1,0:T(8,128)(2,1)S(1)}, u32[]{:S(2)}, u32[]{:S(2)}) collective-permute-start(bf16[256,256]{1,0:T(8,128)(2,1)S(1)} %collective-permute-done.22.refs_1_), channel_id=1, source_target_pairs={{0,2},{1,0},{3,1},{5,3},{7,5},{6,7},{4,6},{2,4},{10,8},{12,10},{14... | collective-permute-start | bytes 393224 | tf_op jit(solution)/shard_map/ppermute | solution.py:235
  71.3 5.0 %collective-permute-start.20 = (bf16[256,256]{1,0:T(8,128)(2,1)S(1)}, bf16[256,256]{1,0:T(8,128)(2,1)S(1)}, u32[]{:S(2)}, u32[]{:S(2)}) collective-permute-start(bf16[256,256]{1,0:T(8,128)(2,1)S(1)} %collective-permute-done.19.refs_0_), channel_id=1, source_target_pairs={{0,1},{1,3},{3,5},{5,7},{7,6},{6,4},{4,2},{2,0},{10,12},{12,14},{1... | collective-permute-start | bytes 393224 | tf_op jit(solution)/shard_map/ppermute | solution.py:235
  71.3 5.9 %collective-permute-start.15 = (bf16[64,256]{1,0:T(8,128)(2,1)S(1)}, bf16[64,256]{1,0:T(8,128)(2,1)S(1)}, u32[]{:S(2)}, u32[]{:S(2)}) collective-permute-start(bf16[64,256]{1,0:T(8,128)(2,1)S(1)} %add_convert_fusion.10), channel_id=1, source_target_pairs={{0,16},{1,17},{2,18},{3,19},{4,20},{5,21},{6,22},{7,23},{8,24},{9,... | collective-permute-start | bytes 98312 | tf_op jit(solution)/shard_map/ppermute | solution.py:235
  77.1 1.9 %collective-permute-start.25 = (bf16[256,256]{1,0:T(8,128)(2,1)S(1)}, bf16[256,256]{1,0:T(8,128)(2,1)S(1)}, u32[]{:S(2)}, u32[]{:S(2)}) collective-permute-start(bf16[256,256]{1,0:T(8,128)(2,1)S(1)} %get-tuple-element.26), channel_id=1, source_target_pairs={{0,8},{1,9},{2,10},{3,11},{4,12},{5,13},{6,14},{7,15},{8,0},{9,1},... | collective-permute-start | bytes 393224 | tf_op jit(solution)/shard_map/ppermute | solution.py:235
  77.3 4.4 %collective-permute-start.16 = (bf16[128,256]{1,0:T(8,128)(2,1)S(1)}, bf16[128,256]{1,0:T(8,128)(2,1)S(1)}, u32[]{:S(2)}, u32[]{:S(2)}) collective-permute-start(bf16[128,256]{1,0:T(8,128)(2,1)S(1)} %maximum_select_fusion.1), channel_id=1, source_target_pairs={{0,8},{1,9},{2,10},{3,11},{4,12},{5,13},{6,14},{7,15},{8,0},{9,1},... | collective-permute-start | bytes 196616 | tf_op jit(solution)/shard_map/ppermute | solution.py:235
  78.7 3.6 %collective-permute-start.24 = (bf16[256,256]{1,0:T(8,128)(2,1)S(1)}, bf16[256,256]{1,0:T(8,128)(2,1)S(1)}, u32[]{:S(2)}, u32[]{:S(2)}) collective-permute-start(bf16[256,256]{1,0:T(8,128)(2,1)S(1)} %get-tuple-element.24), channel_id=1, source_target_pairs={{0,8},{1,9},{2,10},{3,11},{4,12},{5,13},{6,14},{7,15},{8,0},{9,1},... | collective-permute-start | bytes 393224 | tf_op jit(solution)/shard_map/ppermute | solution.py:235
  79.1 5.7 %collective-permute-start.26 = (bf16[256,256]{1,0:T(8,128)(2,1)S(1)}, bf16[256,256]{1,0:T(8,128)(2,1)S(1)}, u32[]{:S(2)}, u32[]{:S(2)}) collective-permute-start(bf16[256,256]{1,0:T(8,128)(2,1)S(1)} %add_convert_fusion.1), channel_id=1, source_target_pairs={{0,16},{1,17},{2,18},{3,19},{4,20},{5,21},{6,22},{7,23},{8,24},{9,... | collective-permute-start | bytes 393224 | tf_op jit(solution)/shard_map/ppermute | solution.py:235
where the time goes:
time: 87.3 us; the launch traced here: 85.8 us
  starting transfers between devices  30.7 us (35%)
  waiting for transfers between devices  20.4 us (23%)
  Pallas kernels  12.3 us (14%)
  local copies, waits for them, and re-layouts  11.2 us (13%)
  other arithmetic  5.46 us (6%)
  matrix products  4.01 us (5%)
  between operations  1.74 us (2%)
    ppermute x27, starting transfers between devices, move(): return lax.ppermute(value, ('row', 'col'), pairs)  30.7 us
    ppermute x27, waiting for transfers between devices, move(): return lax.ppermute(value, ('row', 'col'), pairs)  20.4 us
    pallas_call x9, Pallas kernels, tile_part(): pl.pallas_call(functools.partial(part_kernel, spec), out_shape=out_shape,...  11.8 us
    unnamed x12, local copies, waits for them, and re-layouts  11.1 us
    dot_general x2, matrix products, restore(): lax.dot_general(onehot, values, (((0,), (0,)), ((), ())), preferred_eleme...  1.99 us
  transfers between devices with their start and end apart: 27, of which 13 were waited for; matrix products, arithmetic and copies ran while one was open for 7% of the time, Pallas kernels for 13%

commit v1 on v0

--- a/solution.py
+++ b/solution.py
@@ -10,10 +10,11 @@
 CORES = 2
 GROUP = 4
 UNROLL = 2
-LOADS = 4
 PACK_BITS = 8
 PACK = 1 << PACK_BITS
-VMEM_BYTES = 40 * 1024 * 1024
+VMEM_BYTES = 16 * 1024 * 1024
+LOAD_BYTES = 45 * 1024 * 1024
+LOADS = 4
 F32 = jnp.float32
 BF16 = jnp.bfloat16
 
@@ -40,7 +41,7 @@
     return moved.astype(BF16)
 
 
-def tile_table(bins, bin_total, sources, tile_total):
+def tile_table(bins, bin_total, sources, tile_total, empty):
     slot_total = bins.shape[0]
     group_total = slot_total // GROUP + bin_total + 1
     slots = jnp.arange(slot_total, dtype=jnp.int32)
@@ -56,7 +57,6 @@
     mine = jnp.sum(jnp.where(marks[None, :] < held[:, None], groups[None, :], 0), axis=1)
     place = jnp.where(live, mine * GROUP + before, -1)
     places = jnp.arange(group_total * GROUP, dtype=jnp.int32)
-    empty = slot_total * PACK
     member = (slots * PACK + sources - empty)[None, :]
     members = empty + jnp.sum(jnp.where(place[None, :] == places[:, None], member, 0), axis=1)
     numbers = jnp.arange(group_total, dtype=jnp.int32)
@@ -65,8 +65,7 @@
 
 
 def load_kernel(tiles_ref, out_ref, sems):
-    slot_total = tiles_ref.shape[0]
-    share = slot_total // LOADS
+    share = tiles_ref.shape[0] // LOADS
     copies = [
         pltpu.make_async_copy(
             tiles_ref.at[pl.ds(k * share, share)], out_ref.at[pl.ds(k * share, share)], sems.at[k]
@@ -75,42 +74,35 @@
     ]
     for copy in copies:
         copy.start()
-    out_ref[slot_total] = jnp.zeros(out_ref.shape[1:], out_ref.dtype)
     for copy in copies:
         copy.wait()
 
 
 def load_tiles(tiles):
-    slot_total, tile_size, _ = tiles.shape
-    nbytes = 2 * slot_total * tile_size * tile_size
     return pl.pallas_call(
         load_kernel,
-        out_shape=jax.ShapeDtypeStruct((slot_total + 1, tile_size, tile_size), BF16),
+        out_shape=jax.ShapeDtypeStruct(tiles.shape, tiles.dtype),
         in_specs=[pl.BlockSpec(memory_space=pl.ANY)],
         out_specs=pl.BlockSpec(memory_space=pltpu.VMEM),
         scratch_shapes=[pltpu.SemaphoreType.DMA((LOADS,))],
-        compiler_params=pltpu.CompilerParams(vmem_limit_bytes=VMEM_BYTES),
-        cost_estimate=pl.CostEstimate(flops=0, bytes_accessed=nbytes, transcendentals=0),
+        compiler_params=pltpu.CompilerParams(vmem_limit_bytes=LOAD_BYTES),
+        cost_estimate=pl.CostEstimate(flops=0, bytes_accessed=2 * tiles.size, transcendentals=0),
     )(tiles)
 
 
 def part_kernel(spec, table_ref, tiles_ref, *refs):
     transposed, first_bin, bin_count, bin_total, source_count, carried, finish = spec
     source_refs = refs[:source_count]
-    acc_ref = refs[source_count] if carried is not None else None
-    out_refs = refs[source_count + (carried is not None) : -2]
+    out_refs = refs[source_count + carried : -2]
     source, total = refs[-2:]
-    slot_total = tiles_ref.shape[0] - 1
-    tile_size = tiles_ref.shape[1]
+    slot_total, tile_size, _ = tiles_ref.shape
     group_total = slot_total // GROUP + bin_total + 1
     at = 0
     for ref in source_refs:
         source[at : at + ref.shape[0], :] = ref[...]
         at += ref.shape[0]
-    if carried is None:
-        total[...] = jnp.zeros_like(total)
-    else:
-        total[...] = acc_ref[carried * tile_size : carried * tile_size + total.shape[0], :]
+    source[at:, :] = jnp.zeros((source.shape[0] - at, source.shape[1]), source.dtype)
+    total[...] = refs[source_count][...] if carried else jnp.zeros_like(total)
     bins_at = group_total * GROUP
     firsts_at = bins_at + group_total
     begin = table_ref[firsts_at + first_bin]
@@ -150,9 +142,9 @@
         out_refs[0][...] = total[...]
 
 
-def tile_part(transposed, table, bins, bin_total, tiles, sources, acc=None, acc_at=0, pieces=None):
+def tile_part(transposed, table, bins, bin_total, tiles, sources, empty, acc=None, pieces=None):
     first_bin, bin_count = bins
-    slot_total, tile_size = tiles.shape[0] - 1, tiles.shape[1]
+    slot_total, tile_size, _ = tiles.shape
     width = sources[0].shape[1]
     rows = bin_count * tile_size
     vmem = pl.BlockSpec(memory_space=pltpu.VMEM)
@@ -160,7 +152,7 @@
         out_shape = [jax.ShapeDtypeStruct((rows, width), F32)]
     else:
         out_shape = [jax.ShapeDtypeStruct((pieces, width), BF16)] * (rows // pieces)
-    carried = None if acc is None else acc_at
+    carried = acc is not None
     share = slot_total * bin_count // bin_total
     given = [table, tiles, *sources] + ([] if acc is None else [acc])
     spec = (transposed, first_bin, bin_count, bin_total, len(sources), carried, pieces is not None)
@@ -170,7 +162,7 @@
         in_specs=[pl.BlockSpec(memory_space=pltpu.SMEM)] + [vmem] * (len(given) - 1),
         out_specs=[vmem] * len(out_shape),
         scratch_shapes=[
-            pltpu.VMEM((sum(source.shape[0] for source in sources), width), BF16),
+            pltpu.VMEM(((empty + 1) * tile_size, width), BF16),
             pltpu.VMEM((rows, width), F32),
         ],
         compiler_params=pltpu.CompilerParams(vmem_limit_bytes=VMEM_BYTES),
@@ -235,54 +227,20 @@
     return lax.ppermute(value, ("row", "col"), pairs)
 
 
+def after(value, *others):
+    return lax.optimization_barrier((value, *others))[0]
+
+
 def ring_gather(own, size, pairs_of):
-    found = {0: own}
+    yield {0: own}
     ahead = behind = own
     for step in range(1, size // 2 + 1):
         behind = move(behind, pairs_of(1))
-        found[size - step] = behind
+        found = {size - step: behind}
         if step <= (size - 1) // 2:
             ahead = move(ahead, pairs_of(-1))
             found[step] = ahead
-    return [found[k] for k in range(size)]
-
-
-def ring_scatter(chunks, size, pairs_of):
-    def travel(hops, sign):
-        running = None
-        for hop in range(hops, 0, -1):
-            term = chunks[(sign * hop) % size]
-            if running is not None:
-                term = (running.astype(F32) + term.astype(F32)).astype(BF16)
-            running = move(term, pairs_of(sign))
-        return running
-
-    total = chunks[0].astype(F32)
-    for hops, sign in ((size // 2, 1), ((size - 1) // 2, -1)):
-        if hops:
-            total = total + travel(hops, sign).astype(F32)
-    return total
-
-
-def summed_everywhere(part, grid):
-    row_bits = [1 << k for k in range(grid.rows.bit_length() - 1)]
-    col_bits = [1 << k for k in range(grid.cols.bit_length() - 1)]
-    held = part.astype(BF16)
-    for bit in row_bits:
-        half = held.shape[0] // 2
-        mine = (grid.row // bit) % 2
-        keep = lax.dynamic_slice_in_dim(held, mine * half, half, 0)
-        give = lax.dynamic_slice_in_dim(held, (1 - mine) * half, half, 0)
-        got = move(give, grid.across(bit, 0))
-        held = (keep.astype(F32) + got.astype(F32)).astype(BF16)
-    for bit in col_bits:
-        got = move(held, grid.across(0, bit))
-        held = (held.astype(F32) + got.astype(F32)).astype(BF16)
-    for bit in reversed(row_bits):
-        got = move(held, grid.across(bit, 0))
-        mine = (grid.row // bit) % 2
-        held = jnp.where(mine == 0, jnp.concatenate([held, got]), jnp.concatenate([got, held]))
-    return held.astype(F32)
+        yield found
 
 
 def scatter_order(size):
@@ -303,11 +261,45 @@
 
 
 def arrival_order(size):
-    groups = []
+    groups = [[0]]
     for step in range(1, size // 2 + 1):
         groups.append([size - step] + ([step] if step <= (size - 1) // 2 else []))
-    groups[0].append(0)
     return groups
+
+
+def ring_scatter(chunks_of, size, pairs_of):
+    ahead = behind = None
+
+    def onward(running, term):
+        return term if running is None else (running.astype(F32) + term.astype(F32)).astype(BF16)
+
+    for step, group in enumerate(scatter_order(size)):
+        terms = dict(zip(group, chunks_of(step, ahead)))
+        hop, back = size // 2 - step, (size - 1) // 2 - step
+        ahead = move(onward(ahead, terms[hop]), pairs_of(1))
+        if back > 0:
+            behind = move(onward(behind, terms[size - back]), pairs_of(-1))
+    total = terms[0].astype(F32) + ahead.astype(F32)
+    return total if behind is None else total + behind.astype(F32)
+
+
+def summed_everywhere(part, grid, gate):
+    held = after(part.astype(BF16), *gate)
+    got = move(held, grid.across(1, 0))
+    yield None
+    half = held.shape[0] // CORES
+    chip = (held.astype(F32) + after(got, *gate).astype(F32)).astype(BF16)
+    held = jnp.where(grid.core == 0, chip[:half], chip[half:])
+    bits = [(1 << k, 0) for k in range(1, grid.rows.bit_length() - 1)]
+    bits += [(0, 1 << k) for k in range(grid.cols.bit_length() - 1)]
+    for row_bit, col_bit in bits:
+        got = move(held, grid.across(row_bit, col_bit))
+        yield None
+        held = (held.astype(F32) + after(got, *gate).astype(F32)).astype(BF16)
+    got = move(held, grid.across(1, 0))
+    yield None
+    own_first, own_last = jnp.concatenate([held, got]), jnp.concatenate([got, held])
+    yield jnp.where(grid.core == 0, own_first, own_last).astype(F32)
 
 
 def per_device(features, node_order, tile_vals, tile_coord, tile_count, weight, cotangent):
@@ -336,20 +328,28 @@
     col_dev = row_of // piece
     ahead = sum(jnp.where(col_dev == c, grid.ahead_of[c], 0) for c in range(col_devices))
     source_out = (swap * chips + far) * piece + col_of % piece
-    table_out = tile_table(ahead_bins(ahead, col_devices) * piece + row_of % piece, block_rows, source_out, tile_total)
-
-    along_x = ring_gather(placed, chips, grid.along_x)
-    other_core = [move(block, grid.across(1, 0)) for block in along_x]
+    bins_out = ahead_bins(ahead, col_devices) * piece + row_of % piece
+    table_out = tile_table(bins_out, block_rows, source_out, tile_total, block_cols)
+
+    along_x = {}
+    for found in ring_gather(placed, chips, grid.along_x):
+        along_x.update(found)
+    along_x = [along_x[k] for k in range(chips)]
+    sources_out = along_x + [move(block, grid.across(1, 0)) for block in along_x]
     grads_in = reorder(onehot, cotangent)
-    chunks = {}
-    at = 0
-    for group in scatter_order(col_devices):
-        made = tile_part(
-            False, table_out, (at, len(group) * piece), block_rows, tiles, along_x + other_core, pieces=nodes_here
+    order = scatter_order(col_devices)
+    edges = [sum(len(group) for group in order[:k]) * piece for k in range(len(order) + 1)]
+
+    def chunks_of(step, arrived):
+        table = table_out if step < 2 else after(table_out, earlier[step - 1])
+        earlier.append(arrived)
+        bins = (edges[step], edges[step + 1] - edges[step])
+        return tile_part(
+            False, table, bins, block_rows, tiles, sources_out, block_cols, pieces=nodes_here
         )
-        chunks.update(zip(group, made))
-        at += len(group) * piece
-    own_rows = ring_scatter(chunks, col_devices, grid.along_walk).astype(BF16)
+
+    earlier = []
+    own_rows = ring_scatter(chunks_of, col_devices, grid.along_walk).astype(BF16)
 
     pre_act = jnp.dot(own_rows, weight, preferred_element_type=F32)
     own_act = elu_value(pre_act).astype(BF16)
@@ -357,59 +357,54 @@
     own_agg_grad = lax.dot_general(
         own_grad, weight, (((1,), (1,)), ((), ())), preferred_element_type=F32
     ).astype(BF16)
-    grad_blocks = ring_gather(own_agg_grad, col_devices, grid.along_walk)
+    activations = restore(onehot, own_act)
+
+    arrivals = arrival_order(col_devices)
+    part_of = sum(jnp.where(ahead == k, p, 0) for p, group in enumerate(arrivals) for k in group)
+    block_at = sum(jnp.where(ahead == k, i, 0) for group in arrivals for i, k in enumerate(group))
+    place_back = (swap * chips + far) * piece + col_of % piece
+    bins_back = len(arrivals) * block_cols
+    empty_back = max(len(group) for group in arrivals) * piece
+    table_back = tile_table(
+        part_of * block_cols + place_back,
+        bins_back,
+        block_at * piece + row_of % piece,
+        tile_total,
+        empty_back,
+    )
     weight_part = (
         lax.dot_general(own_rows, own_grad, (((0,), (0,)), ((), ())), preferred_element_type=F32)
         * grad_scale
     )
-    weight_grad = summed_everywhere(weight_part, grid)
-
-    arrivals = arrival_order(col_devices)
-    part_of = sum(jnp.where(ahead == k, p, 0) for p, group in enumerate(arrivals) for k in group)
-    block_at = sum(jnp.where(ahead == k, i, 0) for group in arrivals for i, k in enumerate(group))
-    place_back = ((far - 1) % chips * CORES + swap) * piece + col_of % piece
-    bins_back = len(arrivals) * block_cols
-    table_back = tile_table(
-        part_of * block_cols + place_back, bins_back, block_at * piece + row_of % piece, tile_total
+    acc, gate, weight_grad = None, [], None
+    weight_steps = summed_everywhere(weight_part, grid, gate)
+    for number, found in enumerate(ring_gather(own_agg_grad, col_devices, grid.along_walk)):
+        blocks = [found[k] for k in arrivals[number]]
+        if number == len(arrivals) - 1:
+            break
+        bins = (number * block_cols, block_cols)
+        (acc,) = tile_part(True, table_back, bins, bins_back, tiles, blocks, empty_back, acc=acc)
+        gate[:] = [found[number]] if number in found and number else []
+        if number == 3:
+            gate.append(activations)
+        weight_grad = next(weight_steps, weight_grad)
+    bins = ((len(arrivals) - 1) * block_cols, block_cols)
+    mine, theirs = tile_part(
+        True, table_back, bins, bins_back, tiles, blocks, empty_back, acc=acc, pieces=chips * nodes_here
     )
-    acc = None
-    for number, group in enumerate(arrivals[:-1]):
-        (acc,) = tile_part(
-            True,
-            table_back,
-            (number * block_cols, block_cols),
-            bins_back,
-            tiles,
-            [grad_blocks[k] for k in group],
-            acc=acc,
-        )
-    last = [grad_blocks[k] for k in arrivals[-1]]
-    last_bin = (len(arrivals) - 1) * block_cols
-    near_bins = CORES * piece
-    far_bins = block_cols - near_bins
-    far_chunks = tile_part(
-        True, table_back, (last_bin, far_bins), bins_back, tiles, last, acc=acc, pieces=nodes_here
-    )
-    near_chunks = tile_part(
-        True,
-        table_back,
-        (last_bin + far_bins, near_bins),
-        bins_back,
-        tiles,
-        last,
-        acc=acc,
-        acc_at=far_bins,
-        pieces=nodes_here,
-    )
-    sums = {}
-    for distance in range(1, chips):
-        mine, theirs = far_chunks[CORES * (distance - 1) : CORES * distance]
-        got = move(theirs, grid.across(1, 0))
-        sums[distance] = (mine.astype(F32) + got.astype(F32)).astype(BF16)
-    got = move(near_chunks[1], grid.across(1, 0))
-    sums[0] = near_chunks[0].astype(F32) + got.astype(F32)
-    placed_grad = ring_scatter(sums, chips, grid.along_x).astype(BF16)
-    activations = restore(onehot, own_act)
+    gate[:] = [mine]
+    weight_grad = next(weight_steps, weight_grad)
+    got = move(theirs, grid.across(1, 0))
+    both = mine.astype(F32) + got.astype(F32)
+    sums = [both[k * nodes_here : (k + 1) * nodes_here] for k in range(chips)]
+    sums = [sums[0]] + [term.astype(BF16) for term in sums[1:]]
+    gate[:] = sums[1:]
+    while weight_grad is None:
+        weight_grad = next(weight_steps)
+    order = scatter_order(chips)
+    placed_grad = ring_scatter(
+        lambda step, arrived: [sums[k] for k in order[step]], chips, grid.along_x
+    ).astype(BF16)
     feature_grad = restore(onehot, placed_grad)
     return (activations, weight_grad, feature_grad)
 

time: 87.3 us -> 80.7 us (0.924); the launches traced: 85.8 us -> 80.1 us
  local copies, waits for them, and re-layouts: 11.2 us -> 0.18 us
  waiting for transfers between devices: 20.4 us -> 28.8 us
  starting transfers between devices: 30.7 us -> 27.6 us
    unnamed x12 -> x4, local copies, waits for them, and re-layouts: 11.1 us -> 0.02 us
    ppermute x27 -> x25, waiting for transfers between devices: 20.4 us -> 28.8 us  [move(): return lax.ppermute(value, ('row', 'col'), pairs)]
    ppermute x27 -> x25, starting transfers between devices: 30.7 us -> 27.6 us  [move(): return lax.ppermute(value, ('row', 'col'), pairs)]
    pallas_call x1, Pallas kernels: 0.47 us -> 2.87 us  [load_tiles(): pl.pallas_call(load_kernel, out_shape=jax.ShapeDtypeStruct(tiles.shape, t...]
    pallas_call x9, Pallas kernels: 11.8 us -> 10.2 us  [tile_part(): pl.pallas_call(functools.partial(part_kernel, spec), out_shape=out_shape,...]
  transfers between devices with their start and end apart: 27 -> 25, of which waited for: 13 -> 15; matrix products, arithmetic and copies ran while one was open for 7% -> 7% of each run, Pallas kernels for 13% -> 15%
where the time goes in v1:
time: 80.7 us; the launch traced here: 80.1 us
  waiting for transfers between devices  28.8 us (36%)
  starting transfers between devices  27.6 us (34%)
  Pallas kernels  13 us (16%)
  other arithmetic  4.85 us (6%)
  matrix products  4 us (5%)
  between operations  1.66 us (2%)
    ppermute x25, waiting for transfers between devices, move(): return lax.ppermute(value, ('row', 'col'), pairs)  28.8 us
    ppermute x25, starting transfers between devices, move(): return lax.ppermute(value, ('row', 'col'), pairs)  27.6 us
    pallas_call x9, Pallas kernels, tile_part(): pl.pallas_call(functools.partial(part_kernel, spec), out_shape=out_shape,...  10.2 us
    pallas_call x1, Pallas kernels, load_tiles(): pl.pallas_call(load_kernel, out_shape=jax.ShapeDtypeStruct(tiles.shape, t...  2.87 us
    dot_general x2, matrix products, restore(): lax.dot_general(onehot, values, (((0,), (0,)), ((), ())), preferred_eleme...  1.99 us
  transfers between devices with their start and end apart: 25, of which 15 were waited for; matrix products, arithmetic and copies ran while one was open for 7% of the time, Pallas kernels for 15%

profile of v1, /device:TPU:0, one launch (start us, length us, event | category | flops | bytes accessed | tf_op | source)
XLA Modules:
  0.0 80.1 jit_solution(10661278603624573313)
XLA Ops:
  0.6 0.7 and_select_fusion.12
  1.4 1.1 %convolution_convert_fusion.4.refs_0_ = bf16[256,256]{1,0:T(8,128)(2,1)S(1)} fusion(bf16[256,256]{1,0:T(8,128)(2,1)} %param.7, s32[256]{0:T(256)S(1)} %and_select_fusion.12), kind=kOutput, calls=%fused_computation.9 | convolution fusion | flops 33685504 | bytes 263168 | tf_op jit(solution)/shard_map/dot_general | solution.py:36
  2.5 0.5 collective-permute-start.1
  3.0 2.6 %collective-permute-start = (bf16[256,256]{1,0:T(8,128)(2,1)S(1)}, bf16[256,256]{1,0:T(8,128)(2,1)S(1)}, u32[]{:S(2)}, u32[]{:S(2)}) collective-permute-start(bf16[256,256]{1,0:T(8,128)(2,1)S(1)} %convolution_convert_fusion.4.refs_0_), channel_id=1, source_target_pairs={{0,16},{1,17},{2,18},{3,19},{4,20},{5,21},{6,22},{7,23},{8,24},{9,... | collective-permute-start | bytes 393224 | tf_op jit(solution)/shard_map/ppermute | solution.py:227
  6.3 0.7 fusion.43
  7.0 0.7 add_select_fusion.1
  9.0 0.7 collective-permute-done.refs_1_
  9.8 2.9 %shard_map.94.tiles_ref = bf16[192,128,128]{2,1,0:T(8,128)(2,1)S(1)} custom-call(bf16[192,128,128]{2,1,0:T(8,128)(2,1)} %bitcast.11), custom_call_target="tpu_custom_call" | custom-call | bytes 6291456 | tf_op jit(solution)/shard_map/pallas_call | solution.py:82
  12.8 1.2 %shard_map.95 = (bf16[256,256]{1,0:T(8,128)(2,1)S(1)}, bf16[256,256]{1,0:T(8,128)(2,1)S(1)}) custom-call(s32[342]{0:T(512)S(1)} %pad_add_fusion.table_ref, bf16[192,128,128]{2,1,0:T(8,128)(2,1)S(1)} %shard_map.94.tiles_ref, bf16[256,256]{1,0:T(8,128)(2,1)S(1)} %convolution_convert_fusion.4.refs_0_, bf16[256,256]{1,0:T(8,128)(2,1)S(1)} %collective-permute-done.refs_1_, ...), custom_call_target="tpu_custom_call" | custom-call | flops 402653184 | bytes 1572864 | tf_op jit(solution)/shard_map/pallas_call | solution.py:159
  14.0 1.8 %collective-permute-start.3 = (bf16[256,256]{1,0:T(8,128)(2,1)S(1)}, bf16[256,256]{1,0:T(8,128)(2,1)S(1)}, u32[]{:S(2)}, u32[]{:S(2)}) collective-permute-start(bf16[256,256]{1,0:T(8,128)(2,1)S(1)} %get-tuple-element.20), channel_id=1, source_target_pairs={{0,1},{1,3},{3,5},{5,7},{7,6},{6,4},{4,2},{2,0},{10,12},{12,14},{1... | collective-permute-start | bytes 393224 | tf_op jit(solution)/shard_map/ppermute | solution.py:227
  15.9 0.3 collective-permute-start.7
  16.2 0.9 %shard_map.96 = (bf16[256,256]{1,0:T(8,128)(2,1)S(1)}, bf16[256,256]{1,0:T(8,128)(2,1)S(1)}) custom-call(s32[342]{0:T(512)S(1)} %pad_add_fusion.table_ref, bf16[192,128,128]{2,1,0:T(8,128)(2,1)S(1)} %shard_map.94.tiles_ref, bf16[256,256]{1,0:T(8,128)(2,1)S(1)} %convolution_convert_fusion.4.refs_0_, bf16[256,256]{1,0:T(8,128)(2,1)S(1)} %collective-permute-done.refs_1_, ...), custom_call_target="tpu_custom_call" | custom-call | flops 402653184 | bytes 1572864 | tf_op jit(solution)/shard_map/pallas_call | solution.py:159
  17.1 2.6 %collective-permute-done.3 = bf16[256,256]{1,0:T(8,128)(2,1)S(1)} collective-permute-done((bf16[256,256]{1,0:T(8,128)(2,1)S(1)}, bf16[256,256]{1,0:T(8,128)(2,1)S(1)}, u32[]{:S(2)}, u32[]{:S(2)}) %collective-permute-start.3) | collective-permute-done | bytes 131104 | tf_op jit(solution)/shard_map/ppermute | solution.py:227
  19.7 2.5 %collective-permute-start.4 = (bf16[256,256]{1,0:T(8,128)(2,1)S(1)}, bf16[256,256]{1,0:T(8,128)(2,1)S(1)}, u32[]{:S(2)}, u32[]{:S(2)}) collective-permute-start(bf16[256,256]{1,0:T(8,128)(2,1)S(1)} %add_convert_fusion.6), channel_id=1, source_target_pairs={{0,1},{1,3},{3,5},{5,7},{7,6},{6,4},{4,2},{2,0},{10,12},{12,14},{1... | collective-permute-start | bytes 393224 | tf_op jit(solution)/shard_map/ppermute | solution.py:227
  22.4 1.2 %shard_map.98 = (bf16[256,256]{1,0:T(8,128)(2,1)S(1)}, bf16[256,256]{1,0:T(8,128)(2,1)S(1)}) custom-call(s32[342]{0:T(512)S(1)} %pad_add_fusion.table_ref, bf16[192,128,128]{2,1,0:T(8,128)(2,1)S(1)} %shard_map.94.tiles_ref, bf16[256,256]{1,0:T(8,128)(2,1)S(1)} %convolution_convert_fusion.4.refs_0_, bf16[256,256]{1,0:T(8,128)(2,1)S(1)} %collective-permute-done.refs_1_, ...), custom_call_target="tpu_custom_call" | custom-call | flops 402653184 | bytes 1572864 | tf_op jit(solution)/shard_map/pallas_call | solution.py:159
  23.6 2.6 %collective-permute-done.4 = bf16[256,256]{1,0:T(8,128)(2,1)S(1)} collective-permute-done((bf16[256,256]{1,0:T(8,128)(2,1)S(1)}, bf16[256,256]{1,0:T(8,128)(2,1)S(1)}, u32[]{:S(2)}, u32[]{:S(2)}) %collective-permute-start.4) | collective-permute-done | bytes 131104 | tf_op jit(solution)/shard_map/ppermute | solution.py:227
  26.1 1.7 %collective-permute-start.5 = (bf16[256,256]{1,0:T(8,128)(2,1)S(1)}, bf16[256,256]{1,0:T(8,128)(2,1)S(1)}, u32[]{:S(2)}, u32[]{:S(2)}) collective-permute-start(bf16[256,256]{1,0:T(8,128)(2,1)S(1)} %add_convert_fusion.5), channel_id=1, source_target_pairs={{0,1},{1,3},{3,5},{5,7},{7,6},{6,4},{4,2},{2,0},{10,12},{12,14},{1... | collective-permute-start | bytes 393224 | tf_op jit(solution)/shard_map/ppermute | solution.py:227
  27.9 0.7 collective-permute-done.8
  28.7 0.9 %shard_map.97 = (bf16[256,256]{1,0:T(8,128)(2,1)S(1)}, bf16[256,256]{1,0:T(8,128)(2,1)S(1)}) custom-call(s32[342]{0:T(512)S(1)} %pad_add_fusion.table_ref, bf16[192,128,128]{2,1,0:T(8,128)(2,1)S(1)} %shard_map.94.tiles_ref, bf16[256,256]{1,0:T(8,128)(2,1)S(1)} %convolution_convert_fusion.4.refs_0_, bf16[256,256]{1,0:T(8,128)(2,1)S(1)} %collective-permute-done.refs_1_, ...), custom_call_target="tpu_custom_call" | custom-call | flops 402653184 | bytes 1572864 | tf_op jit(solution)/shard_map/pallas_call | solution.py:159
  29.6 2.1 %collective-permute-done.5 = bf16[256,256]{1,0:T(8,128)(2,1)S(1)} collective-permute-done((bf16[256,256]{1,0:T(8,128)(2,1)S(1)}, bf16[256,256]{1,0:T(8,128)(2,1)S(1)}, u32[]{:S(2)}, u32[]{:S(2)}) %collective-permute-start.5) | collective-permute-done | bytes 131104 | tf_op jit(solution)/shard_map/ppermute | solution.py:227
  31.8 1.1 %collective-permute-start.6 = (bf16[256,256]{1,0:T(8,128)(2,1)S(1)}, bf16[256,256]{1,0:T(8,128)(2,1)S(1)}, u32[]{:S(2)}, u32[]{:S(2)}) collective-permute-start(bf16[256,256]{1,0:T(8,128)(2,1)S(1)} %add_convert_fusion.4), channel_id=1, source_target_pairs={{0,1},{1,3},{3,5},{5,7},{7,6},{6,4},{4,2},{2,0},{10,12},{12,14},{1... | collective-permute-start | bytes 393224 | tf_op jit(solution)/shard_map/ppermute | solution.py:227
  32.9 1.5 %collective-permute-done.9 = bf16[256,256]{1,0:T(8,128)(2,1)S(1)} collective-permute-done((bf16[256,256]{1,0:T(8,128)(2,1)S(1)}, bf16[256,256]{1,0:T(8,128)(2,1)S(1)}, u32[]{:S(2)}, u32[]{:S(2)}) %collective-permute-start.9) | collective-permute-done | bytes 131104 | tf_op jit(solution)/shard_map/ppermute | solution.py:227
  34.4 2.4 %collective-permute-done.6 = bf16[256,256]{1,0:T(8,128)(2,1)S(1)} collective-permute-done((bf16[256,256]{1,0:T(8,128)(2,1)S(1)}, bf16[256,256]{1,0:T(8,128)(2,1)S(1)}, u32[]{:S(2)}, u32[]{:S(2)}) %collective-permute-start.6) | collective-permute-done | bytes 131104 | tf_op jit(solution)/shard_map/ppermute | solution.py:227
  37.8 2.0 %collective-permute-start.11 = (bf16[256,256]{1,0:T(8,128)(2,1)S(1)}, bf16[256,256]{1,0:T(8,128)(2,1)S(1)}, u32[]{:S(2)}, u32[]{:S(2)}) collective-permute-start(bf16[256,256]{1,0:T(8,128)(2,1)S(1)} %convolution_convert_fusion.1.refs_0_), channel_id=1, source_target_pairs={{0,2},{1,0},{3,1},{5,3},{7,5},{6,7},{4,6},{2,4},{10,8},{12,10},{14... | collective-permute-start | bytes 393224 | tf_op jit(solution)/shard_map/ppermute | solution.py:227
  40.1 3.7 %collective-permute-done.11.refs_1_ = bf16[256,256]{1,0:T(8,128)(2,1)S(1)} collective-permute-done((bf16[256,256]{1,0:T(8,128)(2,1)S(1)}, bf16[256,256]{1,0:T(8,128)(2,1)S(1)}, u32[]{:S(2)}, u32[]{:S(2)}) %collective-permute-start.11) | collective-permute-done | bytes 131104 | tf_op jit(solution)/shard_map/ppermute | solution.py:227
  43.9 0.9 %collective-permute-start.12 = (bf16[128,256]{1,0:T(8,128)(2,1)S(1)}, bf16[128,256]{1,0:T(8,128)(2,1)S(1)}, u32[]{:S(2)}, u32[]{:S(2)}) collective-permute-start(bf16[128,256]{1,0:T(8,128)(2,1)S(1)} %slice_select_fusion), channel_id=1, source_target_pairs={{0,16},{1,17},{2,18},{3,19},{4,20},{5,21},{6,22},{7,23},{8,24},{9,... | collective-permute-start | bytes 196616 | tf_op jit(solution)/shard_map/ppermute | solution.py:227
  44.8 1.6 %collective-permute-start.13 = (bf16[256,256]{1,0:T(8,128)(2,1)S(1)}, bf16[256,256]{1,0:T(8,128)(2,1)S(1)}, u32[]{:S(2)}, u32[]{:S(2)}) collective-permute-start(bf16[256,256]{1,0:T(8,128)(2,1)S(1)} %collective-permute-done.11.refs_1_), channel_id=1, source_target_pairs={{0,2},{1,0},{3,1},{5,3},{7,5},{6,7},{4,6},{2,4},{10,8},{12,10},{14... | collective-permute-start | bytes 393224 | tf_op jit(solution)/shard_map/ppermute | solution.py:227
  46.4 0.4 collective-permute-start.18
  46.8 1.0 %convolution_convert_fusion.3 = bf16[256,256]{1,0:T(8,128)(2,1)} fusion(f32[256,256]{1,0:T(8,128)S(1)} %fusion.45, s32[256]{0:T(256)S(1)} %and_select_fusion.12), kind=kOutput, calls=%fused_computation.8 | convolution fusion | flops 33947648 | bytes 394240 | tf_op jit(solution)/shard_map/dot_general | solution.py:40
  47.8 0.4 collective-permute-done.12
  48.2 1.6 %collective-permute-done.13.refs_1_ = bf16[256,256]{1,0:T(8,128)(2,1)S(1)} collective-permute-done((bf16[256,256]{1,0:T(8,128)(2,1)S(1)}, bf16[256,256]{1,0:T(8,128)(2,1)S(1)}, u32[]{:S(2)}, u32[]{:S(2)}) %collective-permute-start.13) | collective-permute-done | bytes 131104 | tf_op jit(solution)/shard_map/ppermute | solution.py:227
  49.8 1.6 %collective-permute-start.15 = (bf16[256,256]{1,0:T(8,128)(2,1)S(1)}, bf16[256,256]{1,0:T(8,128)(2,1)S(1)}, u32[]{:S(2)}, u32[]{:S(2)}) collective-permute-start(bf16[256,256]{1,0:T(8,128)(2,1)S(1)} %collective-permute-done.13.refs_1_), channel_id=1, source_target_pairs={{0,2},{1,0},{3,1},{5,3},{7,5},{6,7},{4,6},{2,4},{10,8},{12,10},{14... | collective-permute-start | bytes 393224 | tf_op jit(solution)/shard_map/ppermute | solution.py:227
  51.4 1.2 %collective-permute-done.18.refs_0_ = bf16[256,256]{1,0:T(8,128)(2,1)S(1)} collective-permute-done((bf16[256,256]{1,0:T(8,128)(2,1)S(1)}, bf16[256,256]{1,0:T(8,128)(2,1)S(1)}, u32[]{:S(2)}, u32[]{:S(2)}) %collective-permute-start.18) | collective-permute-done | bytes 131104 | tf_op jit(solution)/shard_map/ppermute | solution.py:227
  52.6 1.1 %collective-permute-start.14 = (bf16[128,256]{1,0:T(8,128)(2,1)S(1)}, bf16[128,256]{1,0:T(8,128)(2,1)S(1)}, u32[]{:S(2)}, u32[]{:S(2)}) collective-permute-start(bf16[128,256]{1,0:T(8,128)(2,1)S(1)} %add_convert_fusion.10), channel_id=1, source_target_pairs={{0,1},{1,0},{2,3},{3,2},{4,5},{5,4},{6,7},{7,6},{8,9},{9,8},{10,11... | collective-permute-start | bytes 196616 | tf_op jit(solution)/shard_map/ppermute | solution.py:227
  53.6 0.7 shard_map.99.refs_2_
  54.4 1.5 %shard_map.100.refs_2_ = f32[1024,256]{1,0:T(8,128)S(1)} custom-call(s32[486]{0:T(512)S(1)} %pad_add_fusion.1.table_ref, bf16[192,128,128]{2,1,0:T(8,128)(2,1)S(1)} %shard_map.94.tiles_ref, bf16[256,256]{1,0:T(8,128)(2,1)S(1)} %collective-permute-done.17.refs_0_, bf16[256,256]{1,0:T(8,128)(2,1)S(1)} %collective-permute-done.11.refs_1_, ...), custom_call_target="tpu_custom_call" | custom-call | flops 318767104 | bytes 1245184 | tf_op jit(solution)/shard_map/pallas_call | solution.py:159
  55.9 1.5 %shard_map.101.refs_2_ = f32[1024,256]{1,0:T(8,128)S(1)} custom-call(s32[486]{0:T(512)S(1)} %pad_add_fusion.1.table_ref, bf16[192,128,128]{2,1,0:T(8,128)(2,1)S(1)} %shard_map.94.tiles_ref, bf16[256,256]{1,0:T(8,128)(2,1)S(1)} %collective-permute-done.18.refs_0_, bf16[256,256]{1,0:T(8,128)(2,1)S(1)} %collective-permute-done.13.refs_1_, ...), custom_call_target="tpu_custom_call" | custom-call | flops 318767104 | bytes 1245184 | tf_op jit(solution)/shard_map/pallas_call | solution.py:159
  57.5 0.8 collective-permute-start.20
  58.3 1.3 %collective-permute-start.16 = (bf16[128,256]{1,0:T(8,128)(2,1)S(1)}, bf16[128,256]{1,0:T(8,128)(2,1)S(1)}, u32[]{:S(2)}, u32[]{:S(2)}) collective-permute-start(bf16[128,256]{1,0:T(8,128)(2,1)S(1)} %add_convert_fusion.9), channel_id=1, source_target_pairs={{0,2},{1,3},{2,0},{3,1},{4,6},{5,7},{6,4},{7,5},{8,10},{9,11},{10,... | collective-permute-start | bytes 196616 | tf_op jit(solution)/shard_map/ppermute | solution.py:227
  59.7 1.3 %shard_map.102.refs_1_ = f32[1024,256]{1,0:T(8,128)S(1)} custom-call(s32[486]{0:T(512)S(1)} %pad_add_fusion.1.table_ref, bf16[192,128,128]{2,1,0:T(8,128)(2,1)S(1)} %shard_map.94.tiles_ref, bf16[256,256]{1,0:T(8,128)(2,1)S(1)} %collective-permute-done.19.refs_0_, bf16[256,256]{1,0:T(8,128)(2,1)S(1)} %collective-permute-done.15.refs_1_, ...), custom_call_target="tpu_custom_call" | custom-call | flops 318767104 | bytes 1245184 | tf_op jit(solution)/shard_map/pallas_call | solution.py:159
  60.9 1.6 %collective-permute-done.20.refs_0_ = bf16[256,256]{1,0:T(8,128)(2,1)S(1)} collective-permute-done((bf16[256,256]{1,0:T(8,128)(2,1)S(1)}, bf16[256,256]{1,0:T(8,128)(2,1)S(1)}, u32[]{:S(2)}, u32[]{:S(2)}) %collective-permute-start.20) | collective-permute-done | bytes 131104 | tf_op jit(solution)/shard_map/ppermute | solution.py:227
  62.5 1.0 %shard_map.103 = (bf16[512,256]{1,0:T(8,128)(2,1)S(1)}, bf16[512,256]{1,0:T(8,128)(2,1)S(1)}) custom-call(s32[486]{0:T(512)S(1)} %pad_add_fusion.1.table_ref, bf16[192,128,128]{2,1,0:T(8,128)(2,1)S(1)} %shard_map.94.tiles_ref, bf16[256,256]{1,0:T(8,128)(2,1)S(1)} %collective-permute-done.20.refs_0_, f32[1024,256]{1,0:T(8,128)S(1)} %shard_map.102.refs_1_), custom_call_target="tpu_custom_call" | custom-call | flops 318767104 | bytes 1245184 | tf_op jit(solution)/shard_map/pallas_call | solution.py:159
  63.6 6.8 %collective-permute-start.21 = (bf16[128,256]{1,0:T(8,128)(2,1)S(1)}, bf16[128,256]{1,0:T(8,128)(2,1)S(1)}, u32[]{:S(2)}, u32[]{:S(2)}) collective-permute-start(bf16[128,256]{1,0:T(8,128)(2,1)S(1)} %add_convert_fusion.8), channel_id=1, source_target_pairs={{0,4},{1,5},{2,6},{3,7},{4,0},{5,1},{6,2},{7,3},{8,12},{9,13},{10,... | collective-permute-start | bytes 196616 | tf_op jit(solution)/shard_map/ppermute | solution.py:227
  70.5 2.7 %collective-permute-done.21 = bf16[128,256]{1,0:T(8,128)(2,1)S(1)} collective-permute-done((bf16[128,256]{1,0:T(8,128)(2,1)S(1)}, bf16[128,256]{1,0:T(8,128)(2,1)S(1)}, u32[]{:S(2)}, u32[]{:S(2)}) %collective-permute-start.21) | collective-permute-done | bytes 65568 | tf_op jit(solution)/shard_map/ppermute | solution.py:227
  73.3 1.2 %collective-permute-done.23 = bf16[128,256]{1,0:T(8,128)(2,1)S(1)} collective-permute-done((bf16[128,256]{1,0:T(8,128)(2,1)S(1)}, bf16[128,256]{1,0:T(8,128)(2,1)S(1)}, u32[]{:S(2)}, u32[]{:S(2)}) %collective-permute-start.23) | collective-permute-done | bytes 65568 | tf_op jit(solution)/shard_map/ppermute | solution.py:227
  74.5 0.7 fusion.10
  75.2 3.9 %collective-permute-done.24 = bf16[256,256]{1,0:T(8,128)(2,1)S(1)} collective-permute-done((bf16[256,256]{1,0:T(8,128)(2,1)S(1)}, bf16[256,256]{1,0:T(8,128)(2,1)S(1)}, u32[]{:S(2)}, u32[]{:S(2)}) %collective-permute-start.24) | collective-permute-done | bytes 131104 | tf_op jit(solution)/shard_map/ppermute | solution.py:227
  79.2 1.0 %convolution_convert_fusion = bf16[256,256]{1,0:T(8,128)(2,1)} fusion(f32[512,256]{1,0:T(8,128)S(1)} %convert_add_fusion, bf16[256,256]{1,0:T(8,128)(2,1)S(1)} %collective-permute-done.24, s32[256]{0:T(256)S(1)} %and_select_fusion.12), kind=kOutput, calls=%fused_computation.2 | convolution fusion | flops 33882112 | bytes 525312 | tf_op jit(solution)/shard_map/dot_general | solution.py:40
  (62 shorter events, 3.6 us)
Async XLA Ops:
  0.6 36.2 %copy-start = (bf16[256,256]{1,0:T(8,128)(2,1)S(1)}, bf16[256,256]{1,0:T(8,128)(2,1)}, u32[]{:S(2)}) copy-start(bf16[256,256]{1,0:T(8,128)(2,1)} %param.12) | copy-start | bytes 393220
  2.5 10.3 %collective-permute-start.1 = (bf16[256,256]{1,0:T(8,128)(2,1)S(1)}, bf16[256,256]{1,0:T(8,128)(2,1)S(1)}, u32[]{:S(2)}, u32[]{:S(2)}) collective-permute-start(bf16[256,256]{1,0:T(8,128)(2,1)S(1)} %convolution_convert_fusion.4.refs_0_), channel_id=1, source_target_pairs={{0,8},{1,9},{2,10},{3,11},{4,12},{5,13},{6,14},{7,15},{8,0},{9,1},... | collective-permute-start | bytes 393224 | tf_op jit(solution)/shard_map/ppermute | solution.py:227
  3.0 6.7 %collective-permute-start = (bf16[256,256]{1,0:T(8,128)(2,1)S(1)}, bf16[256,256]{1,0:T(8,128)(2,1)S(1)}, u32[]{:S(2)}, u32[]{:S(2)}) collective-permute-start(bf16[256,256]{1,0:T(8,128)(2,1)S(1)} %convolution_convert_fusion.4.refs_0_), channel_id=1, source_target_pairs={{0,16},{1,17},{2,18},{3,19},{4,20},{5,21},{6,22},{7,23},{8,24},{9,... | collective-permute-start | bytes 393224 | tf_op jit(solution)/shard_map/ppermute | solution.py:227
  9.7 3.1 %collective-permute-start.2 = (bf16[256,256]{1,0:T(8,128)(2,1)S(1)}, bf16[256,256]{1,0:T(8,128)(2,1)S(1)}, u32[]{:S(2)}, u32[]{:S(2)}) collective-permute-start(bf16[256,256]{1,0:T(8,128)(2,1)S(1)} %collective-permute-done.refs_1_), channel_id=1, source_target_pairs={{0,8},{1,9},{2,10},{3,11},{4,12},{5,13},{6,14},{7,15},{8,0},{9,1},... | collective-permute-start | bytes 393224 | tf_op jit(solution)/shard_map/ppermute | solution.py:227
  14.0 5.7 %collective-permute-start.3 = (bf16[256,256]{1,0:T(8,128)(2,1)S(1)}, bf16[256,256]{1,0:T(8,128)(2,1)S(1)}, u32[]{:S(2)}, u32[]{:S(2)}) collective-permute-start(bf16[256,256]{1,0:T(8,128)(2,1)S(1)} %get-tuple-element.20), channel_id=1, source_target_pairs={{0,1},{1,3},{3,5},{5,7},{7,6},{6,4},{4,2},{2,0},{10,12},{12,14},{1... | collective-permute-start | bytes 393224 | tf_op jit(solution)/shard_map/ppermute | solution.py:227
  15.9 6.3 %collective-permute-start.7 = (bf16[256,256]{1,0:T(8,128)(2,1)S(1)}, bf16[256,256]{1,0:T(8,128)(2,1)S(1)}, u32[]{:S(2)}, u32[]{:S(2)}) collective-permute-start(bf16[256,256]{1,0:T(8,128)(2,1)S(1)} %get-tuple-element.27), channel_id=1, source_target_pairs={{0,2},{1,0},{3,1},{5,3},{7,5},{6,7},{4,6},{2,4},{10,8},{12,10},{14... | collective-permute-start | bytes 393224 | tf_op jit(solution)/shard_map/ppermute | solution.py:227
  19.7 6.4 %collective-permute-start.4 = (bf16[256,256]{1,0:T(8,128)(2,1)S(1)}, bf16[256,256]{1,0:T(8,128)(2,1)S(1)}, u32[]{:S(2)}, u32[]{:S(2)}) collective-permute-start(bf16[256,256]{1,0:T(8,128)(2,1)S(1)} %add_convert_fusion.6), channel_id=1, source_target_pairs={{0,1},{1,3},{3,5},{5,7},{7,6},{6,4},{4,2},{2,0},{10,12},{12,14},{1... | collective-permute-start | bytes 393224 | tf_op jit(solution)/shard_map/ppermute | solution.py:227
  22.3 14.7 %copy-start.1 = (bf16[256,256]{1,0:T(8,128)(2,1)S(1)}, bf16[256,256]{1,0:T(8,128)(2,1)}, u32[]{:S(2)}) copy-start(bf16[256,256]{1,0:T(8,128)(2,1)} %param.13) | copy-start | bytes 393220
  22.3 6.3 %collective-permute-start.8 = (bf16[256,256]{1,0:T(8,128)(2,1)S(1)}, bf16[256,256]{1,0:T(8,128)(2,1)S(1)}, u32[]{:S(2)}, u32[]{:S(2)}) collective-permute-start(bf16[256,256]{1,0:T(8,128)(2,1)S(1)} %add_convert_fusion.3), channel_id=1, source_target_pairs={{0,2},{1,0},{3,1},{5,3},{7,5},{6,7},{4,6},{2,4},{10,8},{12,10},{14... | collective-permute-start | bytes 393224 | tf_op jit(solution)/shard_map/ppermute | solution.py:227
  26.1 5.6 %collective-permute-start.5 = (bf16[256,256]{1,0:T(8,128)(2,1)S(1)}, bf16[256,256]{1,0:T(8,128)(2,1)S(1)}, u32[]{:S(2)}, u32[]{:S(2)}) collective-permute-start(bf16[256,256]{1,0:T(8,128)(2,1)S(1)} %add_convert_fusion.5), channel_id=1, source_target_pairs={{0,1},{1,3},{3,5},{5,7},{7,6},{6,4},{4,2},{2,0},{10,12},{12,14},{1... | collective-permute-start | bytes 393224 | tf_op jit(solution)/shard_map/ppermute | solution.py:227
  28.6 5.7 %collective-permute-start.9 = (bf16[256,256]{1,0:T(8,128)(2,1)S(1)}, bf16[256,256]{1,0:T(8,128)(2,1)S(1)}, u32[]{:S(2)}, u32[]{:S(2)}) collective-permute-start(bf16[256,256]{1,0:T(8,128)(2,1)S(1)} %add_convert_fusion.2), channel_id=1, source_target_pairs={{0,2},{1,0},{3,1},{5,3},{7,5},{6,7},{4,6},{2,4},{10,8},{12,10},{14... | collective-permute-start | bytes 393224 | tf_op jit(solution)/shard_map/ppermute | solution.py:227
  31.8 5.0 %collective-permute-start.6 = (bf16[256,256]{1,0:T(8,128)(2,1)S(1)}, bf16[256,256]{1,0:T(8,128)(2,1)S(1)}, u32[]{:S(2)}, u32[]{:S(2)}) collective-permute-start(bf16[256,256]{1,0:T(8,128)(2,1)S(1)} %add_convert_fusion.4), channel_id=1, source_target_pairs={{0,1},{1,3},{3,5},{5,7},{7,6},{6,4},{4,2},{2,0},{10,12},{12,14},{1... | collective-permute-start | bytes 393224 | tf_op jit(solution)/shard_map/ppermute | solution.py:227
  37.8 2.3 %collective-permute-start.10 = (bf16[256,256]{1,0:T(8,128)(2,1)S(1)}, bf16[256,256]{1,0:T(8,128)(2,1)S(1)}, u32[]{:S(2)}, u32[]{:S(2)}) collective-permute-start(bf16[256,256]{1,0:T(8,128)(2,1)S(1)} %fusion), channel_id=1, source_target_pairs={{0,8},{1,9},{2,10},{3,11},{4,12},{5,13},{6,14},{7,15},{8,0},{9,1},... | collective-permute-start | bytes 393224 | tf_op jit(solution)/shard_map/ppermute | solution.py:227
  37.8 6.0 %collective-permute-start.11 = (bf16[256,256]{1,0:T(8,128)(2,1)S(1)}, bf16[256,256]{1,0:T(8,128)(2,1)S(1)}, u32[]{:S(2)}, u32[]{:S(2)}) collective-permute-start(bf16[256,256]{1,0:T(8,128)(2,1)S(1)} %convolution_convert_fusion.1.refs_0_), channel_id=1, source_target_pairs={{0,2},{1,0},{3,1},{5,3},{7,5},{6,7},{4,6},{2,4},{10,8},{12,10},{14... | collective-permute-start | bytes 393224 | tf_op jit(solution)/shard_map/ppermute | solution.py:227
  40.0 6.4 %collective-permute-start.17 = (bf16[256,256]{1,0:T(8,128)(2,1)S(1)}, bf16[256,256]{1,0:T(8,128)(2,1)S(1)}, u32[]{:S(2)}, u32[]{:S(2)}) collective-permute-start(bf16[256,256]{1,0:T(8,128)(2,1)S(1)} %convolution_convert_fusion.1.refs_0_), channel_id=1, source_target_pairs={{0,1},{1,3},{3,5},{5,7},{7,6},{6,4},{4,2},{2,0},{10,12},{12,14},{1... | collective-permute-start | bytes 393224 | tf_op jit(solution)/shard_map/ppermute | solution.py:227
  43.9 4.3 %collective-permute-start.12 = (bf16[128,256]{1,0:T(8,128)(2,1)S(1)}, bf16[128,256]{1,0:T(8,128)(2,1)S(1)}, u32[]{:S(2)}, u32[]{:S(2)}) collective-permute-start(bf16[128,256]{1,0:T(8,128)(2,1)S(1)} %slice_select_fusion), channel_id=1, source_target_pairs={{0,16},{1,17},{2,18},{3,19},{4,20},{5,21},{6,22},{7,23},{8,24},{9,... | collective-permute-start | bytes 196616 | tf_op jit(solution)/shard_map/ppermute | solution.py:227
  44.8 5.0 %collective-permute-start.13 = (bf16[256,256]{1,0:T(8,128)(2,1)S(1)}, bf16[256,256]{1,0:T(8,128)(2,1)S(1)}, u32[]{:S(2)}, u32[]{:S(2)}) collective-permute-start(bf16[256,256]{1,0:T(8,128)(2,1)S(1)} %collective-permute-done.11.refs_1_), channel_id=1, source_target_pairs={{0,2},{1,0},{3,1},{5,3},{7,5},{6,7},{4,6},{2,4},{10,8},{12,10},{14... | collective-permute-start | bytes 393224 | tf_op jit(solution)/shard_map/ppermute | solution.py:227
  46.4 6.1 %collective-permute-start.18 = (bf16[256,256]{1,0:T(8,128)(2,1)S(1)}, bf16[256,256]{1,0:T(8,128)(2,1)S(1)}, u32[]{:S(2)}, u32[]{:S(2)}) collective-permute-start(bf16[256,256]{1,0:T(8,128)(2,1)S(1)} %collective-permute-done.17.refs_0_), channel_id=1, source_target_pairs={{0,1},{1,3},{3,5},{5,7},{7,6},{6,4},{4,2},{2,0},{10,12},{12,14},{1... | collective-permute-start | bytes 393224 | tf_op jit(solution)/shard_map/ppermute | solution.py:227
  49.8 7.7 %collective-permute-start.15 = (bf16[256,256]{1,0:T(8,128)(2,1)S(1)}, bf16[256,256]{1,0:T(8,128)(2,1)S(1)}, u32[]{:S(2)}, u32[]{:S(2)}) collective-permute-start(bf16[256,256]{1,0:T(8,128)(2,1)S(1)} %collective-permute-done.13.refs_1_), channel_id=1, source_target_pairs={{0,2},{1,0},{3,1},{5,3},{7,5},{6,7},{4,6},{2,4},{10,8},{12,10},{14... | collective-permute-start | bytes 393224 | tf_op jit(solution)/shard_map/ppermute | solution.py:227
  52.5 5.0 %collective-permute-start.19 = (bf16[256,256]{1,0:T(8,128)(2,1)S(1)}, bf16[256,256]{1,0:T(8,128)(2,1)S(1)}, u32[]{:S(2)}, u32[]{:S(2)}) collective-permute-start(bf16[256,256]{1,0:T(8,128)(2,1)S(1)} %collective-permute-done.18.refs_0_), channel_id=1, source_target_pairs={{0,1},{1,3},{3,5},{5,7},{7,6},{6,4},{4,2},{2,0},{10,12},{12,14},{1... | collective-permute-start | bytes 393224 | tf_op jit(solution)/shard_map/ppermute | solution.py:227
  52.6 4.9 %collective-permute-start.14 = (bf16[128,256]{1,0:T(8,128)(2,1)S(1)}, bf16[128,256]{1,0:T(8,128)(2,1)S(1)}, u32[]{:S(2)}, u32[]{:S(2)}) collective-permute-start(bf16[128,256]{1,0:T(8,128)(2,1)S(1)} %add_convert_fusion.10), channel_id=1, source_target_pairs={{0,1},{1,0},{2,3},{3,2},{4,5},{5,4},{6,7},{7,6},{8,9},{9,8},{10,11... | collective-permute-start | bytes 196616 | tf_op jit(solution)/shard_map/ppermute | solution.py:227
  57.5 5.0 %collective-permute-start.20 = (bf16[256,256]{1,0:T(8,128)(2,1)S(1)}, bf16[256,256]{1,0:T(8,128)(2,1)S(1)}, u32[]{:S(2)}, u32[]{:S(2)}) collective-permute-start(bf16[256,256]{1,0:T(8,128)(2,1)S(1)} %collective-permute-done.19.refs_0_), channel_id=1, source_target_pairs={{0,1},{1,3},{3,5},{5,7},{7,6},{6,4},{4,2},{2,0},{10,12},{12,14},{1... | collective-permute-start | bytes 393224 | tf_op jit(solution)/shard_map/ppermute | solution.py:227
  58.3 5.3 %collective-permute-start.16 = (bf16[128,256]{1,0:T(8,128)(2,1)S(1)}, bf16[128,256]{1,0:T(8,128)(2,1)S(1)}, u32[]{:S(2)}, u32[]{:S(2)}) collective-permute-start(bf16[128,256]{1,0:T(8,128)(2,1)S(1)} %add_convert_fusion.9), channel_id=1, source_target_pairs={{0,2},{1,3},{2,0},{3,1},{4,6},{5,7},{6,4},{7,5},{8,10},{9,11},{10,... | collective-permute-start | bytes 196616 | tf_op jit(solution)/shard_map/ppermute | solution.py:227
  63.5 6.9 %collective-permute-start.22 = (bf16[512,256]{1,0:T(8,128)(2,1)S(1)}, bf16[512,256]{1,0:T(8,128)(2,1)S(1)}, u32[]{:S(2)}, u32[]{:S(2)}) collective-permute-start(bf16[512,256]{1,0:T(8,128)(2,1)S(1)} %get-tuple-element.35), channel_id=1, source_target_pairs={{0,8},{1,9},{2,10},{3,11},{4,12},{5,13},{6,14},{7,15},{8,0},{9,1},... | collective-permute-start | bytes 786440 | tf_op jit(solution)/shard_map/ppermute | solution.py:227
  63.6 9.5 %collective-permute-start.21 = (bf16[128,256]{1,0:T(8,128)(2,1)S(1)}, bf16[128,256]{1,0:T(8,128)(2,1)S(1)}, u32[]{:S(2)}, u32[]{:S(2)}) collective-permute-start(bf16[128,256]{1,0:T(8,128)(2,1)S(1)} %add_convert_fusion.8), channel_id=1, source_target_pairs={{0,4},{1,5},{2,6},{3,7},{4,0},{5,1},{6,2},{7,3},{8,12},{9,13},{10,... | collective-permute-start | bytes 196616 | tf_op jit(solution)/shard_map/ppermute | solution.py:227
  73.2 1.3 %collective-permute-start.23 = (bf16[128,256]{1,0:T(8,128)(2,1)S(1)}, bf16[128,256]{1,0:T(8,128)(2,1)S(1)}, u32[]{:S(2)}, u32[]{:S(2)}) collective-permute-start(bf16[128,256]{1,0:T(8,128)(2,1)S(1)} %add_convert_fusion.7), channel_id=1, source_target_pairs={{0,8},{1,9},{2,10},{3,11},{4,12},{5,13},{6,14},{7,15},{8,0},{9,1},... | collective-permute-start | bytes 196616 | tf_op jit(solution)/shard_map/ppermute | solution.py:227
  73.2 5.9 %collective-permute-start.24 = (bf16[256,256]{1,0:T(8,128)(2,1)S(1)}, bf16[256,256]{1,0:T(8,128)(2,1)S(1)}, u32[]{:S(2)}, u32[]{:S(2)}) collective-permute-start(bf16[256,256]{1,0:T(8,128)(2,1)S(1)} %slice.36), channel_id=1, source_target_pairs={{0,16},{1,17},{2,18},{3,19},{4,20},{5,21},{6,22},{7,23},{8,24},{9,... | collective-permute-start | bytes 393224 | tf_op jit(solution)/shard_map/ppermute | solution.py:227

commit v2 on v1

--- a/solution.py
+++ b/solution.py
@@ -231,11 +231,11 @@
     return lax.optimization_barrier((value, *others))[0]
 
 
-def ring_gather(own, size, pairs_of):
+def ring_gather(own, size, pairs_of, hold):
     yield {0: own}
     ahead = behind = own
     for step in range(1, size // 2 + 1):
-        behind = move(behind, pairs_of(1))
+        behind = move(after(behind, *hold.get(step, [])), pairs_of(1))
         found = {size - step: behind}
         if step <= (size - 1) // 2:
             ahead = move(ahead, pairs_of(-1))
@@ -319,20 +319,22 @@
     tiles = load_tiles(tile_vals[0, 0])
     coord_here = tile_coord[0, 0]
     tile_total = tile_count[0, 0]
-    row_of = coord_here // block_cols
-    col_of = coord_here % block_cols
-
-    row_dev = col_of // piece
-    far = (row_dev // CORES - grid.x) % chips
-    swap = (row_dev % CORES - grid.core) % CORES
-    col_dev = row_of // piece
-    ahead = sum(jnp.where(col_dev == c, grid.ahead_of[c], 0) for c in range(col_devices))
-    source_out = (swap * chips + far) * piece + col_of % piece
-    bins_out = ahead_bins(ahead, col_devices) * piece + row_of % piece
+
+    def block_places(coord):
+        row_of, col_of = coord // block_cols, coord % block_cols
+        row_dev, col_dev = col_of // piece, row_of // piece
+        far = (row_dev // CORES - grid.x) % chips
+        swap = (row_dev % CORES - grid.core) % CORES
+        ahead = sum(jnp.where(col_dev == c, grid.ahead_of[c], 0) for c in range(col_devices))
+        return swap * chips + far, col_of % piece, ahead, row_of % piece
+
+    row_place, col_piece, ahead, row_piece = block_places(coord_here)
+    bins_out = ahead_bins(ahead, col_devices) * piece + row_piece
+    source_out = row_place * piece + col_piece
     table_out = tile_table(bins_out, block_rows, source_out, tile_total, block_cols)
 
     along_x = {}
-    for found in ring_gather(placed, chips, grid.along_x):
+    for found in ring_gather(placed, chips, grid.along_x, {}):
         along_x.update(found)
     along_x = [along_x[k] for k in range(chips)]
     sources_out = along_x + [move(block, grid.across(1, 0)) for block in along_x]
@@ -344,11 +346,13 @@
         table = table_out if step < 2 else after(table_out, earlier[step - 1])
         earlier.append(arrived)
         bins = (edges[step], edges[step + 1] - edges[step])
-        return tile_part(
+        made = tile_part(
             False, table, bins, block_rows, tiles, sources_out, block_cols, pieces=nodes_here
         )
-
-    earlier = []
+        parts.append(made[0])
+        return made
+
+    earlier, parts = [], []
     own_rows = ring_scatter(chunks_of, col_devices, grid.along_walk).astype(BF16)
 
     pre_act = jnp.dot(own_rows, weight, preferred_element_type=F32)
@@ -357,18 +361,16 @@
     own_agg_grad = lax.dot_general(
         own_grad, weight, (((1,), (1,)), ((), ())), preferred_element_type=F32
     ).astype(BF16)
-    activations = restore(onehot, own_act)
-
     arrivals = arrival_order(col_devices)
+    row_place, col_piece, ahead, row_piece = block_places(after(coord_here, parts[1]))
     part_of = sum(jnp.where(ahead == k, p, 0) for p, group in enumerate(arrivals) for k in group)
     block_at = sum(jnp.where(ahead == k, i, 0) for group in arrivals for i, k in enumerate(group))
-    place_back = (swap * chips + far) * piece + col_of % piece
     bins_back = len(arrivals) * block_cols
     empty_back = max(len(group) for group in arrivals) * piece
     table_back = tile_table(
-        part_of * block_cols + place_back,
+        part_of * block_cols + row_place * piece + col_piece,
         bins_back,
-        block_at * piece + row_of % piece,
+        block_at * piece + row_piece,
         tile_total,
         empty_back,
     )
@@ -376,17 +378,17 @@
         lax.dot_general(own_rows, own_grad, (((0,), (0,)), ((), ())), preferred_element_type=F32)
         * grad_scale
     )
-    acc, gate, weight_grad = None, [], None
+    acc, gate, hold, weight_grad = None, [], {}, None
     weight_steps = summed_everywhere(weight_part, grid, gate)
-    for number, found in enumerate(ring_gather(own_agg_grad, col_devices, grid.along_walk)):
+    weight_grad = next(weight_steps)
+    for number, found in enumerate(ring_gather(own_agg_grad, col_devices, grid.along_walk, hold)):
         blocks = [found[k] for k in arrivals[number]]
         if number == len(arrivals) - 1:
             break
         bins = (number * block_cols, block_cols)
         (acc,) = tile_part(True, table_back, bins, bins_back, tiles, blocks, empty_back, acc=acc)
-        gate[:] = [found[number]] if number in found and number else []
-        if number == 3:
-            gate.append(activations)
+        hold[number + 2] = [acc]
+        gate[:] = [found[number]] if number else [acc]
         weight_grad = next(weight_steps, weight_grad)
     bins = ((len(arrivals) - 1) * block_cols, block_cols)
     mine, theirs = tile_part(
@@ -405,6 +407,7 @@
     placed_grad = ring_scatter(
         lambda step, arrived: [sums[k] for k in order[step]], chips, grid.along_x
     ).astype(BF16)
+    activations = restore(onehot, own_act)
     feature_grad = restore(onehot, placed_grad)
     return (activations, weight_grad, feature_grad)
 

time: 80.7 us -> 75.1 us (0.931)
  waiting for transfers between devices: 28.8 us -> 21.5 us
  starting transfers between devices: 27.6 us -> 30.3 us
    ppermute x25, waiting for transfers between devices: 28.8 us -> 21.5 us  [move(): return lax.ppermute(value, ('row', 'col'), pairs)]
    ppermute x25, starting transfers between devices: 27.6 us -> 30.3 us  [move(): return lax.ppermute(value, ('row', 'col'), pairs)]
  transfers between devices with their start and end apart: 25 -> 25, of which waited for: 15 -> 12; matrix products, arithmetic and copies ran while one was open for 7% -> 6% of each run, Pallas kernels for 15% -> 14%
where the time goes in v2:
time: 75.1 us; the launch traced here: 74.6 us
  starting transfers between devices  30.3 us (40%)
  waiting for transfers between devices  21.5 us (29%)
  Pallas kernels  12.8 us (17%)
  other arithmetic  4.24 us (6%)
  matrix products  4 us (5%)
  between operations  1.64 us (2%)
    ppermute x25, starting transfers between devices, move(): return lax.ppermute(value, ('row', 'col'), pairs)  30.3 us
    ppermute x25, waiting for transfers between devices, move(): return lax.ppermute(value, ('row', 'col'), pairs)  21.5 us
    pallas_call x9, Pallas kernels, tile_part(): pl.pallas_call(functools.partial(part_kernel, spec), out_shape=out_shape,...  9.9 us
    pallas_call x1, Pallas kernels, load_tiles(): pl.pallas_call(load_kernel, out_shape=jax.ShapeDtypeStruct(tiles.shape, t...  2.87 us
    dot_general x2, matrix products, restore(): lax.dot_general(onehot, values, (((0,), (0,)), ((), ())), preferred_eleme...  1.99 us
  transfers between devices with their start and end apart: 25, of which 12 were waited for; matrix products, arithmetic and copies ran while one was open for 6% of the time, Pallas kernels for 14%

profile of v2, /device:TPU:0, one launch (start us, length us, event | category | flops | bytes accessed | tf_op | source)
XLA Modules:
  0.0 74.6 jit_solution(13152849047926059405)
XLA Ops:
  0.6 0.7 and_select_fusion.22
  1.4 1.1 %convolution_convert_fusion.4.refs_0_ = bf16[256,256]{1,0:T(8,128)(2,1)S(1)} fusion(bf16[256,256]{1,0:T(8,128)(2,1)} %param.7, s32[256]{0:T(256)S(1)} %and_select_fusion.22), kind=kOutput, calls=%fused_computation.9 | convolution fusion | flops 33685504 | bytes 263168 | tf_op jit(solution)/shard_map/dot_general | solution.py:36
  2.5 0.5 collective-permute-start.1
  3.0 2.6 %collective-permute-start = (bf16[256,256]{1,0:T(8,128)(2,1)S(1)}, bf16[256,256]{1,0:T(8,128)(2,1)S(1)}, u32[]{:S(2)}, u32[]{:S(2)}) collective-permute-start(bf16[256,256]{1,0:T(8,128)(2,1)S(1)} %convolution_convert_fusion.4.refs_0_), channel_id=1, source_target_pairs={{0,16},{1,17},{2,18},{3,19},{4,20},{5,21},{6,22},{7,23},{8,24},{9,... | collective-permute-start | bytes 393224 | tf_op jit(solution)/shard_map/ppermute | solution.py:227
  6.3 0.7 fusion.64
  7.7 1.9 %collective-permute-done.refs_1_ = bf16[256,256]{1,0:T(8,128)(2,1)S(1)} collective-permute-done((bf16[256,256]{1,0:T(8,128)(2,1)S(1)}, bf16[256,256]{1,0:T(8,128)(2,1)S(1)}, u32[]{:S(2)}, u32[]{:S(2)}) %collective-permute-start) | collective-permute-done | bytes 131104 | tf_op jit(solution)/shard_map/ppermute | solution.py:227
  9.8 2.9 %shard_map.94.tiles_ref = bf16[192,128,128]{2,1,0:T(8,128)(2,1)S(1)} custom-call(bf16[192,128,128]{2,1,0:T(8,128)(2,1)} %bitcast.13), custom_call_target="tpu_custom_call" | custom-call | bytes 6291456 | tf_op jit(solution)/shard_map/pallas_call | solution.py:82
  12.7 0.9 %shard_map.96 = (bf16[256,256]{1,0:T(8,128)(2,1)S(1)}, bf16[256,256]{1,0:T(8,128)(2,1)S(1)}) custom-call(s32[342]{0:T(512)S(1)} %pad_add_fusion.table_ref, bf16[192,128,128]{2,1,0:T(8,128)(2,1)S(1)} %shard_map.94.tiles_ref, bf16[256,256]{1,0:T(8,128)(2,1)S(1)} %convolution_convert_fusion.4.refs_0_, bf16[256,256]{1,0:T(8,128)(2,1)S(1)} %collective-permute-done.refs_1_, ...), custom_call_target="tpu_custom_call" | custom-call | flops 402653184 | bytes 1572864 | tf_op jit(solution)/shard_map/pallas_call | solution.py:159
  14.3 1.2 %shard_map.95 = (bf16[256,256]{1,0:T(8,128)(2,1)S(1)}, bf16[256,256]{1,0:T(8,128)(2,1)S(1)}) custom-call(s32[342]{0:T(512)S(1)} %pad_add_fusion.table_ref, bf16[192,128,128]{2,1,0:T(8,128)(2,1)S(1)} %shard_map.94.tiles_ref, bf16[256,256]{1,0:T(8,128)(2,1)S(1)} %convolution_convert_fusion.4.refs_0_, bf16[256,256]{1,0:T(8,128)(2,1)S(1)} %collective-permute-done.refs_1_, ...), custom_call_target="tpu_custom_call" | custom-call | flops 402653184 | bytes 1572864 | tf_op jit(solution)/shard_map/pallas_call | solution.py:159
  15.5 1.8 %collective-permute-start.3 = (bf16[256,256]{1,0:T(8,128)(2,1)S(1)}, bf16[256,256]{1,0:T(8,128)(2,1)S(1)}, u32[]{:S(2)}, u32[]{:S(2)}) collective-permute-start(bf16[256,256]{1,0:T(8,128)(2,1)S(1)} %get-tuple-element.24), channel_id=1, source_target_pairs={{0,1},{1,3},{3,5},{5,7},{7,6},{6,4},{4,2},{2,0},{10,12},{12,14},{1... | collective-permute-start | bytes 393224 | tf_op jit(solution)/shard_map/ppermute | solution.py:227
  17.3 2.1 %collective-permute-start.7 = (bf16[256,256]{1,0:T(8,128)(2,1)S(1)}, bf16[256,256]{1,0:T(8,128)(2,1)S(1)}, u32[]{:S(2)}, u32[]{:S(2)}) collective-permute-start(bf16[256,256]{1,0:T(8,128)(2,1)S(1)} %get-tuple-element.31), channel_id=1, source_target_pairs={{0,2},{1,0},{3,1},{5,3},{7,5},{6,7},{4,6},{2,4},{10,8},{12,10},{14... | collective-permute-start | bytes 393224 | tf_op jit(solution)/shard_map/ppermute | solution.py:227
  19.6 3.4 %collective-permute-done.3 = bf16[256,256]{1,0:T(8,128)(2,1)S(1)} collective-permute-done((bf16[256,256]{1,0:T(8,128)(2,1)S(1)}, bf16[256,256]{1,0:T(8,128)(2,1)S(1)}, u32[]{:S(2)}, u32[]{:S(2)}) %collective-permute-start.3) | collective-permute-done | bytes 131104 | tf_op jit(solution)/shard_map/ppermute | solution.py:227
  23.0 0.4 collective-permute-start.4
  23.5 0.3 collective-permute-done.7
  23.8 1.4 %collective-permute-start.8 = (bf16[256,256]{1,0:T(8,128)(2,1)S(1)}, bf16[256,256]{1,0:T(8,128)(2,1)S(1)}, u32[]{:S(2)}, u32[]{:S(2)}) collective-permute-start(bf16[256,256]{1,0:T(8,128)(2,1)S(1)} %add_convert_fusion.3), channel_id=1, source_target_pairs={{0,2},{1,0},{3,1},{5,3},{7,5},{6,7},{4,6},{2,4},{10,8},{12,10},{14... | collective-permute-start | bytes 393224 | tf_op jit(solution)/shard_map/ppermute | solution.py:227
  25.2 0.9 %shard_map.98 = (bf16[256,256]{1,0:T(8,128)(2,1)S(1)}, bf16[256,256]{1,0:T(8,128)(2,1)S(1)}) custom-call(s32[342]{0:T(512)S(1)} %pad_add_fusion.table_ref, bf16[192,128,128]{2,1,0:T(8,128)(2,1)S(1)} %shard_map.94.tiles_ref, bf16[256,256]{1,0:T(8,128)(2,1)S(1)} %convolution_convert_fusion.4.refs_0_, bf16[256,256]{1,0:T(8,128)(2,1)S(1)} %collective-permute-done.refs_1_, ...), custom_call_target="tpu_custom_call" | custom-call | flops 402653184 | bytes 1572864 | tf_op jit(solution)/shard_map/pallas_call | solution.py:159
  26.1 2.6 %collective-permute-done.4 = bf16[256,256]{1,0:T(8,128)(2,1)S(1)} collective-permute-done((bf16[256,256]{1,0:T(8,128)(2,1)S(1)}, bf16[256,256]{1,0:T(8,128)(2,1)S(1)}, u32[]{:S(2)}, u32[]{:S(2)}) %collective-permute-start.4) | collective-permute-done | bytes 131104 | tf_op jit(solution)/shard_map/ppermute | solution.py:227
  28.8 0.7 collective-permute-start.5
  29.6 1.4 %collective-permute-start.9 = (bf16[256,256]{1,0:T(8,128)(2,1)S(1)}, bf16[256,256]{1,0:T(8,128)(2,1)S(1)}, u32[]{:S(2)}, u32[]{:S(2)}) collective-permute-start(bf16[256,256]{1,0:T(8,128)(2,1)S(1)} %add_convert_fusion.2), channel_id=1, source_target_pairs={{0,2},{1,0},{3,1},{5,3},{7,5},{6,7},{4,6},{2,4},{10,8},{12,10},{14... | collective-permute-start | bytes 393224 | tf_op jit(solution)/shard_map/ppermute | solution.py:227
  31.0 1.2 %shard_map.97 = (bf16[256,256]{1,0:T(8,128)(2,1)S(1)}, bf16[256,256]{1,0:T(8,128)(2,1)S(1)}) custom-call(s32[342]{0:T(512)S(1)} %pad_add_fusion.table_ref, bf16[192,128,128]{2,1,0:T(8,128)(2,1)S(1)} %shard_map.94.tiles_ref, bf16[256,256]{1,0:T(8,128)(2,1)S(1)} %convolution_convert_fusion.4.refs_0_, bf16[256,256]{1,0:T(8,128)(2,1)S(1)} %collective-permute-done.refs_1_, ...), custom_call_target="tpu_custom_call" | custom-call | flops 402653184 | bytes 1572864 | tf_op jit(solution)/shard_map/pallas_call | solution.py:159
  32.1 1.7 %collective-permute-done.5 = bf16[256,256]{1,0:T(8,128)(2,1)S(1)} collective-permute-done((bf16[256,256]{1,0:T(8,128)(2,1)S(1)}, bf16[256,256]{1,0:T(8,128)(2,1)S(1)}, u32[]{:S(2)}, u32[]{:S(2)}) %collective-permute-start.5) | collective-permute-done | bytes 131104 | tf_op jit(solution)/shard_map/ppermute | solution.py:227
  33.9 1.7 %collective-permute-start.6 = (bf16[256,256]{1,0:T(8,128)(2,1)S(1)}, bf16[256,256]{1,0:T(8,128)(2,1)S(1)}, u32[]{:S(2)}, u32[]{:S(2)}) collective-permute-start(bf16[256,256]{1,0:T(8,128)(2,1)S(1)} %add_convert_fusion.4), channel_id=1, source_target_pairs={{0,1},{1,3},{3,5},{5,7},{7,6},{6,4},{4,2},{2,0},{10,12},{12,14},{1... | collective-permute-start | bytes 393224 | tf_op jit(solution)/shard_map/ppermute | solution.py:227
  35.7 3.1 %collective-permute-done.6 = bf16[256,256]{1,0:T(8,128)(2,1)S(1)} collective-permute-done((bf16[256,256]{1,0:T(8,128)(2,1)S(1)}, bf16[256,256]{1,0:T(8,128)(2,1)S(1)}, u32[]{:S(2)}, u32[]{:S(2)}) %collective-permute-start.6) | collective-permute-done | bytes 131104 | tf_op jit(solution)/shard_map/ppermute | solution.py:227
  39.3 0.3 fusion
  39.9 2.0 %collective-permute-start.12 = (bf16[256,256]{1,0:T(8,128)(2,1)S(1)}, bf16[256,256]{1,0:T(8,128)(2,1)S(1)}, u32[]{:S(2)}, u32[]{:S(2)}) collective-permute-start(bf16[256,256]{1,0:T(8,128)(2,1)S(1)} %convolution_convert_fusion.1.refs_0_), channel_id=1, source_target_pairs={{0,2},{1,0},{3,1},{5,3},{7,5},{6,7},{4,6},{2,4},{10,8},{12,10},{14... | collective-permute-start | bytes 393224 | tf_op jit(solution)/shard_map/ppermute | solution.py:227
  42.0 1.0 %shard_map.99.refs_2_ = f32[1024,256]{1,0:T(8,128)S(1)} custom-call(s32[486]{0:T(512)S(1)} %pad_add_fusion.1.table_ref, bf16[192,128,128]{2,1,0:T(8,128)(2,1)S(1)} %shard_map.94.tiles_ref, bf16[256,256]{1,0:T(8,128)(2,1)S(1)} %convolution_convert_fusion.1.refs_0_), custom_call_target="tpu_custom_call" | custom-call | flops 318767104 | bytes 1245184 | tf_op jit(solution)/shard_map/pallas_call | solution.py:159
  43.0 2.6 %collective-permute-start.11 = (bf16[128,256]{1,0:T(8,128)(2,1)S(1)}, bf16[128,256]{1,0:T(8,128)(2,1)S(1)}, u32[]{:S(2)}, u32[]{:S(2)}) collective-permute-start(bf16[128,256]{1,0:T(8,128)(2,1)S(1)} %slice_select_fusion), channel_id=1, source_target_pairs={{0,16},{1,17},{2,18},{3,19},{4,20},{5,21},{6,22},{7,23},{8,24},{9,... | collective-permute-start | bytes 196616 | tf_op jit(solution)/shard_map/ppermute | solution.py:227
  45.6 1.2 %collective-permute-done.18.refs_0_ = bf16[256,256]{1,0:T(8,128)(2,1)S(1)} collective-permute-done((bf16[256,256]{1,0:T(8,128)(2,1)S(1)}, bf16[256,256]{1,0:T(8,128)(2,1)S(1)}, u32[]{:S(2)}, u32[]{:S(2)}) %collective-permute-start.18) | collective-permute-done | bytes 131104 | tf_op jit(solution)/shard_map/ppermute | solution.py:227
  46.8 1.8 %collective-permute-start.19 = (bf16[256,256]{1,0:T(8,128)(2,1)S(1)}, bf16[256,256]{1,0:T(8,128)(2,1)S(1)}, u32[]{:S(2)}, u32[]{:S(2)}) collective-permute-start(bf16[256,256]{1,0:T(8,128)(2,1)S(1)} %collective-permute-done.18.refs_0_), channel_id=1, source_target_pairs={{0,1},{1,3},{3,5},{5,7},{7,6},{6,4},{4,2},{2,0},{10,12},{12,14},{1... | collective-permute-start | bytes 393224 | tf_op jit(solution)/shard_map/ppermute | solution.py:227
  48.9 2.1 %collective-permute-start.13 = (bf16[128,256]{1,0:T(8,128)(2,1)S(1)}, bf16[128,256]{1,0:T(8,128)(2,1)S(1)}, u32[]{:S(2)}, u32[]{:S(2)}) collective-permute-start(bf16[128,256]{1,0:T(8,128)(2,1)S(1)} %add_convert_fusion.10), channel_id=1, source_target_pairs={{0,1},{1,0},{2,3},{3,2},{4,5},{5,4},{6,7},{7,6},{8,9},{9,8},{10,11... | collective-permute-start | bytes 196616 | tf_op jit(solution)/shard_map/ppermute | solution.py:227
  51.0 1.0 %shard_map.100.refs_2_ = f32[1024,256]{1,0:T(8,128)S(1)} custom-call(s32[486]{0:T(512)S(1)} %pad_add_fusion.1.table_ref, bf16[192,128,128]{2,1,0:T(8,128)(2,1)S(1)} %shard_map.94.tiles_ref, bf16[256,256]{1,0:T(8,128)(2,1)S(1)} %collective-permute-done.18.refs_0_, bf16[256,256]{1,0:T(8,128)(2,1)S(1)} %collective-permute-done.12.refs_1_, ...), custom_call_target="tpu_custom_call" | custom-call | flops 318767104 | bytes 1245184 | tf_op jit(solution)/shard_map/pallas_call | solution.py:159
  52.0 0.7 collective-permute-done.19.refs_0_
  52.7 1.5 %collective-permute-start.20 = (bf16[256,256]{1,0:T(8,128)(2,1)S(1)}, bf16[256,256]{1,0:T(8,128)(2,1)S(1)}, u32[]{:S(2)}, u32[]{:S(2)}) collective-permute-start(bf16[256,256]{1,0:T(8,128)(2,1)S(1)} %collective-permute-done.19.refs_0_), channel_id=1, source_target_pairs={{0,1},{1,3},{3,5},{5,7},{7,6},{6,4},{4,2},{2,0},{10,12},{12,14},{1... | collective-permute-start | bytes 393224 | tf_op jit(solution)/shard_map/ppermute | solution.py:227
  54.3 0.5 collective-permute-start.16
  54.8 1.9 %collective-permute-start.15 = (bf16[128,256]{1,0:T(8,128)(2,1)S(1)}, bf16[128,256]{1,0:T(8,128)(2,1)S(1)}, u32[]{:S(2)}, u32[]{:S(2)}) collective-permute-start(bf16[128,256]{1,0:T(8,128)(2,1)S(1)} %add_convert_fusion.9), channel_id=1, source_target_pairs={{0,2},{1,3},{2,0},{3,1},{4,6},{5,7},{6,4},{7,5},{8,10},{9,11},{10,... | collective-permute-start | bytes 196616 | tf_op jit(solution)/shard_map/ppermute | solution.py:227
  56.7 1.5 %shard_map.101.refs_2_ = f32[1024,256]{1,0:T(8,128)S(1)} custom-call(s32[486]{0:T(512)S(1)} %pad_add_fusion.1.table_ref, bf16[192,128,128]{2,1,0:T(8,128)(2,1)S(1)} %shard_map.94.tiles_ref, bf16[256,256]{1,0:T(8,128)(2,1)S(1)} %collective-permute-done.19.refs_0_, bf16[256,256]{1,0:T(8,128)(2,1)S(1)} %collective-permute-done.14.refs_1_, ...), custom_call_target="tpu_custom_call" | custom-call | flops 318767104 | bytes 1245184 | tf_op jit(solution)/shard_map/pallas_call | solution.py:159
  58.3 1.0 %collective-permute-done.15 = bf16[128,256]{1,0:T(8,128)(2,1)S(1)} collective-permute-done((bf16[128,256]{1,0:T(8,128)(2,1)S(1)}, bf16[128,256]{1,0:T(8,128)(2,1)S(1)}, u32[]{:S(2)}, u32[]{:S(2)}) %collective-permute-start.15) | collective-permute-done | bytes 65568 | tf_op jit(solution)/shard_map/ppermute | solution.py:227
  59.3 1.8 %collective-permute-start.21 = (bf16[256,256]{1,0:T(8,128)(2,1)S(1)}, bf16[256,256]{1,0:T(8,128)(2,1)S(1)}, u32[]{:S(2)}, u32[]{:S(2)}) collective-permute-start(bf16[256,256]{1,0:T(8,128)(2,1)S(1)} %collective-permute-done.20.refs_0_), channel_id=1, source_target_pairs={{0,1},{1,3},{3,5},{5,7},{7,6},{6,4},{4,2},{2,0},{10,12},{12,14},{1... | collective-permute-start | bytes 393224 | tf_op jit(solution)/shard_map/ppermute | solution.py:227
  61.1 1.4 %collective-permute-start.17 = (bf16[128,256]{1,0:T(8,128)(2,1)S(1)}, bf16[128,256]{1,0:T(8,128)(2,1)S(1)}, u32[]{:S(2)}, u32[]{:S(2)}) collective-permute-start(bf16[128,256]{1,0:T(8,128)(2,1)S(1)} %add_convert_fusion.8), channel_id=1, source_target_pairs={{0,4},{1,5},{2,6},{3,7},{4,0},{5,1},{6,2},{7,3},{8,12},{9,13},{10,... | collective-permute-start | bytes 196616 | tf_op jit(solution)/shard_map/ppermute | solution.py:227
  62.5 1.3 %shard_map.102.refs_1_ = f32[1024,256]{1,0:T(8,128)S(1)} custom-call(s32[486]{0:T(512)S(1)} %pad_add_fusion.1.table_ref, bf16[192,128,128]{2,1,0:T(8,128)(2,1)S(1)} %shard_map.94.tiles_ref, bf16[256,256]{1,0:T(8,128)(2,1)S(1)} %collective-permute-done.20.refs_0_, bf16[256,256]{1,0:T(8,128)(2,1)S(1)} %collective-permute-done.16.refs_1_, ...), custom_call_target="tpu_custom_call" | custom-call | flops 318767104 | bytes 1245184 | tf_op jit(solution)/shard_map/pallas_call | solution.py:159
  63.8 0.7 collective-permute-done.21.refs_0_
  64.5 1.0 %shard_map.103 = (bf16[512,256]{1,0:T(8,128)(2,1)S(1)}, bf16[512,256]{1,0:T(8,128)(2,1)S(1)}) custom-call(s32[486]{0:T(512)S(1)} %pad_add_fusion.1.table_ref, bf16[192,128,128]{2,1,0:T(8,128)(2,1)S(1)} %shard_map.94.tiles_ref, bf16[256,256]{1,0:T(8,128)(2,1)S(1)} %collective-permute-done.21.refs_0_, f32[1024,256]{1,0:T(8,128)S(1)} %shard_map.102.refs_1_), custom_call_target="tpu_custom_call" | custom-call | flops 318767104 | bytes 1245184 | tf_op jit(solution)/shard_map/pallas_call | solution.py:159
  65.6 1.9 %collective-permute-done.17 = bf16[128,256]{1,0:T(8,128)(2,1)S(1)} collective-permute-done((bf16[128,256]{1,0:T(8,128)(2,1)S(1)}, bf16[128,256]{1,0:T(8,128)(2,1)S(1)}, u32[]{:S(2)}, u32[]{:S(2)}) %collective-permute-start.17) | collective-permute-done | bytes 65568 | tf_op jit(solution)/shard_map/ppermute | solution.py:227
  67.7 1.4 %collective-permute-start.24 = (bf16[256,256]{1,0:T(8,128)(2,1)S(1)}, bf16[256,256]{1,0:T(8,128)(2,1)S(1)}, u32[]{:S(2)}, u32[]{:S(2)}) collective-permute-start(bf16[256,256]{1,0:T(8,128)(2,1)S(1)} %slice.36), channel_id=1, source_target_pairs={{0,16},{1,17},{2,18},{3,19},{4,20},{5,21},{6,22},{7,23},{8,24},{9,... | collective-permute-start | bytes 393224 | tf_op jit(solution)/shard_map/ppermute | solution.py:227
  69.1 1.0 %convolution_convert_fusion.3 = bf16[256,256]{1,0:T(8,128)(2,1)} fusion(f32[256,256]{1,0:T(8,128)S(1)} %fusion.67, s32[256]{0:T(256)S(1)} %and_select_fusion.22), kind=kOutput, calls=%fused_computation.8 | convolution fusion | flops 33947648 | bytes 394240 | tf_op jit(solution)/shard_map/dot_general | solution.py:40
  70.1 0.7 fusion.10
  70.9 2.8 %collective-permute-done.24 = bf16[256,256]{1,0:T(8,128)(2,1)S(1)} collective-permute-done((bf16[256,256]{1,0:T(8,128)(2,1)S(1)}, bf16[256,256]{1,0:T(8,128)(2,1)S(1)}, u32[]{:S(2)}, u32[]{:S(2)}) %collective-permute-start.24) | collective-permute-done | bytes 131104 | tf_op jit(solution)/shard_map/ppermute | solution.py:227
  73.7 1.0 %convolution_convert_fusion = bf16[256,256]{1,0:T(8,128)(2,1)} fusion(f32[512,256]{1,0:T(8,128)S(1)} %convert_add_fusion, bf16[256,256]{1,0:T(8,128)(2,1)S(1)} %collective-permute-done.24, s32[256]{0:T(256)S(1)} %and_select_fusion.22), kind=kOutput, calls=%fused_computation.2 | convolution fusion | flops 33882112 | bytes 525312 | tf_op jit(solution)/shard_map/dot_general | solution.py:40
  (65 shorter events, 3.5 us)
Async XLA Ops:
  0.6 38.3 %copy-start = (bf16[256,256]{1,0:T(8,128)(2,1)S(1)}, bf16[256,256]{1,0:T(8,128)(2,1)}, u32[]{:S(2)}) copy-start(bf16[256,256]{1,0:T(8,128)(2,1)} %param.12) | copy-start | bytes 393220
  2.5 10.2 %collective-permute-start.1 = (bf16[256,256]{1,0:T(8,128)(2,1)S(1)}, bf16[256,256]{1,0:T(8,128)(2,1)S(1)}, u32[]{:S(2)}, u32[]{:S(2)}) collective-permute-start(bf16[256,256]{1,0:T(8,128)(2,1)S(1)} %convolution_convert_fusion.4.refs_0_), channel_id=1, source_target_pairs={{0,8},{1,9},{2,10},{3,11},{4,12},{5,13},{6,14},{7,15},{8,0},{9,1},... | collective-permute-start | bytes 393224 | tf_op jit(solution)/shard_map/ppermute | solution.py:227
  3.0 6.7 %collective-permute-start = (bf16[256,256]{1,0:T(8,128)(2,1)S(1)}, bf16[256,256]{1,0:T(8,128)(2,1)S(1)}, u32[]{:S(2)}, u32[]{:S(2)}) collective-permute-start(bf16[256,256]{1,0:T(8,128)(2,1)S(1)} %convolution_convert_fusion.4.refs_0_), channel_id=1, source_target_pairs={{0,16},{1,17},{2,18},{3,19},{4,20},{5,21},{6,22},{7,23},{8,24},{9,... | collective-permute-start | bytes 393224 | tf_op jit(solution)/shard_map/ppermute | solution.py:227
  9.7 3.1 %collective-permute-start.2 = (bf16[256,256]{1,0:T(8,128)(2,1)S(1)}, bf16[256,256]{1,0:T(8,128)(2,1)S(1)}, u32[]{:S(2)}, u32[]{:S(2)}) collective-permute-start(bf16[256,256]{1,0:T(8,128)(2,1)S(1)} %collective-permute-done.refs_1_), channel_id=1, source_target_pairs={{0,8},{1,9},{2,10},{3,11},{4,12},{5,13},{6,14},{7,15},{8,0},{9,1},... | collective-permute-start | bytes 393224 | tf_op jit(solution)/shard_map/ppermute | solution.py:227
  12.6 1.0 %copy-start.1 = (s32[1,1,192]{2,1,0:T(1,128)S(1)}, s32[1,1,192]{2,1,0:T(1,128)}, u32[]{:S(2)}) copy-start(s32[1,1,192]{2,1,0:T(1,128)} %param.10) | copy-start | bytes 2308
  15.5 7.5 %collective-permute-start.3 = (bf16[256,256]{1,0:T(8,128)(2,1)S(1)}, bf16[256,256]{1,0:T(8,128)(2,1)S(1)}, u32[]{:S(2)}, u32[]{:S(2)}) collective-permute-start(bf16[256,256]{1,0:T(8,128)(2,1)S(1)} %get-tuple-element.24), channel_id=1, source_target_pairs={{0,1},{1,3},{3,5},{5,7},{7,6},{6,4},{4,2},{2,0},{10,12},{12,14},{1... | collective-permute-start | bytes 393224 | tf_op jit(solution)/shard_map/ppermute | solution.py:227
  17.3 6.4 %collective-permute-start.7 = (bf16[256,256]{1,0:T(8,128)(2,1)S(1)}, bf16[256,256]{1,0:T(8,128)(2,1)S(1)}, u32[]{:S(2)}, u32[]{:S(2)}) collective-permute-start(bf16[256,256]{1,0:T(8,128)(2,1)S(1)} %get-tuple-element.31), channel_id=1, source_target_pairs={{0,2},{1,0},{3,1},{5,3},{7,5},{6,7},{4,6},{2,4},{10,8},{12,10},{14... | collective-permute-start | bytes 393224 | tf_op jit(solution)/shard_map/ppermute | solution.py:227
  23.0 5.7 %collective-permute-start.4 = (bf16[256,256]{1,0:T(8,128)(2,1)S(1)}, bf16[256,256]{1,0:T(8,128)(2,1)S(1)}, u32[]{:S(2)}, u32[]{:S(2)}) collective-permute-start(bf16[256,256]{1,0:T(8,128)(2,1)S(1)} %add_convert_fusion.6), channel_id=1, source_target_pairs={{0,1},{1,3},{3,5},{5,7},{7,6},{6,4},{4,2},{2,0},{10,12},{12,14},{1... | collective-permute-start | bytes 393224 | tf_op jit(solution)/shard_map/ppermute | solution.py:227
  23.8 15.3 %copy-start.2 = (bf16[256,256]{1,0:T(8,128)(2,1)S(1)}, bf16[256,256]{1,0:T(8,128)(2,1)}, u32[]{:S(2)}) copy-start(bf16[256,256]{1,0:T(8,128)(2,1)} %param.13) | copy-start | bytes 393220
  23.8 5.7 %collective-permute-start.8 = (bf16[256,256]{1,0:T(8,128)(2,1)S(1)}, bf16[256,256]{1,0:T(8,128)(2,1)S(1)}, u32[]{:S(2)}, u32[]{:S(2)}) collective-permute-start(bf16[256,256]{1,0:T(8,128)(2,1)S(1)} %add_convert_fusion.3), channel_id=1, source_target_pairs={{0,2},{1,0},{3,1},{5,3},{7,5},{6,7},{4,6},{2,4},{10,8},{12,10},{14... | collective-permute-start | bytes 393224 | tf_op jit(solution)/shard_map/ppermute | solution.py:227
  28.8 5.0 %collective-permute-start.5 = (bf16[256,256]{1,0:T(8,128)(2,1)S(1)}, bf16[256,256]{1,0:T(8,128)(2,1)S(1)}, u32[]{:S(2)}, u32[]{:S(2)}) collective-permute-start(bf16[256,256]{1,0:T(8,128)(2,1)S(1)} %add_convert_fusion.5), channel_id=1, source_target_pairs={{0,1},{1,3},{3,5},{5,7},{7,6},{6,4},{4,2},{2,0},{10,12},{12,14},{1... | collective-permute-start | bytes 393224 | tf_op jit(solution)/shard_map/ppermute | solution.py:227
  29.6 6.2 %collective-permute-start.9 = (bf16[256,256]{1,0:T(8,128)(2,1)S(1)}, bf16[256,256]{1,0:T(8,128)(2,1)S(1)}, u32[]{:S(2)}, u32[]{:S(2)}) collective-permute-start(bf16[256,256]{1,0:T(8,128)(2,1)S(1)} %add_convert_fusion.2), channel_id=1, source_target_pairs={{0,2},{1,0},{3,1},{5,3},{7,5},{6,7},{4,6},{2,4},{10,8},{12,10},{14... | collective-permute-start | bytes 393224 | tf_op jit(solution)/shard_map/ppermute | solution.py:227
  33.9 5.0 %collective-permute-start.6 = (bf16[256,256]{1,0:T(8,128)(2,1)S(1)}, bf16[256,256]{1,0:T(8,128)(2,1)S(1)}, u32[]{:S(2)}, u32[]{:S(2)}) collective-permute-start(bf16[256,256]{1,0:T(8,128)(2,1)S(1)} %add_convert_fusion.4), channel_id=1, source_target_pairs={{0,1},{1,3},{3,5},{5,7},{7,6},{6,4},{4,2},{2,0},{10,12},{12,14},{1... | collective-permute-start | bytes 393224 | tf_op jit(solution)/shard_map/ppermute | solution.py:227
  39.6 3.4 %collective-permute-start.10 = (bf16[256,256]{1,0:T(8,128)(2,1)S(1)}, bf16[256,256]{1,0:T(8,128)(2,1)S(1)}, u32[]{:S(2)}, u32[]{:S(2)}) collective-permute-start(bf16[256,256]{1,0:T(8,128)(2,1)S(1)} %fusion), channel_id=1, source_target_pairs={{0,8},{1,9},{2,10},{3,11},{4,12},{5,13},{6,14},{7,15},{8,0},{9,1},... | collective-permute-start | bytes 393224 | tf_op jit(solution)/shard_map/ppermute | solution.py:227
  39.9 8.8 %collective-permute-start.12 = (bf16[256,256]{1,0:T(8,128)(2,1)S(1)}, bf16[256,256]{1,0:T(8,128)(2,1)S(1)}, u32[]{:S(2)}, u32[]{:S(2)}) collective-permute-start(bf16[256,256]{1,0:T(8,128)(2,1)S(1)} %convolution_convert_fusion.1.refs_0_), channel_id=1, source_target_pairs={{0,2},{1,0},{3,1},{5,3},{7,5},{6,7},{4,6},{2,4},{10,8},{12,10},{14... | collective-permute-start | bytes 393224 | tf_op jit(solution)/shard_map/ppermute | solution.py:227
  41.9 5.0 %collective-permute-start.18 = (bf16[256,256]{1,0:T(8,128)(2,1)S(1)}, bf16[256,256]{1,0:T(8,128)(2,1)S(1)}, u32[]{:S(2)}, u32[]{:S(2)}) collective-permute-start(bf16[256,256]{1,0:T(8,128)(2,1)S(1)} %convolution_convert_fusion.1.refs_0_), channel_id=1, source_target_pairs={{0,1},{1,3},{3,5},{5,7},{7,6},{6,4},{4,2},{2,0},{10,12},{12,14},{1... | collective-permute-start | bytes 393224 | tf_op jit(solution)/shard_map/ppermute | solution.py:227
  43.0 5.8 %collective-permute-start.11 = (bf16[128,256]{1,0:T(8,128)(2,1)S(1)}, bf16[128,256]{1,0:T(8,128)(2,1)S(1)}, u32[]{:S(2)}, u32[]{:S(2)}) collective-permute-start(bf16[128,256]{1,0:T(8,128)(2,1)S(1)} %slice_select_fusion), channel_id=1, source_target_pairs={{0,16},{1,17},{2,18},{3,19},{4,20},{5,21},{6,22},{7,23},{8,24},{9,... | collective-permute-start | bytes 196616 | tf_op jit(solution)/shard_map/ppermute | solution.py:227
  46.8 5.9 %collective-permute-start.19 = (bf16[256,256]{1,0:T(8,128)(2,1)S(1)}, bf16[256,256]{1,0:T(8,128)(2,1)S(1)}, u32[]{:S(2)}, u32[]{:S(2)}) collective-permute-start(bf16[256,256]{1,0:T(8,128)(2,1)S(1)} %collective-permute-done.18.refs_0_), channel_id=1, source_target_pairs={{0,1},{1,3},{3,5},{5,7},{7,6},{6,4},{4,2},{2,0},{10,12},{12,14},{1... | collective-permute-start | bytes 393224 | tf_op jit(solution)/shard_map/ppermute | solution.py:227
  48.7 5.6 %collective-permute-start.14 = (bf16[256,256]{1,0:T(8,128)(2,1)S(1)}, bf16[256,256]{1,0:T(8,128)(2,1)S(1)}, u32[]{:S(2)}, u32[]{:S(2)}) collective-permute-start(bf16[256,256]{1,0:T(8,128)(2,1)S(1)} %collective-permute-done.12.refs_1_), channel_id=1, source_target_pairs={{0,2},{1,0},{3,1},{5,3},{7,5},{6,7},{4,6},{2,4},{10,8},{12,10},{14... | collective-permute-start | bytes 393224 | tf_op jit(solution)/shard_map/ppermute | solution.py:227
  48.9 5.9 %collective-permute-start.13 = (bf16[128,256]{1,0:T(8,128)(2,1)S(1)}, bf16[128,256]{1,0:T(8,128)(2,1)S(1)}, u32[]{:S(2)}, u32[]{:S(2)}) collective-permute-start(bf16[128,256]{1,0:T(8,128)(2,1)S(1)} %add_convert_fusion.10), channel_id=1, source_target_pairs={{0,1},{1,0},{2,3},{3,2},{4,5},{5,4},{6,7},{7,6},{8,9},{9,8},{10,11... | collective-permute-start | bytes 196616 | tf_op jit(solution)/shard_map/ppermute | solution.py:227
  52.7 6.5 %collective-permute-start.20 = (bf16[256,256]{1,0:T(8,128)(2,1)S(1)}, bf16[256,256]{1,0:T(8,128)(2,1)S(1)}, u32[]{:S(2)}, u32[]{:S(2)}) collective-permute-start(bf16[256,256]{1,0:T(8,128)(2,1)S(1)} %collective-permute-done.19.refs_0_), channel_id=1, source_target_pairs={{0,1},{1,3},{3,5},{5,7},{7,6},{6,4},{4,2},{2,0},{10,12},{12,14},{1... | collective-permute-start | bytes 393224 | tf_op jit(solution)/shard_map/ppermute | solution.py:227
  54.3 5.0 %collective-permute-start.16 = (bf16[256,256]{1,0:T(8,128)(2,1)S(1)}, bf16[256,256]{1,0:T(8,128)(2,1)S(1)}, u32[]{:S(2)}, u32[]{:S(2)}) collective-permute-start(bf16[256,256]{1,0:T(8,128)(2,1)S(1)} %collective-permute-done.14.refs_1_), channel_id=1, source_target_pairs={{0,2},{1,0},{3,1},{5,3},{7,5},{6,7},{4,6},{2,4},{10,8},{12,10},{14... | collective-permute-start | bytes 393224 | tf_op jit(solution)/shard_map/ppermute | solution.py:227
  54.8 4.5 %collective-permute-start.15 = (bf16[128,256]{1,0:T(8,128)(2,1)S(1)}, bf16[128,256]{1,0:T(8,128)(2,1)S(1)}, u32[]{:S(2)}, u32[]{:S(2)}) collective-permute-start(bf16[128,256]{1,0:T(8,128)(2,1)S(1)} %add_convert_fusion.9), channel_id=1, source_target_pairs={{0,2},{1,3},{2,0},{3,1},{4,6},{5,7},{6,4},{7,5},{8,10},{9,11},{10,... | collective-permute-start | bytes 196616 | tf_op jit(solution)/shard_map/ppermute | solution.py:227
  59.3 5.2 %collective-permute-start.21 = (bf16[256,256]{1,0:T(8,128)(2,1)S(1)}, bf16[256,256]{1,0:T(8,128)(2,1)S(1)}, u32[]{:S(2)}, u32[]{:S(2)}) collective-permute-start(bf16[256,256]{1,0:T(8,128)(2,1)S(1)} %collective-permute-done.20.refs_0_), channel_id=1, source_target_pairs={{0,1},{1,3},{3,5},{5,7},{7,6},{6,4},{4,2},{2,0},{10,12},{12,14},{1... | collective-permute-start | bytes 393224 | tf_op jit(solution)/shard_map/ppermute | solution.py:227
  61.1 6.4 %collective-permute-start.17 = (bf16[128,256]{1,0:T(8,128)(2,1)S(1)}, bf16[128,256]{1,0:T(8,128)(2,1)S(1)}, u32[]{:S(2)}, u32[]{:S(2)}) collective-permute-start(bf16[128,256]{1,0:T(8,128)(2,1)S(1)} %add_convert_fusion.8), channel_id=1, source_target_pairs={{0,4},{1,5},{2,6},{3,7},{4,0},{5,1},{6,2},{7,3},{8,12},{9,13},{10,... | collective-permute-start | bytes 196616 | tf_op jit(solution)/shard_map/ppermute | solution.py:227
  65.5 2.1 %collective-permute-start.23 = (bf16[512,256]{1,0:T(8,128)(2,1)S(1)}, bf16[512,256]{1,0:T(8,128)(2,1)S(1)}, u32[]{:S(2)}, u32[]{:S(2)}) collective-permute-start(bf16[512,256]{1,0:T(8,128)(2,1)S(1)} %get-tuple-element.44), channel_id=1, source_target_pairs={{0,8},{1,9},{2,10},{3,11},{4,12},{5,13},{6,14},{7,15},{8,0},{9,1},... | collective-permute-start | bytes 786440 | tf_op jit(solution)/shard_map/ppermute | solution.py:227
  67.5 2.6 %collective-permute-start.22 = (bf16[128,256]{1,0:T(8,128)(2,1)S(1)}, bf16[128,256]{1,0:T(8,128)(2,1)S(1)}, u32[]{:S(2)}, u32[]{:S(2)}) collective-permute-start(bf16[128,256]{1,0:T(8,128)(2,1)S(1)} %add_convert_fusion.7), channel_id=1, source_target_pairs={{0,8},{1,9},{2,10},{3,11},{4,12},{5,13},{6,14},{7,15},{8,0},{9,1},... | collective-permute-start | bytes 196616 | tf_op jit(solution)/shard_map/ppermute | solution.py:227
  67.7 6.0 %collective-permute-start.24 = (bf16[256,256]{1,0:T(8,128)(2,1)S(1)}, bf16[256,256]{1,0:T(8,128)(2,1)S(1)}, u32[]{:S(2)}, u32[]{:S(2)}) collective-permute-start(bf16[256,256]{1,0:T(8,128)(2,1)S(1)} %slice.36), channel_id=1, source_target_pairs={{0,16},{1,17},{2,18},{3,19},{4,20},{5,21},{6,22},{7,23},{8,24},{9,... | collective-permute-start | bytes 393224 | tf_op jit(solution)/shard_map/ppermute | solution.py:227

commit v3 on v2

--- a/solution.py
+++ b/solution.py
@@ -231,26 +231,42 @@
     return lax.optimization_barrier((value, *others))[0]
 
 
+def ring_hops(size):
+    return (size - 1) // 2
+
+
+def arrival_order(size):
+    hops = ring_hops(size)
+    groups = [[0]] + [[size - step, step] for step in range(1, hops + 1)]
+    if size % 2 == 0:
+        if hops:
+            groups[min(2, hops)].append(size // 2)
+        else:
+            groups.append([size // 2])
+    return groups
+
+
 def ring_gather(own, size, pairs_of, hold):
     yield {0: own}
     ahead = behind = own
-    for step in range(1, size // 2 + 1):
-        behind = move(after(behind, *hold.get(step, [])), pairs_of(1))
-        found = {size - step: behind}
-        if step <= (size - 1) // 2:
+    for step, group in enumerate(arrival_order(size)[1:], 1):
+        found = {}
+        if step == 1:
+            opposite = move(own, pairs_of(size // 2)) if size % 2 == 0 else None
+        if step <= ring_hops(size):
+            behind = move(after(behind, *hold.get(step, [])), pairs_of(1))
             ahead = move(ahead, pairs_of(-1))
-            found[step] = ahead
+            found = {size - step: behind, step: ahead}
+        if size // 2 in group and size % 2 == 0:
+            found[size // 2] = opposite
         yield found
 
 
 def scatter_order(size):
-    groups = []
-    for step in range(size // 2):
-        group = [size // 2 - step]
-        back = (size - 1) // 2 - step
-        if back > 0:
-            group.append(size - back)
-        groups.append(group)
+    hops = ring_hops(size)
+    groups = [[hop, size - hop] for hop in range(hops, 0, -1)] or [[]]
+    if size % 2 == 0:
+        groups[min(1, len(groups) - 1)].insert(0, size // 2)
     groups[-1].append(0)
     return groups
 
@@ -260,27 +276,25 @@
     return sum(jnp.where(ahead == k, place, 0) for place, k in enumerate(order))
 
 
-def arrival_order(size):
-    groups = [[0]]
-    for step in range(1, size // 2 + 1):
-        groups.append([size - step] + ([step] if step <= (size - 1) // 2 else []))
-    return groups
-
-
 def ring_scatter(chunks_of, size, pairs_of):
-    ahead = behind = None
+    ahead = behind = opposite = None
 
     def onward(running, term):
         return term if running is None else (running.astype(F32) + term.astype(F32)).astype(BF16)
 
     for step, group in enumerate(scatter_order(size)):
         terms = dict(zip(group, chunks_of(step, ahead)))
-        hop, back = size // 2 - step, (size - 1) // 2 - step
-        ahead = move(onward(ahead, terms[hop]), pairs_of(1))
-        if back > 0:
-            behind = move(onward(behind, terms[size - back]), pairs_of(-1))
-    total = terms[0].astype(F32) + ahead.astype(F32)
-    return total if behind is None else total + behind.astype(F32)
+        hop = ring_hops(size) - step
+        if hop > 0:
+            ahead = move(onward(ahead, terms[hop]), pairs_of(1))
+            behind = move(onward(behind, terms[size - hop]), pairs_of(-1))
+        if size // 2 in group and size % 2 == 0:
+            opposite = move(terms[size // 2], pairs_of(size // 2))
+    total = terms[0].astype(F32)
+    for part in (opposite, ahead, behind):
+        if part is not None:
+            total = total + part.astype(F32)
+    return total
 
 
 def summed_everywhere(part, grid, gate):
@@ -317,7 +331,7 @@
     onehot = permuter(node_order, nodes_here)
     placed = reorder(onehot, features)
     tiles = load_tiles(tile_vals[0, 0])
-    coord_here = tile_coord[0, 0]
+    coord_here = after(tile_coord[0, 0], tiles)
     tile_total = tile_count[0, 0]
 
     def block_places(coord):
@@ -346,13 +360,11 @@
         table = table_out if step < 2 else after(table_out, earlier[step - 1])
         earlier.append(arrived)
         bins = (edges[step], edges[step + 1] - edges[step])
-        made = tile_part(
+        return tile_part(
             False, table, bins, block_rows, tiles, sources_out, block_cols, pieces=nodes_here
         )
-        parts.append(made[0])
-        return made
-
-    earlier, parts = [], []
+
+    earlier = []
     own_rows = ring_scatter(chunks_of, col_devices, grid.along_walk).astype(BF16)
 
     pre_act = jnp.dot(own_rows, weight, preferred_element_type=F32)
@@ -362,7 +374,7 @@
         own_grad, weight, (((1,), (1,)), ((), ())), preferred_element_type=F32
     ).astype(BF16)
     arrivals = arrival_order(col_devices)
-    row_place, col_piece, ahead, row_piece = block_places(after(coord_here, parts[1]))
+    row_place, col_piece, ahead, row_piece = block_places(after(tile_coord[0, 0], *earlier[1:2]))
     part_of = sum(jnp.where(ahead == k, p, 0) for p, group in enumerate(arrivals) for k in group)
     block_at = sum(jnp.where(ahead == k, i, 0) for group in arrivals for i, k in enumerate(group))
     bins_back = len(arrivals) * block_cols
@@ -390,12 +402,12 @@
         hold[number + 2] = [acc]
         gate[:] = [found[number]] if number else [acc]
         weight_grad = next(weight_steps, weight_grad)
+    gate[:] = blocks
+    weight_grad = next(weight_steps, weight_grad)
     bins = ((len(arrivals) - 1) * block_cols, block_cols)
     mine, theirs = tile_part(
         True, table_back, bins, bins_back, tiles, blocks, empty_back, acc=acc, pieces=chips * nodes_here
     )
-    gate[:] = [mine]
-    weight_grad = next(weight_steps, weight_grad)
     got = move(theirs, grid.across(1, 0))
     both = mine.astype(F32) + got.astype(F32)
     sums = [both[k * nodes_here : (k + 1) * nodes_here] for k in range(chips)]

time: 75.1 us -> 75 us (level)
  waiting for transfers between devices: 21.5 us -> 14.5 us
  local copies, waits for them, and re-layouts: 0.18 us -> 5.61 us
  Pallas kernels: 12.8 us -> 17.5 us
  starting transfers between devices: 30.3 us -> 27.9 us
    ppermute x25, waiting for transfers between devices: 21.5 us -> 14.5 us  [move(): return lax.ppermute(value, ('row', 'col'), pairs)]
    unnamed x6 -> x10, local copies, waits for them, and re-layouts: 0.02 us -> 5.45 us
    pallas_call x9 -> x7, Pallas kernels: 9.9 us -> 14.6 us  [tile_part(): pl.pallas_call(functools.partial(part_kernel, spec), out_shape=out_shape,...]
    ppermute x25, starting transfers between devices: 30.3 us -> 27.9 us  [move(): return lax.ppermute(value, ('row', 'col'), pairs)]
  transfers between devices with their start and end apart: 25 -> 25, of which waited for: 12 -> 8; matrix products, arithmetic and copies ran while one was open for 6% -> 6% of each run, Pallas kernels for 14% -> 21%
where the time goes in v3:
time: 75 us; the launch traced here: 74.8 us
  starting transfers between devices  27.9 us (37%)
  Pallas kernels  17.5 us (23%)
  waiting for transfers between devices  14.5 us (19%)
  local copies, waits for them, and re-layouts  5.61 us (7%)
  matrix products  3.97 us (5%)
  other arithmetic  3.57 us (5%)
  between operations  1.75 us (2%)
    ppermute x25, starting transfers between devices, move(): return lax.ppermute(value, ('row', 'col'), pairs)  27.9 us
    pallas_call x7, Pallas kernels, tile_part(): pl.pallas_call(functools.partial(part_kernel, spec), out_shape=out_shape,...  14.6 us
    ppermute x25, waiting for transfers between devices, move(): return lax.ppermute(value, ('row', 'col'), pairs)  14.5 us
    unnamed x10, local copies, waits for them, and re-layouts  5.45 us
    pallas_call x1, Pallas kernels, load_tiles(): pl.pallas_call(load_kernel, out_shape=jax.ShapeDtypeStruct(tiles.shape, t...  2.88 us
    dot_general x2, matrix products, restore(): lax.dot_general(onehot, values, (((0,), (0,)), ((), ())), preferred_eleme...  1.99 us
  transfers between devices with their start and end apart: 25, of which 8 were waited for; matrix products, arithmetic and copies ran while one was open for 6% of the time, Pallas kernels for 21%

profile of v3, /device:TPU:0, one launch (start us, length us, event | category | flops | bytes accessed | tf_op | source)
XLA Modules:
  0.0 74.8 jit_solution(1991567998776651793)
XLA Ops:
  0.6 0.7 and_select_fusion.22
  1.4 1.1 %convolution_convert_fusion.4.refs_0_ = bf16[256,256]{1,0:T(8,128)(2,1)S(1)} fusion(bf16[256,256]{1,0:T(8,128)(2,1)} %param.7, s32[256]{0:T(256)S(1)} %and_select_fusion.22), kind=kOutput, calls=%fused_computation.9 | convolution fusion | flops 33685504 | bytes 263168 | tf_op jit(solution)/shard_map/dot_general | solution.py:36
  2.5 3.0 %collective-permute-start = (bf16[256,256]{1,0:T(8,128)(2,1)S(1)}, bf16[256,256]{1,0:T(8,128)(2,1)S(1)}, u32[]{:S(2)}, u32[]{:S(2)}) collective-permute-start(bf16[256,256]{1,0:T(8,128)(2,1)S(1)} %convolution_convert_fusion.4.refs_0_), channel_id=1, source_target_pairs={{0,16},{1,17},{2,18},{3,19},{4,20},{5,21},{6,22},{7,23},{8,24},{9,... | collective-permute-start | bytes 393224 | tf_op jit(solution)/shard_map/ppermute | solution.py:227
  5.5 2.9 %shard_map.94.tiles_ref = bf16[192,128,128]{2,1,0:T(8,128)(2,1)S(1)} custom-call(bf16[192,128,128]{2,1,0:T(8,128)(2,1)} %bitcast.15), custom_call_target="tpu_custom_call" | custom-call | bytes 6291456 | tf_op jit(solution)/shard_map/pallas_call | solution.py:82
  8.4 2.6 %copy-done.1 = bf16[192,128,128]{2,1,0:T(8,128)(2,1)} copy-done((bf16[192,128,128]{2,1,0:T(8,128)(2,1)}, bf16[192,128,128]{2,1,0:T(8,128)(2,1)S(1)}, u32[]{:S(2)}) %copy-start.1) | copy-done | bytes 6291480
  12.0 0.2 convert_reduce_fusion.1
  12.4 0.1 select_reduce_fusion.1
  12.6 0.6 collective-permute-start.2
  13.3 0.8 %collective-permute-done.2.refs_3_ = bf16[256,256]{1,0:T(8,128)(2,1)S(1)} collective-permute-done((bf16[256,256]{1,0:T(8,128)(2,1)S(1)}, bf16[256,256]{1,0:T(8,128)(2,1)S(1)}, u32[]{:S(2)}, u32[]{:S(2)}) %collective-permute-start.2) | collective-permute-done | bytes 131104 | tf_op jit(solution)/shard_map/ppermute | solution.py:227
  14.2 2.8 %copy-done.2 = bf16[192,128,128]{2,1,0:T(8,128)(2,1)S(1)} copy-done((bf16[192,128,128]{2,1,0:T(8,128)(2,1)S(1)}, bf16[192,128,128]{2,1,0:T(8,128)(2,1)}, u32[]{:S(2)}) %copy-start.2) | copy-done | bytes 6291480
  16.9 1.9 %shard_map.95 = (bf16[256,256]{1,0:T(8,128)(2,1)S(1)}, bf16[256,256]{1,0:T(8,128)(2,1)S(1)}) custom-call(s32[342]{0:T(512)S(1)} %pad_add_fusion.table_ref, bf16[192,128,128]{2,1,0:T(8,128)(2,1)S(1)} %copy-done.2, bf16[256,256]{1,0:T(8,128)(2,1)S(1)} %convolution_convert_fusion.4.refs_0_, bf16[256,256]{1,0:T(8,128)(2,1)S(1)} %collective-permute-done.refs_1_, ...), custom_call_target="tpu_custom_call" | custom-call | flops 402653184 | bytes 1572864 | tf_op jit(solution)/shard_map/pallas_call | solution.py:159
  18.8 1.3 %collective-permute-start.3 = (bf16[256,256]{1,0:T(8,128)(2,1)S(1)}, bf16[256,256]{1,0:T(8,128)(2,1)S(1)}, u32[]{:S(2)}, u32[]{:S(2)}) collective-permute-start(bf16[256,256]{1,0:T(8,128)(2,1)S(1)} %get-tuple-element.24), channel_id=1, source_target_pairs={{0,1},{1,3},{3,5},{5,7},{7,6},{6,4},{4,2},{2,0},{10,12},{12,14},{1... | collective-permute-start | bytes 393224 | tf_op jit(solution)/shard_map/ppermute | solution.py:227
  20.2 0.8 %collective-permute-start.7 = (bf16[256,256]{1,0:T(8,128)(2,1)S(1)}, bf16[256,256]{1,0:T(8,128)(2,1)S(1)}, u32[]{:S(2)}, u32[]{:S(2)}) collective-permute-start(bf16[256,256]{1,0:T(8,128)(2,1)S(1)} %get-tuple-element.30), channel_id=1, source_target_pairs={{0,2},{1,0},{3,1},{5,3},{7,5},{6,7},{4,6},{2,4},{10,8},{12,10},{14... | collective-permute-start | bytes 393224 | tf_op jit(solution)/shard_map/ppermute | solution.py:227
  20.9 1.9 %shard_map.97 = (bf16[256,256]{1,0:T(8,128)(2,1)S(1)}, bf16[256,256]{1,0:T(8,128)(2,1)S(1)}, bf16[256,256]{1,0:T(8,128)(2,1)S(1)}) custom-call(s32[342]{0:T(512)S(1)} %pad_add_fusion.table_ref, bf16[192,128,128]{2,1,0:T(8,128)(2,1)S(1)} %copy-done.2, bf16[256,256]{1,0:T(8,128)(2,1)S(1)} %convolution_convert_fusion.4.refs_0_, ...), custom_call_target="tpu_custom_call" | custom-call | flops 603979776 | bytes 2359296 | tf_op jit(solution)/shard_map/pallas_call | solution.py:159
  22.9 3.4 %collective-permute-start.4 = (bf16[256,256]{1,0:T(8,128)(2,1)S(1)}, bf16[256,256]{1,0:T(8,128)(2,1)S(1)}, u32[]{:S(2)}, u32[]{:S(2)}) collective-permute-start(bf16[256,256]{1,0:T(8,128)(2,1)S(1)} %get-tuple-element.27), channel_id=1, source_target_pairs={{0,7},{1,6},{3,4},{5,2},{7,0},{6,1},{4,3},{2,5},{10,13},{12,11},{1... | collective-permute-start | bytes 393224 | tf_op jit(solution)/shard_map/ppermute | solution.py:227
  26.5 0.2 convert_reduce_fusion
  26.8 2.1 %collective-permute-start.5 = (bf16[256,256]{1,0:T(8,128)(2,1)S(1)}, bf16[256,256]{1,0:T(8,128)(2,1)S(1)}, u32[]{:S(2)}, u32[]{:S(2)}) collective-permute-start(bf16[256,256]{1,0:T(8,128)(2,1)S(1)} %add_convert_fusion.5), channel_id=1, source_target_pairs={{0,1},{1,3},{3,5},{5,7},{7,6},{6,4},{4,2},{2,0},{10,12},{12,14},{1... | collective-permute-start | bytes 393224 | tf_op jit(solution)/shard_map/ppermute | solution.py:227
  29.3 2.2 %shard_map.96 = (bf16[256,256]{1,0:T(8,128)(2,1)S(1)}, bf16[256,256]{1,0:T(8,128)(2,1)S(1)}, bf16[256,256]{1,0:T(8,128)(2,1)S(1)}) custom-call(s32[342]{0:T(512)S(1)} %pad_add_fusion.table_ref, bf16[192,128,128]{2,1,0:T(8,128)(2,1)S(1)} %copy-done.2, bf16[256,256]{1,0:T(8,128)(2,1)S(1)} %convolution_convert_fusion.4.refs_0_, ...), custom_call_target="tpu_custom_call" | custom-call | flops 603979776 | bytes 2359296 | tf_op jit(solution)/shard_map/pallas_call | solution.py:159
  31.5 1.9 %collective-permute-done.8 = bf16[256,256]{1,0:T(8,128)(2,1)S(1)} collective-permute-done((bf16[256,256]{1,0:T(8,128)(2,1)S(1)}, bf16[256,256]{1,0:T(8,128)(2,1)S(1)}, u32[]{:S(2)}, u32[]{:S(2)}) %collective-permute-start.8) | collective-permute-done | bytes 131104 | tf_op jit(solution)/shard_map/ppermute | solution.py:227
  33.4 1.6 %collective-permute-start.9 = (bf16[256,256]{1,0:T(8,128)(2,1)S(1)}, bf16[256,256]{1,0:T(8,128)(2,1)S(1)}, u32[]{:S(2)}, u32[]{:S(2)}) collective-permute-start(bf16[256,256]{1,0:T(8,128)(2,1)S(1)} %add_convert_fusion.2), channel_id=1, source_target_pairs={{0,2},{1,0},{3,1},{5,3},{7,5},{6,7},{4,6},{2,4},{10,8},{12,10},{14... | collective-permute-start | bytes 393224 | tf_op jit(solution)/shard_map/ppermute | solution.py:227
  35.1 0.5 collective-permute-start.6
  35.8 3.3 %collective-permute-done.9 = bf16[256,256]{1,0:T(8,128)(2,1)S(1)} collective-permute-done((bf16[256,256]{1,0:T(8,128)(2,1)S(1)}, bf16[256,256]{1,0:T(8,128)(2,1)S(1)}, u32[]{:S(2)}, u32[]{:S(2)}) %collective-permute-start.9) | collective-permute-done | bytes 131104 | tf_op jit(solution)/shard_map/ppermute | solution.py:227
  39.0 1.6 %collective-permute-done.6 = bf16[256,256]{1,0:T(8,128)(2,1)S(1)} collective-permute-done((bf16[256,256]{1,0:T(8,128)(2,1)S(1)}, bf16[256,256]{1,0:T(8,128)(2,1)S(1)}, u32[]{:S(2)}, u32[]{:S(2)}) %collective-permute-start.6) | collective-permute-done | bytes 131104 | tf_op jit(solution)/shard_map/ppermute | solution.py:227
  40.7 0.2 fusion.65
  40.9 0.2 fusion.3
  41.1 0.2 fusion
  41.4 0.2 convolution_convert_fusion.1.refs_0_
  41.7 2.1 %collective-permute-start.12 = (bf16[256,256]{1,0:T(8,128)(2,1)S(1)}, bf16[256,256]{1,0:T(8,128)(2,1)S(1)}, u32[]{:S(2)}, u32[]{:S(2)}) collective-permute-start(bf16[256,256]{1,0:T(8,128)(2,1)S(1)} %convolution_convert_fusion.1.refs_0_), channel_id=1, source_target_pairs={{0,2},{1,0},{3,1},{5,3},{7,5},{6,7},{4,6},{2,4},{10,8},{12,10},{14... | collective-permute-start | bytes 393224 | tf_op jit(solution)/shard_map/ppermute | solution.py:227
  43.7 1.5 %shard_map.98.refs_2_ = f32[1024,256]{1,0:T(8,128)S(1)} custom-call(s32[438]{0:T(512)S(1)} %pad_add_fusion.1.table_ref, bf16[192,128,128]{2,1,0:T(8,128)(2,1)S(1)} %copy-done.2, bf16[256,256]{1,0:T(8,128)(2,1)S(1)} %convolution_convert_fusion.1.refs_0_), custom_call_target="tpu_custom_call" | custom-call | flops 402653184 | bytes 1572864 | tf_op jit(solution)/shard_map/pallas_call | solution.py:159
  45.4 0.7 collective-permute-start.11
  46.0 2.7 %collective-permute-done.16.refs_0_ = bf16[256,256]{1,0:T(8,128)(2,1)S(1)} collective-permute-done((bf16[256,256]{1,0:T(8,128)(2,1)S(1)}, bf16[256,256]{1,0:T(8,128)(2,1)S(1)}, u32[]{:S(2)}, u32[]{:S(2)}) %collective-permute-start.16) | collective-permute-done | bytes 131104 | tf_op jit(solution)/shard_map/ppermute | solution.py:227
  48.7 2.0 %collective-permute-start.14 = (bf16[256,256]{1,0:T(8,128)(2,1)S(1)}, bf16[256,256]{1,0:T(8,128)(2,1)S(1)}, u32[]{:S(2)}, u32[]{:S(2)}) collective-permute-start(bf16[256,256]{1,0:T(8,128)(2,1)S(1)} %collective-permute-done.12.refs_1_), channel_id=1, source_target_pairs={{0,2},{1,0},{3,1},{5,3},{7,5},{6,7},{4,6},{2,4},{10,8},{12,10},{14... | collective-permute-start | bytes 393224 | tf_op jit(solution)/shard_map/ppermute | solution.py:227
  50.8 2.6 %collective-permute-start.21 = (bf16[256,256]{1,0:T(8,128)(2,1)S(1)}, bf16[256,256]{1,0:T(8,128)(2,1)S(1)}, u32[]{:S(2)}, u32[]{:S(2)}) collective-permute-start(bf16[256,256]{1,0:T(8,128)(2,1)S(1)} %convolution_convert_fusion.1.refs_0_), channel_id=1, source_target_pairs={{0,7},{1,6},{3,4},{5,2},{7,0},{6,1},{4,3},{2,5},{10,13},{12,11},{1... | collective-permute-start | bytes 393224 | tf_op jit(solution)/shard_map/ppermute | solution.py:227
  53.4 2.4 %shard_map.99.refs_3_ = f32[1024,256]{1,0:T(8,128)S(1)} custom-call(s32[438]{0:T(512)S(1)} %pad_add_fusion.1.table_ref, bf16[192,128,128]{2,1,0:T(8,128)(2,1)S(1)} %copy-done.2, bf16[256,256]{1,0:T(8,128)(2,1)S(1)} %collective-permute-done.16.refs_0_, bf16[256,256]{1,0:T(8,128)(2,1)S(1)} %collective-permute-done.12.refs_1_, f32[1024,256]{1,0:T(8,128)S(1)} %shard_map.98.refs_2_), custom_call_target="tpu_custom_call" | custom-call | flops 402653184 | bytes 1572864 | tf_op jit(solution)/shard_map/pallas_call | solution.py:159
  55.8 0.6 collective-permute-start.18
  56.4 1.4 %collective-permute-start.19 = (bf16[256,256]{1,0:T(8,128)(2,1)S(1)}, bf16[256,256]{1,0:T(8,128)(2,1)S(1)}, u32[]{:S(2)}, u32[]{:S(2)}) collective-permute-start(bf16[256,256]{1,0:T(8,128)(2,1)S(1)} %collective-permute-done.14.refs_1_), channel_id=1, source_target_pairs={{0,2},{1,0},{3,1},{5,3},{7,5},{6,7},{4,6},{2,4},{10,8},{12,10},{14... | collective-permute-start | bytes 393224 | tf_op jit(solution)/shard_map/ppermute | solution.py:227
  57.9 2.2 %collective-permute-start.15 = (bf16[128,256]{1,0:T(8,128)(2,1)S(1)}, bf16[128,256]{1,0:T(8,128)(2,1)S(1)}, u32[]{:S(2)}, u32[]{:S(2)}) collective-permute-start(bf16[128,256]{1,0:T(8,128)(2,1)S(1)} %add_convert_fusion.8), channel_id=1, source_target_pairs={{0,2},{1,3},{2,0},{3,1},{4,6},{5,7},{6,4},{7,5},{8,10},{9,11},{10,... | collective-permute-start | bytes 196616 | tf_op jit(solution)/shard_map/ppermute | solution.py:227
  60.1 2.4 %shard_map.100.refs_2_ = f32[1024,256]{1,0:T(8,128)S(1)} custom-call(s32[438]{0:T(512)S(1)} %pad_add_fusion.1.table_ref, bf16[192,128,128]{2,1,0:T(8,128)(2,1)S(1)} %copy-done.2, bf16[256,256]{1,0:T(8,128)(2,1)S(1)} %collective-permute-done.17.refs_0_, bf16[256,256]{1,0:T(8,128)(2,1)S(1)} %collective-permute-done.14.refs_1_, ...), custom_call_target="tpu_custom_call" | custom-call | flops 402653184 | bytes 1572864 | tf_op jit(solution)/shard_map/pallas_call | solution.py:159
  62.5 2.3 %shard_map.101 = (bf16[512,256]{1,0:T(8,128)(2,1)S(1)}, bf16[512,256]{1,0:T(8,128)(2,1)S(1)}) custom-call(s32[438]{0:T(512)S(1)} %pad_add_fusion.1.table_ref, bf16[192,128,128]{2,1,0:T(8,128)(2,1)S(1)} %copy-done.2, bf16[256,256]{1,0:T(8,128)(2,1)S(1)} %collective-permute-done.18.refs_0_, bf16[256,256]{1,0:T(8,128)(2,1)S(1)} %collective-permute-done.19.refs_1_, ...), custom_call_target="tpu_custom_call" | custom-call | flops 402653184 | bytes 1572864 | tf_op jit(solution)/shard_map/pallas_call | solution.py:159
  65.0 1.0 %collective-permute-start.20 = (bf16[128,256]{1,0:T(8,128)(2,1)S(1)}, bf16[128,256]{1,0:T(8,128)(2,1)S(1)}, u32[]{:S(2)}, u32[]{:S(2)}) collective-permute-start(bf16[128,256]{1,0:T(8,128)(2,1)S(1)} %add_convert_fusion.7), channel_id=1, source_target_pairs={{0,4},{1,5},{2,6},{3,7},{4,0},{5,1},{6,2},{7,3},{8,12},{9,13},{10,... | collective-permute-start | bytes 196616 | tf_op jit(solution)/shard_map/ppermute | solution.py:227
  65.9 0.5 collective-permute-done.22
  66.5 1.6 %collective-permute-start.24 = (bf16[256,256]{1,0:T(8,128)(2,1)S(1)}, bf16[256,256]{1,0:T(8,128)(2,1)S(1)}, u32[]{:S(2)}, u32[]{:S(2)}) collective-permute-start(bf16[256,256]{1,0:T(8,128)(2,1)S(1)} %slice.36), channel_id=1, source_target_pairs={{0,16},{1,17},{2,18},{3,19},{4,20},{5,21},{6,22},{7,23},{8,24},{9,... | collective-permute-start | bytes 393224 | tf_op jit(solution)/shard_map/ppermute | solution.py:227
  68.1 3.6 %collective-permute-done.20 = bf16[128,256]{1,0:T(8,128)(2,1)S(1)} collective-permute-done((bf16[128,256]{1,0:T(8,128)(2,1)S(1)}, bf16[128,256]{1,0:T(8,128)(2,1)S(1)}, u32[]{:S(2)}, u32[]{:S(2)}) %collective-permute-start.20) | collective-permute-done | bytes 65568 | tf_op jit(solution)/shard_map/ppermute | solution.py:227
  71.8 0.1 collective-permute-start.23
  71.9 1.0 %convolution_convert_fusion.3 = bf16[256,256]{1,0:T(8,128)(2,1)} fusion(f32[256,256]{1,0:T(8,128)S(1)} %fusion.65, s32[256]{0:T(256)S(1)} %and_select_fusion.22), kind=kOutput, calls=%fused_computation.8 | convolution fusion | flops 33947648 | bytes 394240 | tf_op jit(solution)/shard_map/dot_general | solution.py:40
  72.9 0.2 collective-permute-done.23
  73.1 0.7 fusion.10
  73.8 1.0 %convolution_convert_fusion = bf16[256,256]{1,0:T(8,128)(2,1)} fusion(f32[512,256]{1,0:T(8,128)S(1)} %convert_add_fusion, bf16[256,256]{1,0:T(8,128)(2,1)S(1)} %collective-permute-done.24, s32[256]{0:T(256)S(1)} %and_select_fusion.22), kind=kOutput, calls=%fused_computation.2 | convolution fusion | flops 33882112 | bytes 525312 | tf_op jit(solution)/shard_map/dot_general | solution.py:40
  (67 shorter events, 2.1 us)
Async XLA Ops:
  0.6 40.0 %copy-start = (bf16[256,256]{1,0:T(8,128)(2,1)S(1)}, bf16[256,256]{1,0:T(8,128)(2,1)}, u32[]{:S(2)}) copy-start(bf16[256,256]{1,0:T(8,128)(2,1)} %param.12) | copy-start | bytes 393220
  2.5 10.1 %collective-permute-start = (bf16[256,256]{1,0:T(8,128)(2,1)S(1)}, bf16[256,256]{1,0:T(8,128)(2,1)S(1)}, u32[]{:S(2)}, u32[]{:S(2)}) collective-permute-start(bf16[256,256]{1,0:T(8,128)(2,1)S(1)} %convolution_convert_fusion.4.refs_0_), channel_id=1, source_target_pairs={{0,16},{1,17},{2,18},{3,19},{4,20},{5,21},{6,22},{7,23},{8,24},{9,... | collective-permute-start | bytes 393224 | tf_op jit(solution)/shard_map/ppermute | solution.py:227
  5.5 7.8 %collective-permute-start.1 = (bf16[256,256]{1,0:T(8,128)(2,1)S(1)}, bf16[256,256]{1,0:T(8,128)(2,1)S(1)}, u32[]{:S(2)}, u32[]{:S(2)}) collective-permute-start(bf16[256,256]{1,0:T(8,128)(2,1)S(1)} %convolution_convert_fusion.4.refs_0_), channel_id=1, source_target_pairs={{0,8},{1,9},{2,10},{3,11},{4,12},{5,13},{6,14},{7,15},{8,0},{9,1},... | collective-permute-start | bytes 393224 | tf_op jit(solution)/shard_map/ppermute | solution.py:227
  5.5 6.3 %copy-start.3 = (s32[1,1,192]{2,1,0:T(1,128)S(1)}, s32[1,1,192]{2,1,0:T(1,128)}, u32[]{:S(2)}) copy-start(s32[1,1,192]{2,1,0:T(1,128)} %param.10) | copy-start | bytes 2308
  8.4 2.7 %copy-start.1 = (bf16[192,128,128]{2,1,0:T(8,128)(2,1)}, bf16[192,128,128]{2,1,0:T(8,128)(2,1)S(1)}, u32[]{:S(2)}) copy-start(bf16[192,128,128]{2,1,0:T(8,128)(2,1)S(1)} %shard_map.94.tiles_ref) | copy-start | bytes 18874372
  12.6 1.6 %collective-permute-start.2 = (bf16[256,256]{1,0:T(8,128)(2,1)S(1)}, bf16[256,256]{1,0:T(8,128)(2,1)S(1)}, u32[]{:S(2)}, u32[]{:S(2)}) collective-permute-start(bf16[256,256]{1,0:T(8,128)(2,1)S(1)} %collective-permute-done.refs_1_), channel_id=1, source_target_pairs={{0,8},{1,9},{2,10},{3,11},{4,12},{5,13},{6,14},{7,15},{8,0},{9,1},... | collective-permute-start | bytes 393224 | tf_op jit(solution)/shard_map/ppermute | solution.py:227
  14.1 2.8 %copy-start.2 = (bf16[192,128,128]{2,1,0:T(8,128)(2,1)S(1)}, bf16[192,128,128]{2,1,0:T(8,128)(2,1)}, u32[]{:S(2)}) copy-start(bf16[192,128,128]{2,1,0:T(8,128)(2,1)} %copy-done.1) | copy-start | bytes 18874372
  18.8 7.4 %collective-permute-start.3 = (bf16[256,256]{1,0:T(8,128)(2,1)S(1)}, bf16[256,256]{1,0:T(8,128)(2,1)S(1)}, u32[]{:S(2)}, u32[]{:S(2)}) collective-permute-start(bf16[256,256]{1,0:T(8,128)(2,1)S(1)} %get-tuple-element.24), channel_id=1, source_target_pairs={{0,1},{1,3},{3,5},{5,7},{7,6},{6,4},{4,2},{2,0},{10,12},{12,14},{1... | collective-permute-start | bytes 393224 | tf_op jit(solution)/shard_map/ppermute | solution.py:227
  20.2 6.5 %collective-permute-start.7 = (bf16[256,256]{1,0:T(8,128)(2,1)S(1)}, bf16[256,256]{1,0:T(8,128)(2,1)S(1)}, u32[]{:S(2)}, u32[]{:S(2)}) collective-permute-start(bf16[256,256]{1,0:T(8,128)(2,1)S(1)} %get-tuple-element.30), channel_id=1, source_target_pairs={{0,2},{1,0},{3,1},{5,3},{7,5},{6,7},{4,6},{2,4},{10,8},{12,10},{14... | collective-permute-start | bytes 393224 | tf_op jit(solution)/shard_map/ppermute | solution.py:227
  22.9 18.0 %copy-start.4 = (bf16[256,256]{1,0:T(8,128)(2,1)S(1)}, bf16[256,256]{1,0:T(8,128)(2,1)}, u32[]{:S(2)}) copy-start(bf16[256,256]{1,0:T(8,128)(2,1)} %param.13) | copy-start | bytes 393220
  22.9 12.9 %collective-permute-start.4 = (bf16[256,256]{1,0:T(8,128)(2,1)S(1)}, bf16[256,256]{1,0:T(8,128)(2,1)S(1)}, u32[]{:S(2)}, u32[]{:S(2)}) collective-permute-start(bf16[256,256]{1,0:T(8,128)(2,1)S(1)} %get-tuple-element.27), channel_id=1, source_target_pairs={{0,7},{1,6},{3,4},{5,2},{7,0},{6,1},{4,3},{2,5},{10,13},{12,11},{1... | collective-permute-start | bytes 393224 | tf_op jit(solution)/shard_map/ppermute | solution.py:227
  26.7 6.7 %collective-permute-start.8 = (bf16[256,256]{1,0:T(8,128)(2,1)S(1)}, bf16[256,256]{1,0:T(8,128)(2,1)S(1)}, u32[]{:S(2)}, u32[]{:S(2)}) collective-permute-start(bf16[256,256]{1,0:T(8,128)(2,1)S(1)} %add_convert_fusion.3), channel_id=1, source_target_pairs={{0,2},{1,0},{3,1},{5,3},{7,5},{6,7},{4,6},{2,4},{10,8},{12,10},{14... | collective-permute-start | bytes 393224 | tf_op jit(solution)/shard_map/ppermute | solution.py:227
  26.8 8.3 %collective-permute-start.5 = (bf16[256,256]{1,0:T(8,128)(2,1)S(1)}, bf16[256,256]{1,0:T(8,128)(2,1)S(1)}, u32[]{:S(2)}, u32[]{:S(2)}) collective-permute-start(bf16[256,256]{1,0:T(8,128)(2,1)S(1)} %add_convert_fusion.5), channel_id=1, source_target_pairs={{0,1},{1,3},{3,5},{5,7},{7,6},{6,4},{4,2},{2,0},{10,12},{12,14},{1... | collective-permute-start | bytes 393224 | tf_op jit(solution)/shard_map/ppermute | solution.py:227
  33.4 5.6 %collective-permute-start.9 = (bf16[256,256]{1,0:T(8,128)(2,1)S(1)}, bf16[256,256]{1,0:T(8,128)(2,1)S(1)}, u32[]{:S(2)}, u32[]{:S(2)}) collective-permute-start(bf16[256,256]{1,0:T(8,128)(2,1)S(1)} %add_convert_fusion.2), channel_id=1, source_target_pairs={{0,2},{1,0},{3,1},{5,3},{7,5},{6,7},{4,6},{2,4},{10,8},{12,10},{14... | collective-permute-start | bytes 393224 | tf_op jit(solution)/shard_map/ppermute | solution.py:227
  35.1 5.5 %collective-permute-start.6 = (bf16[256,256]{1,0:T(8,128)(2,1)S(1)}, bf16[256,256]{1,0:T(8,128)(2,1)S(1)}, u32[]{:S(2)}, u32[]{:S(2)}) collective-permute-start(bf16[256,256]{1,0:T(8,128)(2,1)S(1)} %add_convert_fusion.4), channel_id=1, source_target_pairs={{0,1},{1,3},{3,5},{5,7},{7,6},{6,4},{4,2},{2,0},{10,12},{12,14},{1... | collective-permute-start | bytes 393224 | tf_op jit(solution)/shard_map/ppermute | solution.py:227
  41.3 3.9 %collective-permute-start.10 = (bf16[256,256]{1,0:T(8,128)(2,1)S(1)}, bf16[256,256]{1,0:T(8,128)(2,1)S(1)}, u32[]{:S(2)}, u32[]{:S(2)}) collective-permute-start(bf16[256,256]{1,0:T(8,128)(2,1)S(1)} %fusion), channel_id=1, source_target_pairs={{0,8},{1,9},{2,10},{3,11},{4,12},{5,13},{6,14},{7,15},{8,0},{9,1},... | collective-permute-start | bytes 393224 | tf_op jit(solution)/shard_map/ppermute | solution.py:227
  41.7 7.1 %collective-permute-start.12 = (bf16[256,256]{1,0:T(8,128)(2,1)S(1)}, bf16[256,256]{1,0:T(8,128)(2,1)S(1)}, u32[]{:S(2)}, u32[]{:S(2)}) collective-permute-start(bf16[256,256]{1,0:T(8,128)(2,1)S(1)} %convolution_convert_fusion.1.refs_0_), channel_id=1, source_target_pairs={{0,2},{1,0},{3,1},{5,3},{7,5},{6,7},{4,6},{2,4},{10,8},{12,10},{14... | collective-permute-start | bytes 393224 | tf_op jit(solution)/shard_map/ppermute | solution.py:227
  43.7 5.0 %collective-permute-start.16 = (bf16[256,256]{1,0:T(8,128)(2,1)S(1)}, bf16[256,256]{1,0:T(8,128)(2,1)S(1)}, u32[]{:S(2)}, u32[]{:S(2)}) collective-permute-start(bf16[256,256]{1,0:T(8,128)(2,1)S(1)} %convolution_convert_fusion.1.refs_0_), channel_id=1, source_target_pairs={{0,1},{1,3},{3,5},{5,7},{7,6},{6,4},{4,2},{2,0},{10,12},{12,14},{1... | collective-permute-start | bytes 393224 | tf_op jit(solution)/shard_map/ppermute | solution.py:227
  45.4 5.4 %collective-permute-start.11 = (bf16[128,256]{1,0:T(8,128)(2,1)S(1)}, bf16[128,256]{1,0:T(8,128)(2,1)S(1)}, u32[]{:S(2)}, u32[]{:S(2)}) collective-permute-start(bf16[128,256]{1,0:T(8,128)(2,1)S(1)} %slice_select_fusion), channel_id=1, source_target_pairs={{0,16},{1,17},{2,18},{3,19},{4,20},{5,21},{6,22},{7,23},{8,24},{9,... | collective-permute-start | bytes 196616 | tf_op jit(solution)/shard_map/ppermute | solution.py:227
  48.7 7.1 %collective-permute-start.17 = (bf16[256,256]{1,0:T(8,128)(2,1)S(1)}, bf16[256,256]{1,0:T(8,128)(2,1)S(1)}, u32[]{:S(2)}, u32[]{:S(2)}) collective-permute-start(bf16[256,256]{1,0:T(8,128)(2,1)S(1)} %collective-permute-done.16.refs_0_), channel_id=1, source_target_pairs={{0,1},{1,3},{3,5},{5,7},{7,6},{6,4},{4,2},{2,0},{10,12},{12,14},{1... | collective-permute-start | bytes 393224 | tf_op jit(solution)/shard_map/ppermute | solution.py:227
  48.7 7.1 %collective-permute-start.14 = (bf16[256,256]{1,0:T(8,128)(2,1)S(1)}, bf16[256,256]{1,0:T(8,128)(2,1)S(1)}, u32[]{:S(2)}, u32[]{:S(2)}) collective-permute-start(bf16[256,256]{1,0:T(8,128)(2,1)S(1)} %collective-permute-done.12.refs_1_), channel_id=1, source_target_pairs={{0,2},{1,0},{3,1},{5,3},{7,5},{6,7},{4,6},{2,4},{10,8},{12,10},{14... | collective-permute-start | bytes 393224 | tf_op jit(solution)/shard_map/ppermute | solution.py:227
  50.8 5.0 %collective-permute-start.13 = (bf16[128,256]{1,0:T(8,128)(2,1)S(1)}, bf16[128,256]{1,0:T(8,128)(2,1)S(1)}, u32[]{:S(2)}, u32[]{:S(2)}) collective-permute-start(bf16[128,256]{1,0:T(8,128)(2,1)S(1)} %add_convert_fusion.9), channel_id=1, source_target_pairs={{0,1},{1,0},{2,3},{3,2},{4,5},{5,4},{6,7},{7,6},{8,9},{9,8},{10,11... | collective-permute-start | bytes 196616 | tf_op jit(solution)/shard_map/ppermute | solution.py:227
  50.8 9.3 %collective-permute-start.21 = (bf16[256,256]{1,0:T(8,128)(2,1)S(1)}, bf16[256,256]{1,0:T(8,128)(2,1)S(1)}, u32[]{:S(2)}, u32[]{:S(2)}) collective-permute-start(bf16[256,256]{1,0:T(8,128)(2,1)S(1)} %convolution_convert_fusion.1.refs_0_), channel_id=1, source_target_pairs={{0,7},{1,6},{3,4},{5,2},{7,0},{6,1},{4,3},{2,5},{10,13},{12,11},{1... | collective-permute-start | bytes 393224 | tf_op jit(solution)/shard_map/ppermute | solution.py:227
  55.8 6.7 %collective-permute-start.18 = (bf16[256,256]{1,0:T(8,128)(2,1)S(1)}, bf16[256,256]{1,0:T(8,128)(2,1)S(1)}, u32[]{:S(2)}, u32[]{:S(2)}) collective-permute-start(bf16[256,256]{1,0:T(8,128)(2,1)S(1)} %collective-permute-done.17.refs_0_), channel_id=1, source_target_pairs={{0,1},{1,3},{3,5},{5,7},{7,6},{6,4},{4,2},{2,0},{10,12},{12,14},{1... | collective-permute-start | bytes 393224 | tf_op jit(solution)/shard_map/ppermute | solution.py:227
  56.4 6.1 %collective-permute-start.19 = (bf16[256,256]{1,0:T(8,128)(2,1)S(1)}, bf16[256,256]{1,0:T(8,128)(2,1)S(1)}, u32[]{:S(2)}, u32[]{:S(2)}) collective-permute-start(bf16[256,256]{1,0:T(8,128)(2,1)S(1)} %collective-permute-done.14.refs_1_), channel_id=1, source_target_pairs={{0,2},{1,0},{3,1},{5,3},{7,5},{6,7},{4,6},{2,4},{10,8},{12,10},{14... | collective-permute-start | bytes 393224 | tf_op jit(solution)/shard_map/ppermute | solution.py:227
  57.9 7.0 %collective-permute-start.15 = (bf16[128,256]{1,0:T(8,128)(2,1)S(1)}, bf16[128,256]{1,0:T(8,128)(2,1)S(1)}, u32[]{:S(2)}, u32[]{:S(2)}) collective-permute-start(bf16[128,256]{1,0:T(8,128)(2,1)S(1)} %add_convert_fusion.8), channel_id=1, source_target_pairs={{0,2},{1,3},{2,0},{3,1},{4,6},{5,7},{6,4},{7,5},{8,10},{9,11},{10,... | collective-permute-start | bytes 196616 | tf_op jit(solution)/shard_map/ppermute | solution.py:227
  64.8 1.6 %collective-permute-start.22 = (bf16[512,256]{1,0:T(8,128)(2,1)S(1)}, bf16[512,256]{1,0:T(8,128)(2,1)S(1)}, u32[]{:S(2)}, u32[]{:S(2)}) collective-permute-start(bf16[512,256]{1,0:T(8,128)(2,1)S(1)} %get-tuple-element.41), channel_id=1, source_target_pairs={{0,8},{1,9},{2,10},{3,11},{4,12},{5,13},{6,14},{7,15},{8,0},{9,1},... | collective-permute-start | bytes 786440 | tf_op jit(solution)/shard_map/ppermute | solution.py:227
  65.0 6.8 %collective-permute-start.20 = (bf16[128,256]{1,0:T(8,128)(2,1)S(1)}, bf16[128,256]{1,0:T(8,128)(2,1)S(1)}, u32[]{:S(2)}, u32[]{:S(2)}) collective-permute-start(bf16[128,256]{1,0:T(8,128)(2,1)S(1)} %add_convert_fusion.7), channel_id=1, source_target_pairs={{0,4},{1,5},{2,6},{3,7},{4,0},{5,1},{6,2},{7,3},{8,12},{9,13},{10,... | collective-permute-start | bytes 196616 | tf_op jit(solution)/shard_map/ppermute | solution.py:227
  66.5 7.3 %collective-permute-start.24 = (bf16[256,256]{1,0:T(8,128)(2,1)S(1)}, bf16[256,256]{1,0:T(8,128)(2,1)S(1)}, u32[]{:S(2)}, u32[]{:S(2)}) collective-permute-start(bf16[256,256]{1,0:T(8,128)(2,1)S(1)} %slice.36), channel_id=1, source_target_pairs={{0,16},{1,17},{2,18},{3,19},{4,20},{5,21},{6,22},{7,23},{8,24},{9,... | collective-permute-start | bytes 393224 | tf_op jit(solution)/shard_map/ppermute | solution.py:227
  71.8 1.3 %collective-permute-start.23 = (bf16[128,256]{1,0:T(8,128)(2,1)S(1)}, bf16[128,256]{1,0:T(8,128)(2,1)S(1)}, u32[]{:S(2)}, u32[]{:S(2)}) collective-permute-start(bf16[128,256]{1,0:T(8,128)(2,1)S(1)} %add_convert_fusion.6), channel_id=1, source_target_pairs={{0,8},{1,9},{2,10},{3,11},{4,12},{5,13},{6,14},{7,15},{8,0},{9,1},... | collective-permute-start | bytes 196616 | tf_op jit(solution)/shard_map/ppermute | solution.py:227
